TPU v7x, 32 devices: a whole 2x2x4 slice. The times are simulated.
32 devices in a mesh: src: 8 (over z, x), tgt: 4 (over y, core).
Axes of the slice: x: 2, y: 2, z: 4, core: 2. Of those that a mesh axis runs over, the one named last changes fastest.
Arguments:
- sources: float32 [50, 4096], P(None, 'src'), may hold values from -1.2 to 1.2
- targets: float32 [50, 16384], P(None, 'tgt'), may hold values from -1.2 to 1.2
- pair_active: int32 [8, 4], P('src', 'tgt'), may hold values from 0 to 1, as said below
- count_src: int32 [8], replicated, may hold values from 256 to 512, as said below
- count_tgt: int32 [4], replicated, may hold values from 2048 to 4096, as said below
Outputs:
- source_potential: float32 [4096], P('src')
- target_potential: float32 [16384], P('tgt')
- ancestors: float32 [50, 16384], P(None, ('tgt', 'src'))
Inputs may be any that keep to these rules, and one draw needn't show every extreme that they name: `pair_active`: every source block has at least one listed tile and every target tile is listed with at least one source block. `count_src`: some block holds exactly 512 live cells and another exactly 256. `count_tgt`: some tile holds exactly 4096 live cells and another exactly 2048.
All inputs are finite; a program needn't handle non-finite values.
Results may differ from a plain program's by a relative error of at most 0.0003.
Values sent between devices are 32-bit elements; how exact they have to be, the bound alone decides.
No kernel may reach another device: no remote copies, remote signals or barrier semaphores. Data moves between devices by JAX's collectives and lax.ppermute only.
A program may use at most 64 MiB of HBM per device.

v0:
```python
import functools
import math

import jax
import jax.numpy as jnp
from jax import lax
from jax.experimental import pallas as pl
from jax.experimental.pallas import tpu as pltpu
from jax.sharding import PartitionSpec as P

ITERS = 4
EPS = 0.02
NEG = -1e30
LOG2E = math.log2(math.e)
SCALE = LOG2E / EPS
LANES = 128
DEPTH = 64
FACTOR_MAX = 2.0**20
SUM_MIN = 2.0**-70
TOTAL_MAX = 2.0**100
VMEM_LIMIT = 14 * 1024 * 1024

VMEM_SPEC = pl.BlockSpec(memory_space=pltpu.VMEM)
SMEM_SPEC = pl.BlockSpec(memory_space=pltpu.SMEM)


def pinned(x):
    return pltpu.with_memory_space_constraint(x, pltpu.VMEM)


def split(x):
    high = x.astype(jnp.bfloat16)
    rest = x - high.astype(jnp.float32)
    mid = rest.astype(jnp.bfloat16)
    low = (rest - mid.astype(jnp.float32)).astype(jnp.bfloat16)
    return high, mid, low


def put(ref, row):
    for k in range(row.shape[1] // LANES):
        ref[k : k + 1, :] = row[:, k * LANES : (k + 1) * LANES]


def positions(shape):
    return lax.broadcasted_iota(jnp.int32, shape, 0) * LANES + lax.broadcasted_iota(jnp.int32, shape, 1)


def to_sublanes(vector_ref, col_ref):
    for k in range(vector_ref.shape[0]):
        col_ref[k * LANES : (k + 1) * LANES, :] = jnp.broadcast_to(vector_ref[k : k + 1, :], (LANES, LANES)).T


def fold_lanes(peak_ref, total_ref, out_ref):
    for k in range(out_ref.shape[0]):
        here = slice(k * LANES, (k + 1) * LANES)
        peaks = peak_ref[here, :].T
        top = jnp.max(peaks, axis=0, keepdims=True)
        total = jnp.sum(total_ref[here, :].T * jnp.exp2(peaks - top), axis=0, keepdims=True)
        out_ref[k : k + 1, :] = top + jnp.log2(total)


def row_lse(score_ref, add_ref, peak_ref, total_ref, out_ref):
    rows, cols = score_ref.shape

    def block(i, _):
        here = pl.ds(pl.multiple_of(i * 8, 8), 8)
        z = []
        for k in range(cols // LANES):
            value = score_ref[here, k * LANES : (k + 1) * LANES]
            if add_ref is not None:
                value = value + add_ref[k : k + 1, :]
            z.append(value)
        peak = functools.reduce(jnp.maximum, z)
        peak_ref[here, :] = peak
        total_ref[here, :] = functools.reduce(jnp.add, [jnp.exp2(v - peak) for v in z])
        return 0

    lax.fori_loop(0, rows // 8, block, 0)
    fold_lanes(peak_ref, total_ref, out_ref)


def col_lse(score_ref, add_ref, out_ref, kernel_ref=None, top_ref=None):
    rows, cols = score_ref.shape
    group = 16
    tall = 4

    for first in range(0, cols // LANES, group):
        lanes = [slice((first + k) * LANES, (first + k + 1) * LANES) for k in range(group)]

        def peaks(i, tops):
            for r in range(tall):
                here = pl.ds(pl.multiple_of((i * tall + r) * 8, 8), 8)
                add = add_ref[here, :]
                tops = tuple(jnp.maximum(t, score_ref[here, s] + add) for t, s in zip(tops, lanes))
            return tops

        start = (jnp.full((8, LANES), -jnp.inf, jnp.float32),) * group
        tops = lax.fori_loop(0, rows // (8 * tall), peaks, start)
        tops = [jnp.max(t, axis=0, keepdims=True) for t in tops]
        wide_tops = [jnp.broadcast_to(t, (8, LANES)) for t in tops]

        def totals(i, sums):
            for r in range(tall):
                here = pl.ds(pl.multiple_of((i * tall + r) * 8, 8), 8)
                add = add_ref[here, :]
                terms = [jnp.exp2(score_ref[here, s] + (add - t)) for t, s in zip(wide_tops, lanes)]
                if kernel_ref is not None:
                    for s, t in zip(lanes, terms):
                        kernel_ref[here, s] = t
                sums = tuple(u + t for u, t in zip(sums, terms))
            return sums

        start = (jnp.zeros((8, LANES), jnp.float32),) * group
        sums = lax.fori_loop(0, rows // (8 * tall), totals, start)
        for k, (t, u) in enumerate(zip(tops, sums)):
            spot = slice(first + k, first + k + 1)
            if top_ref is not None:
                top_ref[spot, :] = t
            out_ref[spot, :] = t + jnp.log2(jnp.sum(u, axis=0, keepdims=True))


def source_terms(x):
    high, mid, low = split(x * (2.0 * SCALE))
    return [high, high, mid, mid, high, low]


def target_terms(y):
    high, mid, low = split(y)
    return [high, mid, high, mid, low, high]


def pad_into(pad_ref, values):
    pad_ref[...] = jnp.zeros(pad_ref.shape, jnp.float32)
    pad_ref[0 : values.shape[0], :] = values


def live_sum(counts):
    total = counts[0]
    for i in range(1, counts.shape[0]):
        total = total + counts[i]
    return jnp.full((1, LANES), total, jnp.int32).astype(jnp.float32)


def wide(x, size):
    return jnp.concatenate([x] * (size // LANES), axis=1)


def first_kernel(
    src_hbm, tgt_hbm, count_src_hbm, count_tgt_hbm, pair,
    score_ref, lse_ref, row_aux, col_aux, own_ref, half_ref,
    src_ref, tgt_ref, count_src, count_tgt, sems,
    right_pad, left_pad, terms_ref, norm_ref, col_ref, peak_ref, total_ref,
):
    rows, cols = score_ref.shape
    dims = src_ref.shape[0]
    copies = [
        pltpu.make_async_copy(one, two, sems.at[i])
        for i, (one, two) in enumerate(
            [(count_src_hbm, count_src), (count_tgt_hbm, count_tgt), (src_hbm, src_ref), (tgt_hbm, tgt_ref)]
        )
    ]
    for copy in copies:
        copy.start()
    for ref in (right_pad, left_pad, own_ref):
        ref[...] = jnp.zeros(ref.shape, jnp.float32)
    n_half = -(-dims // 2)
    for copy in copies[:3]:
        copy.wait()
    n_rows = count_src[lax.axis_index("src")]
    n_cols = count_tgt[lax.axis_index("tgt")]
    listed = pair[0, 0] > 0
    row_live = positions(row_aux.shape[1:]) < n_rows
    col_live = positions(col_aux.shape[1:]) < n_cols
    row_aux[0] = row_live.astype(jnp.float32)
    row_aux[1] = jnp.where(row_live, -jnp.log2(live_sum(count_src)), 0.0)
    row_aux[2] = (row_live & listed).astype(jnp.float32)
    col_aux[0] = col_live.astype(jnp.float32)
    col_aux[1] = jnp.where(col_live, -jnp.log2(live_sum(count_tgt)), 0.0)
    left_pad[0:dims, :] = src_ref[...]
    left = left_pad[...]
    half = jnp.where(lax.axis_index("tgt") % 2 == 0, left[0:n_half], left[n_half : 2 * n_half])
    half_ref[...] = jnp.zeros(half_ref.shape, jnp.float32)
    for k in range(rows // LANES):
        half_ref[0, k * n_half : (k + 1) * n_half, :] = half[:, k * LANES : (k + 1) * LANES]
    put(norm_ref, -SCALE * jnp.sum(left * left, axis=0, keepdims=True))
    norm_ref[...] = jnp.where(row_live, norm_ref[...], NEG)
    to_sublanes(norm_ref, col_ref)
    terms_ref[...] = jnp.concatenate(source_terms(left.T), axis=1)
    copies[3].wait()
    size = 512

    def scores(c):
        here = pl.ds(pl.multiple_of(c * size, size), size)
        right_pad[0:dims, :] = tgt_ref[:, here]
        right = right_pad[...]
        spot = lax.broadcasted_iota(jnp.int32, (1, size), 1) + c * size
        norm = -SCALE * jnp.sum(right * right, axis=0, keepdims=True)
        norm = jnp.where((spot < n_cols) & listed, norm, NEG)
        terms = jnp.concatenate(target_terms(right), axis=0)
        cross = jnp.dot(terms_ref[...], terms, preferred_element_type=jnp.float32)
        score = cross + (wide(col_ref[...], size) + norm)
        score_ref[:, here] = score
        return [score[:, k : k + LANES] for k in range(0, size, LANES)]

    first = scores(0)
    peak = jnp.max(functools.reduce(jnp.maximum, first), axis=1, keepdims=True)
    peak_ref[...] = jnp.broadcast_to(peak, peak_ref.shape)
    total_ref[...] = functools.reduce(jnp.add, [jnp.exp2(z - peak_ref[...]) for z in first])

    def block(c, _):
        total_ref[...] += functools.reduce(jnp.add, [jnp.exp2(z - peak_ref[...]) for z in scores(c)])
        return 0

    lax.fori_loop(1, cols // size, block, 0)
    share = own_ref.shape[1]
    own_ref[0:dims, :] = tgt_ref[:, pl.ds(pl.multiple_of(lax.axis_index("src") * share, share), share)]
    fold_lanes(peak_ref, total_ref, lse_ref)

    @pl.when(jnp.logical_not(jnp.max(total_ref[...]) <= TOTAL_MAX))
    def _():
        row_lse(score_ref, None, peak_ref, total_ref, lse_ref)


def slab_kernel(
    own_ref, mine_ref, theirs_ref, slab_ref, terms_out, token_ref, right_pad, terms_ref, norm_ref, col_ref,
    *, first, n_half,
):
    share = own_ref.shape[1]
    rows = right_pad.shape[1]
    left = own_ref[...]
    put(norm_ref, -SCALE * jnp.sum(left * left, axis=0, keepdims=True))
    to_sublanes(norm_ref, col_ref)
    terms_ref[...] = jnp.concatenate(target_terms(left.T), axis=1)
    even = lax.axis_index("tgt") % 2 == 0
    right_pad[...] = jnp.zeros(right_pad.shape, jnp.float32)
    for b in range(slab_ref.shape[1] // rows):
        mine, theirs = mine_ref[first + b], theirs_ref[first + b]
        upper = jnp.where(even, mine, theirs)
        lower = jnp.where(even, theirs, mine)
        for k in range(rows // LANES):
            here = slice(k * n_half, (k + 1) * n_half)
            right_pad[0:n_half, k * LANES : (k + 1) * LANES] = upper[here]
            right_pad[n_half : 2 * n_half, k * LANES : (k + 1) * LANES] = lower[here]
        right = right_pad[...]
        norm = -SCALE * jnp.sum(right * right, axis=0, keepdims=True)
        terms = jnp.concatenate(source_terms(right), axis=0)
        cross = jnp.dot(terms_ref[...], terms, preferred_element_type=jnp.float32)
        here = slice(b * rows, (b + 1) * rows)
        slab_ref[:, here] = cross + (wide(col_ref[...], rows) + norm)
        terms_out[here, :] = jnp.concatenate(split(right.T), axis=1)
    token_ref[...] = jnp.zeros(token_ref.shape, jnp.float32)


def row_sums(kernel_ref, factor_ref, total_ref, out_ref):
    rows, cols = kernel_ref.shape
    tall = 8

    def block(i, _):
        spots = [pl.ds(pl.multiple_of((i * tall + k) * 8, 8), 8) for k in range(tall)]
        sums = [jnp.zeros((8, LANES), jnp.float32)] * tall
        for t in range(cols // LANES):
            lanes = slice(t * LANES, (t + 1) * LANES)
            factor = jnp.broadcast_to(factor_ref[t : t + 1, :], (8, LANES))
            sums = [u + kernel_ref[s, lanes] * factor for u, s in zip(sums, spots)]
        for s, u in zip(spots, sums):
            total_ref[s, :] = u
        return 0

    lax.fori_loop(0, rows // (8 * tall), block, 0)
    for k in range(out_ref.shape[0]):
        out_ref[k : k + 1, :] = jnp.sum(total_ref[k * LANES : (k + 1) * LANES, :].T, axis=0, keepdims=True)


def col_sums(kernel_ref, factor_ref, out_ref):
    rows, cols = kernel_ref.shape
    lanes = [slice(start, start + LANES) for start in range(0, cols, LANES)]
    tall = 4

    def block(i, sums):
        for r in range(tall):
            here = pl.ds(pl.multiple_of((i * tall + r) * 8, 8), 8)
            factor = factor_ref[here, :]
            sums = tuple(u + kernel_ref[here, s] * factor for u, s in zip(sums, lanes))
        return sums

    sums = lax.fori_loop(0, rows // (8 * tall), block, (jnp.zeros((8, LANES), jnp.float32),) * len(lanes))
    for k, u in enumerate(sums):
        out_ref[k : k + 1, :] = jnp.sum(u, axis=0, keepdims=True)


def out_of_range(total, needed, factor):
    small = jnp.where(needed & jnp.logical_not(total >= SUM_MIN), 1.0, 0.0)
    large = jnp.where(factor <= FACTOR_MAX, 0.0, 1.0)
    return jnp.max(jnp.maximum(jnp.max(small, axis=0, keepdims=True), jnp.max(large, axis=0, keepdims=True))) > 0.5


def set_f(lse_ref, aux_ref, f_ref, masked_ref):
    f = aux_ref[1] - lse_ref[...] * aux_ref[0]
    f_ref[...] = f
    masked_ref[...] = jnp.where(aux_ref[2] > 0, f, NEG)


def first_col_kernel(score_ref, lse_ref, aux_ref, out_ref, f_ref, masked_ref, kernel_ref, top_ref, col_ref):
    set_f(lse_ref, aux_ref, f_ref, masked_ref)
    to_sublanes(f_ref, col_ref)
    col_lse(score_ref, col_ref, out_ref, kernel_ref, top_ref)


def col_kernel(
    score_ref, kernel_ref, top_ref, base_ref, lse_ref, aux_ref, out_ref, f_ref, masked_ref, factor_ref, col_ref
):
    set_f(lse_ref, aux_ref, f_ref, masked_ref)
    factor_ref[...] = jnp.exp2(f_ref[...] - base_ref[...])
    to_sublanes(factor_ref, col_ref)
    col_sums(kernel_ref, col_ref, out_ref)
    total = out_ref[...]
    top = top_ref[...]
    redo = out_of_range(total, top > 0.5 * NEG, factor_ref[...])
    out_ref[...] = jnp.where(total > 0, top + jnp.log2(total), NEG)

    @pl.when(redo)
    def _():
        to_sublanes(f_ref, col_ref)
        col_lse(score_ref, col_ref, out_ref)


def row_kernel(
    score_ref, kernel_ref, top_ref, base_ref, parts_ref, row_aux, col_aux, out_ref,
    g_ref, factor_ref, peak_ref, total_ref,
):
    parts = parts_ref[...]
    peak = jnp.max(parts, axis=0)
    lse = peak + jnp.log2(jnp.sum(jnp.exp2(parts - peak[None]), axis=0))
    g_ref[...] = col_aux[1] - lse * col_aux[0]
    factor_ref[...] = jnp.where(col_aux[0] > 0, jnp.exp2(top_ref[...] - lse), 0.0)
    row_sums(kernel_ref, factor_ref, total_ref, out_ref)
    total = out_ref[...]
    redo = out_of_range(total, row_aux[2] > 0, factor_ref[...])
    log_b = col_aux[1, 0:1, 0:1]
    out_ref[...] = jnp.where(total > 0, jnp.log2(total) - base_ref[...] + log_b, NEG)

    @pl.when(redo)
    def _():
        row_lse(score_ref, g_ref, peak_ref, total_ref, out_ref)


def last_kernel(*refs, pieces):
    slabs, refs = refs[:pieces], refs[pieces:]
    terms, refs = refs[:pieces], refs[pieces:]
    f_all_ref, lse_ref, aux_ref, f_ref, out_ref, f_out, g_out, own_ref, col_ref, sum_ref = refs
    f_out[...] = f_ref[...] * (1.0 / SCALE)
    g_out[...] = (aux_ref[1] - lse_ref[...] * aux_ref[0]) * (1.0 / SCALE)
    n_own = own_ref.shape[0]
    for k in range(n_own):
        spot = pl.ds(lax.axis_index("src") * n_own + k, 1)
        own_ref[k : k + 1, :] = jnp.where(aux_ref[0, spot, :] > 0, -lse_ref[spot, :], NEG)
    to_sublanes(own_ref, col_ref)
    spot = 0
    for slab_ref, terms_ref in zip(slabs, terms):
        high, mid = [], []
        first = spot == 0
        for start in range(0, slab_ref.shape[1], LANES):
            add = col_ref[...] + f_all_ref[spot : spot + 1, :]
            parts = split(jnp.exp2(slab_ref[:, start : start + LANES] + add))
            high.append(parts[0])
            mid.append(parts[1])
            spot += 1
        sums = jnp.dot(
            jnp.concatenate(high + mid, axis=1), jnp.concatenate([terms_ref[...]] * 2, axis=0),
            preferred_element_type=jnp.float32,
        )
        if first:
            sum_ref[...] = sums
        else:
            sum_ref[...] += sums
    sums = sum_ref[...].T
    out_ref[...] = (sums[0:DEPTH] + sums[DEPTH : 2 * DEPTH] + sums[2 * DEPTH :])[0 : out_ref.shape[0]]


def merge(one, two):
    top = jnp.maximum(one, two)
    return top + jnp.log2(1.0 + jnp.exp2(jnp.minimum(one, two) - top))


def swap(value, axis, step):
    return lax.ppermute(value, axis, [(i, i ^ step) for i in range(lax.axis_size(axis))])


def doubling(size):
    return [1 << k for k in range(size.bit_length() - 1)]


def buffer(space, shape):
    return space(*shape) if isinstance(shape[0], tuple) else space(shape, jnp.float32)


def call(kernel, outs, scratch, ins, flops, expos=0, pin=True):
    return pl.pallas_call(
        kernel,
        out_shape=[buffer(pltpu.VMEM if pin else jax.ShapeDtypeStruct, shape) for shape in outs],
        in_specs=[VMEM_SPEC] * len(ins),
        out_specs=[VMEM_SPEC] * len(outs),
        scratch_shapes=[buffer(pltpu.VMEM, shape) for shape in scratch],
        compiler_params=pltpu.CompilerParams(vmem_limit_bytes=VMEM_LIMIT),
        cost_estimate=pl.CostEstimate(flops=flops, bytes_accessed=0, transcendentals=expos),
    )(*[pinned(x) for x in ins])


def tie(*values):
    return lax.optimization_barrier(values)


class Beside:
    def __init__(self, half, own, steps, rows, n_half):
        self.parts = half
        self.own = own
        self.steps = list(steps)
        self.coming = None
        self.mine = []
        self.theirs = []
        self.ready = []
        self.todo = []
        self.terms = []
        self.rows = rows
        self.n_half = n_half
        self.slabs = []

    def start(self, value, axis, step):
        if self.coming is not None or not self.steps:
            return swap(value, axis, step)
        value, parts = tie(value, self.parts)
        if self.mine:
            self.mine = [parts]
        self.parts = parts
        other = swap(value, axis, step)
        self.coming = swap(parts, "src", self.steps.pop(0))
        return other

    def land(self, value):
        if self.coming is None:
            return value
        value, coming = tie(value, self.coming)
        self.coming = None
        if self.steps:
            self.parts = jnp.concatenate([self.parts, coming], axis=0)
            if len(self.steps) == 1:
                self.mine = [self.parts]
        else:
            self.mine.append(coming)
        return value

    def trade(self, value):
        group = len(self.theirs)
        if group == len(self.mine):
            return value
        value, self.mine[group] = tie(value, self.mine[group])
        self.theirs.append(swap(self.mine[group], "tgt", 1))
        return value

    def traded(self, value):
        for group in range(len(self.ready), len(self.theirs)):
            value, self.theirs[group] = tie(value, self.theirs[group])
            self.ready.append(group)
            size = max(self.mine[group].shape[0] // 2, 1)
            self.todo += [(group, first, size) for first in range(0, self.mine[group].shape[0], size)]
        return value

    def piece(self):
        group, first, size = self.todo.pop(0)
        mine, theirs = self.mine[group], self.theirs[group]
        share = self.own.shape[1]
        rows = self.rows
        slab, terms, token = call(
            functools.partial(slab_kernel, first=first, n_half=self.n_half),
            [(share, size * rows), ((size * rows, 3 * DEPTH), jnp.bfloat16), (8, LANES)],
            [(DEPTH, rows), ((share, 6 * DEPTH), jnp.bfloat16), (share // LANES, LANES), (share, LANES)],
            [self.own, mine, theirs],
            12 * DEPTH * share * size * rows,
        )
        self.terms.append(terms)
        self.slabs.append(slab)
        return token

    def work(self, value, axis, step):
        if not self.todo:
            return swap(value, axis, step)
        value, self.own = tie(value, self.own)
        other = swap(value, axis, step)
        other, _ = tie(other, self.piece())
        return other

    def finish(self, value):
        while self.steps or self.coming is not None:
            if self.coming is None:
                self.coming = swap(self.parts, "src", self.steps.pop(0))
            value = self.land(value)
        while len(self.theirs) < len(self.mine):
            value = self.trade(value)
        self.traded(value)
        while self.todo:
            self.piece()


def shards(sources, targets, pair_active, count_src, count_tgt):
    dims, rows = sources.shape
    cols = targets.shape[1]
    share = cols // lax.axis_size("src")
    column = (rows, LANES)
    by_row = (rows // LANES, LANES)
    by_col = (cols // LANES, LANES)
    pairs = rows * cols
    hbm = [pltpu.with_memory_space_constraint(x, pltpu.HBM) for x in (sources, targets, count_src, count_tgt)]
    n_half = -(-dims // 2)
    packed = -(-n_half * by_row[0] // 8) * 8
    outs = [(rows, cols), by_row, (3, *by_row), (3, *by_col), (DEPTH, share), (1, packed, LANES)]
    score, lse, row_aux, col_aux, own, half = pl.pallas_call(
        first_kernel,
        out_shape=[pltpu.VMEM(shape, jnp.float32) for shape in outs],
        in_specs=[pl.BlockSpec(memory_space=pltpu.HBM)] * 4 + [SMEM_SPEC],
        out_specs=[VMEM_SPEC] * len(outs),
        scratch_shapes=[
            pltpu.VMEM((dims, rows), jnp.float32),
            pltpu.VMEM((dims, cols), jnp.float32),
            pltpu.SMEM(count_src.shape, jnp.int32),
            pltpu.SMEM(count_tgt.shape, jnp.int32),
            pltpu.SemaphoreType.DMA((4,)),
            pltpu.VMEM((DEPTH, 512), jnp.float32),
            pltpu.VMEM((DEPTH, rows), jnp.float32),
            pltpu.VMEM((rows, 6 * DEPTH), jnp.bfloat16),
            pltpu.VMEM(by_row, jnp.float32),
            pltpu.VMEM(column, jnp.float32),
            pltpu.VMEM(column, jnp.float32),
            pltpu.VMEM(column, jnp.float32),
        ],
        compiler_params=pltpu.CompilerParams(vmem_limit_bytes=VMEM_LIMIT),
        cost_estimate=pl.CostEstimate(flops=12 * DEPTH * pairs, bytes_accessed=0, transcendentals=pairs),
    )(*hbm, pair_active)
    over_tgt = doubling(lax.axis_size("tgt"))
    over_src = doubling(lax.axis_size("src"))
    over_src = over_src[1:] + over_src[:1]
    side = Beside(half, own, over_src, rows, n_half)
    for step in range(ITERS):
        for bit in over_tgt:
            if step == ITERS - 1 and bit == over_tgt[0]:
                lse = side.trade(lse)
            if bit != over_tgt[-1]:
                other = swap(lse, "tgt", bit)
            elif step < ITERS - 1:
                other = side.start(lse, "tgt", bit)
            else:
                other = side.work(lse, "tgt", bit)
            lse = merge(lse, other)
        if step == ITERS - 2:
            lse = side.trade(lse)
        if step == 0:
            lse, base, masked, kernel, top = call(
                first_col_kernel,
                [by_col, by_row, by_row, (rows, cols), by_col],
                [column], [score, lse, row_aux], 0,
            )
        else:
            lse, f, masked = call(
                col_kernel,
                [by_col, by_row, by_row],
                [by_row, column], [score, kernel, top, base, lse, row_aux], 0,
            )
        if step < ITERS - 1:
            lse = side.traded(side.land(lse))
            lse = jnp.broadcast_to(lse, (lax.axis_size("src"), *by_col))
            lse = lax.all_to_all(lse, "src", 0, 0, tiled=True)
            (lse,) = call(
                row_kernel,
                [by_row],
                [by_col, by_col, column, column],
                [score, kernel, top, base, lse, row_aux, col_aux], 0,
            )
    lse = side.traded(lse)
    for bit in over_src:
        both = jnp.concatenate([lse, masked], axis=0)
        other = side.work(both, "src", bit)
        lse = merge(lse, other[: by_col[0]])
        masked = jnp.concatenate([masked, other[by_col[0] :]], axis=0)
    side.finish(lse)
    ancestors, f, g = call(
        functools.partial(last_kernel, pieces=len(side.slabs)),
        [(dims, share), by_row, by_col],
        [(share // LANES, LANES), (share, LANES), (share, 3 * DEPTH)],
        [*side.slabs, *side.terms, masked, lse, col_aux, f],
        18 * DEPTH * pairs, pairs, pin=False,
    )
    return (f.reshape(rows), g.reshape(cols), ancestors)


def solution(mesh):
    return jax.shard_map(
        shards,
        mesh=mesh,
        in_specs=(P(None, "src"), P(None, "tgt"), P("src", "tgt"), P(), P()),
        out_specs=(P("src"), P("tgt"), P(None, ("tgt", "src"))),
        check_vma=False,
    )
```

profile of v0, /device:TPU:0, one launch (start us, length us, event | category | flops | bytes accessed | tf_op | source)
XLA Modules:
  0.0 108.9 jit_solution(2360910546493174858)
XLA Ops:
  1.3 5.5 %shard_map.76 = (f32[512,4096]{1,0:T(8,128)S(1)}, f32[4,128]{1,0:T(4,128)S(1)}, f32[3,4,128]{2,1,0:T(4,128)S(1)}, f32[3,32,128]{2,1,0:T(8,128)S(1)}, f32[64,512]{1,0:T(8,128)S(1)}, /*index=5*/f32[1,104,128]{2,1,0:T(8,128)S(1)}) custom-call(f32[50,512]{1,0:T(8,128)} %src_hbm.1, f32[50,4096]{1,0:T(8,128)} %tgt_hbm.1, s32[8]{0:T(128)} %count_src_hbm.1, ...), custom_call_target="tpu_custom_call" | custom-call | flops 1610612736 | tf_op jit(solution)/shard_map/pallas_call | solution.py:516
  7.3 0.8 collective-permute-done
  8.1 7.9 %collective-permute-start.1 = (f32[4,128]{1,0:T(4,128)S(1)}, f32[4,128]{1,0:T(4,128)S(1)}, u32[]{:S(2)}, u32[]{:S(2)}) collective-permute-start(f32[4,128]{1,0:T(4,128)S(1)} %multiply_add_fusion.10), channel_id=1, source_target_pairs={{0,2},{1,3},{2,0},{3,1},{4,6},{5,7},{6,4},{7,5},{8,10},{9,11},{10,... | collective-permute-start | bytes 6152 | tf_op jit(solution)/shard_map/ppermute | solution.py:386
  16.0 1.6 %collective-permute-start.2 = (f32[1,104,128]{2,1,0:T(8,128)S(1)}, f32[1,104,128]{2,1,0:T(8,128)S(1)}, u32[]{:S(2)}, u32[]{:S(2)}) collective-permute-start(f32[1,104,128]{2,1,0:T(8,128)S(1)} %get-tuple-element.66), channel_id=1, source_target_pairs={{0,8},{4,12},{8,0},{12,4},{16,24},{20,28},{24,16},{28,20},{1,9},{5... | collective-permute-start | bytes 159752 | tf_op jit(solution)/shard_map/ppermute | solution.py:386
  17.6 3.3 %shard_map.77 = (f32[32,128]{1,0:T(8,128)S(1)}, f32[4,128]{1,0:T(4,128)S(1)}, f32[4,128]{1,0:T(4,128)}, f32[512,4096]{1,0:T(8,128)S(1)}, f32[32,128]{1,0:T(8,128)S(1)}) custom-call(f32[512,4096]{1,0:T(8,128)S(1)} %get-tuple-element.57.score_ref, f32[4,128]{1,0:T(4,128)S(1)} %multiply_add_fusion.9.lse_ref, f32[3,4,128]{2,1,0:T(4,128)S(1)} %get-tuple-element.61.aux_ref.row_aux), custom_call_target="tpu_custom_call" | custom-call | tf_op jit(solution)/shard_map/pallas_call | solution.py:398
  20.9 11.9 %all_to_all.15.parts_ref = f32[8,32,128]{2,1,0:T(8,128)S(1)} all-to-all(f32[8,32,128]{2,1,0:T(8,128)S(1)} %broadcast_in_dim.9), channel_id=1, replica_groups=mesh['src'=8,'tgt'=4] {'src'}, dimensions={0} | all-to-all | bytes 262144 | tf_op jit(solution)/shard_map/all_to_all | solution.py:570
  32.8 1.1 shard_map.78
  33.9 3.2 %collective-permute-start.3 = (f32[4,128]{1,0:T(4,128)S(1)}, f32[4,128]{1,0:T(4,128)S(1)}, u32[]{:S(2)}, u32[]{:S(2)}) collective-permute-start(f32[4,128]{1,0:T(4,128)S(1)} %shard_map.78), channel_id=1, source_target_pairs={{0,1},{1,0},{2,3},{3,2},{4,5},{5,4},{6,7},{7,6},{8,9},{9,8},{10,11... | collective-permute-start | bytes 6152 | tf_op jit(solution)/shard_map/ppermute | solution.py:386
  38.0 4.3 %collective-permute-start.4 = (f32[4,128]{1,0:T(4,128)S(1)}, f32[4,128]{1,0:T(4,128)S(1)}, u32[]{:S(2)}, u32[]{:S(2)}) collective-permute-start(f32[4,128]{1,0:T(4,128)S(1)} %multiply_add_fusion.8), channel_id=1, source_target_pairs={{0,2},{1,3},{2,0},{3,1},{4,6},{5,7},{6,4},{7,5},{8,10},{9,11},{10,... | collective-permute-start | bytes 6152 | tf_op jit(solution)/shard_map/ppermute | solution.py:386
  42.7 1.2 %collective-permute-done.4 = f32[4,128]{1,0:T(4,128)S(1)} collective-permute-done((f32[4,128]{1,0:T(4,128)S(1)}, f32[4,128]{1,0:T(4,128)S(1)}, u32[]{:S(2)}, u32[]{:S(2)}) %collective-permute-start.4) | collective-permute-done | bytes 2080 | tf_op jit(solution)/shard_map/ppermute | solution.py:386
  43.9 1.6 %shard_map.79 = (f32[32,128]{1,0:T(8,128)S(1)}, f32[4,128]{1,0:T(4,128)}, f32[4,128]{1,0:T(4,128)}) custom-call(f32[512,4096]{1,0:T(8,128)S(1)} %get-tuple-element.57.score_ref, f32[512,4096]{1,0:T(8,128)S(1)} %get-tuple-element.62.kernel_ref, f32[32,128]{1,0:T(8,128)S(1)} %get-tuple-element.63.top_ref, f32[4,128]{1,0:T(4,128)S(1)} %get-tuple-element.64.base_ref, ...), custom_call_target="tpu_custom_call" | custom-call | tf_op jit(solution)/shard_map/pallas_call | solution.py:398
  45.5 2.5 %collective-permute-done.5 = f32[2,104,128]{2,1,0:T(8,128)S(1)} collective-permute-done((f32[2,104,128]{2,1,0:T(8,128)S(1)}, f32[2,104,128]{2,1,0:T(8,128)S(1)}, u32[]{:S(2)}, u32[]{:S(2)}) %collective-permute-start.5) | collective-permute-done | bytes 106528 | tf_op jit(solution)/shard_map/ppermute | solution.py:386
  48.0 9.7 %all_to_all.16.parts_ref = f32[8,32,128]{2,1,0:T(8,128)S(1)} all-to-all(f32[8,32,128]{2,1,0:T(8,128)S(1)} %broadcast_in_dim.10), channel_id=1, replica_groups=mesh['src'=8,'tgt'=4] {'src'}, dimensions={0} | all-to-all | bytes 262144 | tf_op jit(solution)/shard_map/all_to_all | solution.py:570
  57.7 1.1 shard_map.80
  58.8 3.0 %collective-permute-start.6 = (f32[4,128]{1,0:T(4,128)S(1)}, f32[4,128]{1,0:T(4,128)S(1)}, u32[]{:S(2)}, u32[]{:S(2)}) collective-permute-start(f32[4,128]{1,0:T(4,128)S(1)} %shard_map.80), channel_id=1, source_target_pairs={{0,1},{1,0},{2,3},{3,2},{4,5},{5,4},{6,7},{7,6},{8,9},{9,8},{10,11... | collective-permute-start | bytes 6152 | tf_op jit(solution)/shard_map/ppermute | solution.py:386
  62.7 2.9 %collective-permute-start.7 = (f32[4,128]{1,0:T(4,128)S(1)}, f32[4,128]{1,0:T(4,128)S(1)}, u32[]{:S(2)}, u32[]{:S(2)}) collective-permute-start(f32[4,128]{1,0:T(4,128)S(1)} %multiply_add_fusion.6), channel_id=1, source_target_pairs={{0,2},{1,3},{2,0},{3,1},{4,6},{5,7},{6,4},{7,5},{8,10},{9,11},{10,... | collective-permute-start | bytes 6152 | tf_op jit(solution)/shard_map/ppermute | solution.py:386
  65.8 1.4 %collective-permute-done.7 = f32[4,128]{1,0:T(4,128)S(1)} collective-permute-done((f32[4,128]{1,0:T(4,128)S(1)}, f32[4,128]{1,0:T(4,128)S(1)}, u32[]{:S(2)}, u32[]{:S(2)}) %collective-permute-start.7) | collective-permute-done | bytes 2080 | tf_op jit(solution)/shard_map/ppermute | solution.py:386
  67.2 1.6 %shard_map.81 = (f32[32,128]{1,0:T(8,128)S(1)}, f32[4,128]{1,0:T(4,128)}, f32[4,128]{1,0:T(4,128)}) custom-call(f32[512,4096]{1,0:T(8,128)S(1)} %get-tuple-element.57.score_ref, f32[512,4096]{1,0:T(8,128)S(1)} %get-tuple-element.62.kernel_ref, f32[32,128]{1,0:T(8,128)S(1)} %get-tuple-element.63.top_ref, f32[4,128]{1,0:T(4,128)S(1)} %get-tuple-element.64.base_ref, ...), custom_call_target="tpu_custom_call" | custom-call | tf_op jit(solution)/shard_map/pallas_call | solution.py:398
  68.8 3.8 %collective-permute-done.8.mine_ref = f32[4,104,128]{2,1,0:T(8,128)S(1)} collective-permute-done((f32[4,104,128]{2,1,0:T(8,128)S(1)}, f32[4,104,128]{2,1,0:T(8,128)S(1)}, u32[]{:S(2)}, u32[]{:S(2)}) %collective-permute-start.8) | collective-permute-done | bytes 213024 | tf_op jit(solution)/shard_map/ppermute | solution.py:386
  72.6 9.7 %all_to_all.17.parts_ref = f32[8,32,128]{2,1,0:T(8,128)S(1)} all-to-all(f32[8,32,128]{2,1,0:T(8,128)S(1)} %broadcast_in_dim.11), channel_id=1, replica_groups=mesh['src'=8,'tgt'=4] {'src'}, dimensions={0} | all-to-all | bytes 262144 | tf_op jit(solution)/shard_map/all_to_all | solution.py:570
  82.4 1.1 shard_map.82
  83.5 3.0 %collective-permute-start.10 = (f32[4,128]{1,0:T(4,128)S(1)}, f32[4,128]{1,0:T(4,128)S(1)}, u32[]{:S(2)}, u32[]{:S(2)}) collective-permute-start(f32[4,128]{1,0:T(4,128)S(1)} %shard_map.82), channel_id=1, source_target_pairs={{0,1},{1,0},{2,3},{3,2},{4,5},{5,4},{6,7},{7,6},{8,9},{9,8},{10,11... | collective-permute-start | bytes 6152 | tf_op jit(solution)/shard_map/ppermute | solution.py:386
  87.3 2.9 %collective-permute-start.11 = (f32[4,128]{1,0:T(4,128)S(1)}, f32[4,128]{1,0:T(4,128)S(1)}, u32[]{:S(2)}, u32[]{:S(2)}) collective-permute-start(f32[4,128]{1,0:T(4,128)S(1)} %multiply_add_fusion.4), channel_id=1, source_target_pairs={{0,2},{1,3},{2,0},{3,1},{4,6},{5,7},{6,4},{7,5},{8,10},{9,11},{10,... | collective-permute-start | bytes 6152 | tf_op jit(solution)/shard_map/ppermute | solution.py:386
  90.2 1.0 shard_map.83
  91.7 1.2 %shard_map.84 = (f32[32,128]{1,0:T(8,128)S(1)}, f32[4,128]{1,0:T(4,128)S(1)}, f32[4,128]{1,0:T(4,128)S(1)}) custom-call(f32[512,4096]{1,0:T(8,128)S(1)} %get-tuple-element.57.score_ref, f32[512,4096]{1,0:T(8,128)S(1)} %get-tuple-element.62.kernel_ref, f32[32,128]{1,0:T(8,128)S(1)} %get-tuple-element.63.top_ref, f32[4,128]{1,0:T(4,128)S(1)} %get-tuple-element.64.base_ref, ...), custom_call_target="tpu_custom_call" | custom-call | tf_op jit(solution)/shard_map/pallas_call | solution.py:398
  93.1 1.0 shard_map.85
  94.1 2.7 %collective-permute-done.13 = f32[36,128]{1,0:T(8,128)S(1)} collective-permute-done((f32[36,128]{1,0:T(8,128)S(1)}, f32[36,128]{1,0:T(8,128)S(1)}, u32[]{:S(2)}, u32[]{:S(2)}) %collective-permute-start.13) | collective-permute-done | bytes 18464 | tf_op jit(solution)/shard_map/ppermute | solution.py:386
  97.3 1.0 shard_map.86
  98.4 3.3 %collective-permute-done.14 = f32[40,128]{1,0:T(8,128)S(1)} collective-permute-done((f32[40,128]{1,0:T(8,128)S(1)}, f32[40,128]{1,0:T(8,128)S(1)}, u32[]{:S(2)}, u32[]{:S(2)}) %collective-permute-start.14) | collective-permute-done | bytes 20512 | tf_op jit(solution)/shard_map/ppermute | solution.py:386
  102.0 1.0 shard_map.87
  103.0 2.6 %collective-permute-done.15 = f32[48,128]{1,0:T(8,128)S(1)} collective-permute-done((f32[48,128]{1,0:T(8,128)S(1)}, f32[48,128]{1,0:T(8,128)S(1)}, u32[]{:S(2)}, u32[]{:S(2)}) %collective-permute-start.15) | collective-permute-done | bytes 24608 | tf_op jit(solution)/shard_map/ppermute | solution.py:386
  105.6 3.3 %shard_map.88 = (f32[50,512]{1,0:T(8,128)}, f32[4,128]{1,0:T(4,128)}, f32[32,128]{1,0:T(8,128)}) custom-call(f32[512,1024]{1,0:T(8,128)S(1)} %get-tuple-element.87.refs_0_, f32[512,1024]{1,0:T(8,128)S(1)} %get-tuple-element.94.refs_1_, f32[512,1024]{1,0:T(8,128)S(1)} %get-tuple-element.98.refs_2_, f32[512,1024]{1,0:T(8,128)S(1)} %get-tuple-element.101.refs_3_, ...), custom_call_target="tpu_custom_call" | custom-call | flops 2415919104 | tf_op jit(solution)/shard_map/pallas_call | solution.py:398
  (38 shorter events, 5.2 us)
Async XLA Ops:
  6.8 1.3 %collective-permute-start = (f32[4,128]{1,0:T(4,128)S(1)}, f32[4,128]{1,0:T(4,128)S(1)}, u32[]{:S(2)}, u32[]{:S(2)}) collective-permute-start(f32[4,128]{1,0:T(4,128)S(1)} %get-tuple-element.58), channel_id=1, source_target_pairs={{0,1},{1,0},{2,3},{3,2},{4,5},{5,4},{6,7},{7,6},{8,9},{9,8},{10,11... | collective-permute-start | bytes 6152 | tf_op jit(solution)/shard_map/ppermute | solution.py:386
  8.1 9.4 %collective-permute-start.1 = (f32[4,128]{1,0:T(4,128)S(1)}, f32[4,128]{1,0:T(4,128)S(1)}, u32[]{:S(2)}, u32[]{:S(2)}) collective-permute-start(f32[4,128]{1,0:T(4,128)S(1)} %multiply_add_fusion.10), channel_id=1, source_target_pairs={{0,2},{1,3},{2,0},{3,1},{4,6},{5,7},{6,4},{7,5},{8,10},{9,11},{10,... | collective-permute-start | bytes 6152 | tf_op jit(solution)/shard_map/ppermute | solution.py:386
  16.0 4.9 %collective-permute-start.2 = (f32[1,104,128]{2,1,0:T(8,128)S(1)}, f32[1,104,128]{2,1,0:T(8,128)S(1)}, u32[]{:S(2)}, u32[]{:S(2)}) collective-permute-start(f32[1,104,128]{2,1,0:T(8,128)S(1)} %get-tuple-element.66), channel_id=1, source_target_pairs={{0,8},{4,12},{8,0},{12,4},{16,24},{20,28},{24,16},{28,20},{1,9},{5... | collective-permute-start | bytes 159752 | tf_op jit(solution)/shard_map/ppermute | solution.py:386
  33.9 4.0 %collective-permute-start.3 = (f32[4,128]{1,0:T(4,128)S(1)}, f32[4,128]{1,0:T(4,128)S(1)}, u32[]{:S(2)}, u32[]{:S(2)}) collective-permute-start(f32[4,128]{1,0:T(4,128)S(1)} %shard_map.78), channel_id=1, source_target_pairs={{0,1},{1,0},{2,3},{3,2},{4,5},{5,4},{6,7},{7,6},{8,9},{9,8},{10,11... | collective-permute-start | bytes 6152 | tf_op jit(solution)/shard_map/ppermute | solution.py:386
  38.0 5.9 %collective-permute-start.4 = (f32[4,128]{1,0:T(4,128)S(1)}, f32[4,128]{1,0:T(4,128)S(1)}, u32[]{:S(2)}, u32[]{:S(2)}) collective-permute-start(f32[4,128]{1,0:T(4,128)S(1)} %multiply_add_fusion.8), channel_id=1, source_target_pairs={{0,2},{1,3},{2,0},{3,1},{4,6},{5,7},{6,4},{7,5},{8,10},{9,11},{10,... | collective-permute-start | bytes 6152 | tf_op jit(solution)/shard_map/ppermute | solution.py:386
  42.3 5.7 %collective-permute-start.5 = (f32[2,104,128]{2,1,0:T(8,128)S(1)}, f32[2,104,128]{2,1,0:T(8,128)S(1)}, u32[]{:S(2)}, u32[]{:S(2)}) collective-permute-start(f32[2,104,128]{2,1,0:T(8,128)S(1)} %pad_maximum_fusion.1), channel_id=1, source_target_pairs={{0,16},{4,20},{8,24},{12,28},{16,0},{20,4},{24,8},{28,12},{1,17},{... | collective-permute-start | bytes 319496 | tf_op jit(solution)/shard_map/ppermute | solution.py:386
  58.8 3.8 %collective-permute-start.6 = (f32[4,128]{1,0:T(4,128)S(1)}, f32[4,128]{1,0:T(4,128)S(1)}, u32[]{:S(2)}, u32[]{:S(2)}) collective-permute-start(f32[4,128]{1,0:T(4,128)S(1)} %shard_map.80), channel_id=1, source_target_pairs={{0,1},{1,0},{2,3},{3,2},{4,5},{5,4},{6,7},{7,6},{8,9},{9,8},{10,11... | collective-permute-start | bytes 6152 | tf_op jit(solution)/shard_map/ppermute | solution.py:386
  62.7 4.5 %collective-permute-start.7 = (f32[4,128]{1,0:T(4,128)S(1)}, f32[4,128]{1,0:T(4,128)S(1)}, u32[]{:S(2)}, u32[]{:S(2)}) collective-permute-start(f32[4,128]{1,0:T(4,128)S(1)} %multiply_add_fusion.6), channel_id=1, source_target_pairs={{0,2},{1,3},{2,0},{3,1},{4,6},{5,7},{6,4},{7,5},{8,10},{9,11},{10,... | collective-permute-start | bytes 6152 | tf_op jit(solution)/shard_map/ppermute | solution.py:386
  65.5 7.1 %collective-permute-start.8 = (f32[4,104,128]{2,1,0:T(8,128)S(1)}, f32[4,104,128]{2,1,0:T(8,128)S(1)}, u32[]{:S(2)}, u32[]{:S(2)}) collective-permute-start(f32[4,104,128]{2,1,0:T(8,128)S(1)} %pad_maximum_fusion.mine_ref), channel_id=1, source_target_pairs={{0,4},{4,0},{8,12},{12,8},{16,20},{20,16},{24,28},{28,24},{1,5},{5... | collective-permute-start | bytes 638984 | tf_op jit(solution)/shard_map/ppermute | solution.py:386
  67.1 5.5 %collective-permute-start.9 = (f32[4,104,128]{2,1,0:T(8,128)S(1)}, f32[4,104,128]{2,1,0:T(8,128)S(1)}, u32[]{:S(2)}, u32[]{:S(2)}) collective-permute-start(f32[4,104,128]{2,1,0:T(8,128)S(1)} %pad_maximum_fusion.mine_ref), channel_id=1, source_target_pairs={{0,1},{1,0},{2,3},{3,2},{4,5},{5,4},{6,7},{7,6},{8,9},{9,8},{10,11... | collective-permute-start | bytes 638984 | tf_op jit(solution)/shard_map/ppermute | solution.py:386
  83.5 3.8 %collective-permute-start.10 = (f32[4,128]{1,0:T(4,128)S(1)}, f32[4,128]{1,0:T(4,128)S(1)}, u32[]{:S(2)}, u32[]{:S(2)}) collective-permute-start(f32[4,128]{1,0:T(4,128)S(1)} %shard_map.82), channel_id=1, source_target_pairs={{0,1},{1,0},{2,3},{3,2},{4,5},{5,4},{6,7},{7,6},{8,9},{9,8},{10,11... | collective-permute-start | bytes 6152 | tf_op jit(solution)/shard_map/ppermute | solution.py:386
  86.4 6.5 %collective-permute-start.12 = (f32[4,104,128]{2,1,0:T(8,128)S(1)}, f32[4,104,128]{2,1,0:T(8,128)S(1)}, u32[]{:S(2)}, u32[]{:S(2)}) collective-permute-start(f32[4,104,128]{2,1,0:T(8,128)S(1)} %collective-permute-done.8.mine_ref), channel_id=1, source_target_pairs={{0,1},{1,0},{2,3},{3,2},{4,5},{5,4},{6,7},{7,6},{8,9},{9,8},{10,11... | collective-permute-start | bytes 638984 | tf_op jit(solution)/shard_map/ppermute | solution.py:386
  87.3 4.4 %collective-permute-start.11 = (f32[4,128]{1,0:T(4,128)S(1)}, f32[4,128]{1,0:T(4,128)S(1)}, u32[]{:S(2)}, u32[]{:S(2)}) collective-permute-start(f32[4,128]{1,0:T(4,128)S(1)} %multiply_add_fusion.4), channel_id=1, source_target_pairs={{0,2},{1,3},{2,0},{3,1},{4,6},{5,7},{6,4},{7,5},{8,10},{9,11},{10,... | collective-permute-start | bytes 6152 | tf_op jit(solution)/shard_map/ppermute | solution.py:386
  93.0 3.8 %collective-permute-start.13 = (f32[36,128]{1,0:T(8,128)S(1)}, f32[36,128]{1,0:T(8,128)S(1)}, u32[]{:S(2)}, u32[]{:S(2)}) collective-permute-start(f32[36,128]{1,0:T(8,128)S(1)} %pad_maximum_fusion.3), channel_id=1, source_target_pairs={{0,8},{4,12},{8,0},{12,4},{16,24},{20,28},{24,16},{28,20},{1,9},{5... | collective-permute-start | bytes 55304 | tf_op jit(solution)/shard_map/ppermute | solution.py:386
  96.9 4.7 %collective-permute-start.14 = (f32[40,128]{1,0:T(8,128)S(1)}, f32[40,128]{1,0:T(8,128)S(1)}, u32[]{:S(2)}, u32[]{:S(2)}) collective-permute-start(f32[40,128]{1,0:T(8,128)S(1)} %pad_maximum_fusion.4), channel_id=1, source_target_pairs={{0,16},{4,20},{8,24},{12,28},{16,0},{20,4},{24,8},{28,12},{1,17},{... | collective-permute-start | bytes 61448 | tf_op jit(solution)/shard_map/ppermute | solution.py:386
  101.7 3.9 %collective-permute-start.15 = (f32[48,128]{1,0:T(8,128)S(1)}, f32[48,128]{1,0:T(8,128)S(1)}, u32[]{:S(2)}, u32[]{:S(2)}) collective-permute-start(f32[48,128]{1,0:T(8,128)S(1)} %pad_maximum_fusion.2), channel_id=1, source_target_pairs={{0,4},{4,0},{8,12},{12,8},{16,20},{20,16},{24,28},{28,24},{1,5},{5... | collective-permute-start | bytes 73736 | tf_op jit(solution)/shard_map/ppermute | solution.py:386
where the time goes:
time: 110 us; the launch traced here: 109 us
  blocking collectives  31.4 us (29%)
  starting transfers between devices  30.8 us (28%)
  Pallas kernels  23.8 us (22%)
  waiting for transfers between devices  21.2 us (19%)
  between operations  1.46 us (1%)
    all_to_all x3, blocking collectives, shards(): lse = lax.all_to_all(lse, 'src', 0, 0, tiled=True)  31.4 us
    ppermute x16, starting transfers between devices, swap(): lax.ppermute(value, axis, [(i, i ^ step) for i in range(lax.axis_size(axi...  30.8 us
    ppermute x16, waiting for transfers between devices, swap(): lax.ppermute(value, axis, [(i, i ^ step) for i in range(lax.axis_size(axi...  21.2 us
    pallas_call x12, Pallas kernels, call(): pl.pallas_call(kernel, out_shape=[buffer(pltpu.VMEM if pin else jax.Shape...  18.3 us
    pallas_call x1, Pallas kernels, shards(): pl.pallas_call(first_kernel, out_shape=[pltpu.VMEM(shape, jnp.float32) fo...  5.51 us
  transfers between devices with their start and end apart: 16, of which 12 were waited for; matrix products, arithmetic and copies ran while one was open for 0% of the time, Pallas kernels for 11%

commit v1 on v0

--- a/solution.py
+++ b/solution.py
@@ -15,9 +15,10 @@
 SCALE = LOG2E / EPS
 LANES = 128
 DEPTH = 64
-FACTOR_MAX = 2.0**20
-SUM_MIN = 2.0**-70
-TOTAL_MAX = 2.0**100
+SHIFT = 40.0
+ROW_FACTOR_MAX = 2.0**20
+COL_FACTOR_MAX = 2.0**60
+SUM_MIN = 2.0**-30
 VMEM_LIMIT = 14 * 1024 * 1024
 
 VMEM_SPEC = pl.BlockSpec(memory_space=pltpu.VMEM)
@@ -66,10 +67,7 @@
         here = pl.ds(pl.multiple_of(i * 8, 8), 8)
         z = []
         for k in range(cols // LANES):
-            value = score_ref[here, k * LANES : (k + 1) * LANES]
-            if add_ref is not None:
-                value = value + add_ref[k : k + 1, :]
-            z.append(value)
+            z.append(score_ref[here, k * LANES : (k + 1) * LANES] + add_ref[k : k + 1, :])
         peak = functools.reduce(jnp.maximum, z)
         peak_ref[here, :] = peak
         total_ref[here, :] = functools.reduce(jnp.add, [jnp.exp2(v - peak) for v in z])
@@ -96,7 +94,7 @@
 
         start = (jnp.full((8, LANES), -jnp.inf, jnp.float32),) * group
         tops = lax.fori_loop(0, rows // (8 * tall), peaks, start)
-        tops = [jnp.max(t, axis=0, keepdims=True) for t in tops]
+        tops = [jnp.max(t, axis=0, keepdims=True) - SHIFT for t in tops]
         wide_tops = [jnp.broadcast_to(t, (8, LANES)) for t in tops]
 
         def totals(i, sums):
@@ -202,23 +200,23 @@
         score_ref[:, here] = score
         return [score[:, k : k + LANES] for k in range(0, size, LANES)]
 
-    first = scores(0)
-    peak = jnp.max(functools.reduce(jnp.maximum, first), axis=1, keepdims=True)
-    peak_ref[...] = jnp.broadcast_to(peak, peak_ref.shape)
-    total_ref[...] = functools.reduce(jnp.add, [jnp.exp2(z - peak_ref[...]) for z in first])
+    peak_ref[...] = jnp.full(peak_ref.shape, 2.0 * NEG, jnp.float32)
+    total_ref[...] = jnp.zeros(total_ref.shape, jnp.float32)
 
     def block(c, _):
-        total_ref[...] += functools.reduce(jnp.add, [jnp.exp2(z - peak_ref[...]) for z in scores(c)])
+        z = scores(c)
+        before = peak_ref[...]
+        peak = functools.reduce(jnp.maximum, z, before)
+        total_ref[...] = functools.reduce(
+            jnp.add, [jnp.exp2(v - peak) for v in z], total_ref[...] * jnp.exp2(before - peak)
+        )
+        peak_ref[...] = peak
         return 0
 
-    lax.fori_loop(1, cols // size, block, 0)
+    lax.fori_loop(0, cols // size, block, 0)
     share = own_ref.shape[1]
     own_ref[0:dims, :] = tgt_ref[:, pl.ds(pl.multiple_of(lax.axis_index("src") * share, share), share)]
     fold_lanes(peak_ref, total_ref, lse_ref)
-
-    @pl.when(jnp.logical_not(jnp.max(total_ref[...]) <= TOTAL_MAX))
-    def _():
-        row_lse(score_ref, None, peak_ref, total_ref, lse_ref)
 
 
 def slab_kernel(
@@ -288,9 +286,9 @@
         out_ref[k : k + 1, :] = jnp.sum(u, axis=0, keepdims=True)
 
 
-def out_of_range(total, needed, factor):
+def out_of_range(total, needed, factor, most):
     small = jnp.where(needed & jnp.logical_not(total >= SUM_MIN), 1.0, 0.0)
-    large = jnp.where(factor <= FACTOR_MAX, 0.0, 1.0)
+    large = jnp.where(factor <= most, 0.0, 1.0)
     return jnp.max(jnp.maximum(jnp.max(small, axis=0, keepdims=True), jnp.max(large, axis=0, keepdims=True))) > 0.5
 
 
@@ -315,7 +313,7 @@
     col_sums(kernel_ref, col_ref, out_ref)
     total = out_ref[...]
     top = top_ref[...]
-    redo = out_of_range(total, top > 0.5 * NEG, factor_ref[...])
+    redo = out_of_range(total, top > 0.5 * NEG, factor_ref[...], ROW_FACTOR_MAX)
     out_ref[...] = jnp.where(total > 0, top + jnp.log2(total), NEG)
 
     @pl.when(redo)
@@ -324,20 +322,23 @@
         col_lse(score_ref, col_ref, out_ref)
 
 
+def merged(parts):
+    peak = jnp.max(parts, axis=0)
+    return peak + jnp.log2(jnp.sum(jnp.exp2(parts - peak[None]), axis=0))
+
+
 def row_kernel(
     score_ref, kernel_ref, top_ref, base_ref, parts_ref, row_aux, col_aux, out_ref,
     g_ref, factor_ref, peak_ref, total_ref,
 ):
-    parts = parts_ref[...]
-    peak = jnp.max(parts, axis=0)
-    lse = peak + jnp.log2(jnp.sum(jnp.exp2(parts - peak[None]), axis=0))
+    lse = merged(parts_ref[...])
     g_ref[...] = col_aux[1] - lse * col_aux[0]
-    factor_ref[...] = jnp.where(col_aux[0] > 0, jnp.exp2(top_ref[...] - lse), 0.0)
+    factor_ref[...] = jnp.where(col_aux[0] > 0, jnp.exp2(top_ref[...] - lse + 2.0 * SHIFT), 0.0)
     row_sums(kernel_ref, factor_ref, total_ref, out_ref)
     total = out_ref[...]
-    redo = out_of_range(total, row_aux[2] > 0, factor_ref[...])
+    redo = out_of_range(total, row_aux[2] > 0, factor_ref[...], COL_FACTOR_MAX)
     log_b = col_aux[1, 0:1, 0:1]
-    out_ref[...] = jnp.where(total > 0, jnp.log2(total) - base_ref[...] + log_b, NEG)
+    out_ref[...] = jnp.where(total > 0, jnp.log2(total) - 2.0 * SHIFT - base_ref[...] + log_b, NEG)
 
     @pl.when(redo)
     def _():
@@ -345,31 +346,35 @@
 
 
 def last_kernel(*refs, pieces):
-    slabs, refs = refs[:pieces], refs[pieces:]
-    terms, refs = refs[:pieces], refs[pieces:]
-    f_all_ref, lse_ref, aux_ref, f_ref, out_ref, f_out, g_out, own_ref, col_ref, sum_ref = refs
+    slabs, refs = refs[: len(pieces)], refs[len(pieces) :]
+    terms, refs = refs[: len(pieces)], refs[len(pieces) :]
+    parts_ref, aux_ref, f_ref, *_, out_ref, f_out, g_out, lse_ref, own_ref, col_ref, sum_ref = refs
+    n_col = aux_ref.shape[1]
+    lse = merged(parts_ref[:, 0:n_col, :])
+    lse_ref[...] = lse
     f_out[...] = f_ref[...] * (1.0 / SCALE)
-    g_out[...] = (aux_ref[1] - lse_ref[...] * aux_ref[0]) * (1.0 / SCALE)
+    g_out[...] = (aux_ref[1] - lse * aux_ref[0]) * (1.0 / SCALE)
+    me = lax.axis_index("src")
     n_own = own_ref.shape[0]
     for k in range(n_own):
-        spot = pl.ds(lax.axis_index("src") * n_own + k, 1)
+        spot = pl.ds(me * n_own + k, 1)
         own_ref[k : k + 1, :] = jnp.where(aux_ref[0, spot, :] > 0, -lse_ref[spot, :], NEG)
     to_sublanes(own_ref, col_ref)
-    spot = 0
-    for slab_ref, terms_ref in zip(slabs, terms):
+    for i, (slab_ref, terms_ref, offsets) in enumerate(zip(slabs, terms, pieces)):
         high, mid = [], []
-        first = spot == 0
-        for start in range(0, slab_ref.shape[1], LANES):
-            add = col_ref[...] + f_all_ref[spot : spot + 1, :]
-            parts = split(jnp.exp2(slab_ref[:, start : start + LANES] + add))
-            high.append(parts[0])
-            mid.append(parts[1])
-            spot += 1
+        start = 0
+        for offset in offsets:
+            for row in range(n_col, parts_ref.shape[1]):
+                add = col_ref[...] + parts_ref[me ^ offset, row : row + 1, :]
+                term = split(jnp.exp2(slab_ref[:, start : start + LANES] + add))
+                high.append(term[0])
+                mid.append(term[1])
+                start += LANES
         sums = jnp.dot(
             jnp.concatenate(high + mid, axis=1), jnp.concatenate([terms_ref[...]] * 2, axis=0),
             preferred_element_type=jnp.float32,
         )
-        if first:
+        if i == 0:
             sum_ref[...] = sums
         else:
             sum_ref[...] += sums
@@ -416,46 +421,55 @@
         self.own = own
         self.steps = list(steps)
         self.coming = None
+        self.come = None
         self.mine = []
         self.theirs = []
         self.ready = []
         self.todo = []
         self.terms = []
+        self.tokens = []
+        self.done = []
+        self.offsets = [0]
+        for bit in steps:
+            self.offsets += [offset ^ bit for offset in self.offsets]
         self.rows = rows
         self.n_half = n_half
         self.slabs = []
 
+    def launch(self):
+        self.coming = swap(self.parts, "src", self.steps.pop(0))
+        if not self.steps:
+            self.mine = [self.parts]
+            self.trade()
+
     def start(self, value, axis, step):
         if self.coming is not None or not self.steps:
             return swap(value, axis, step)
-        value, parts = tie(value, self.parts)
-        if self.mine:
-            self.mine = [parts]
-        self.parts = parts
+        value, self.parts = tie(value, self.parts)
         other = swap(value, axis, step)
-        self.coming = swap(parts, "src", self.steps.pop(0))
+        self.launch()
         return other
 
     def land(self, value):
-        if self.coming is None:
+        if self.coming is not None:
+            value, self.come = tie(value, self.coming)
+            self.coming = None
+        return value
+
+    def join(self, value):
+        if self.come is None:
             return value
-        value, coming = tie(value, self.coming)
-        self.coming = None
+        value, parts, come = tie(value, self.parts, self.come)
+        self.come = None
         if self.steps:
-            self.parts = jnp.concatenate([self.parts, coming], axis=0)
-            if len(self.steps) == 1:
-                self.mine = [self.parts]
+            self.parts = jnp.concatenate([parts, come], axis=0)
         else:
-            self.mine.append(coming)
+            self.mine.append(come)
+            self.trade()
         return value
 
-    def trade(self, value):
-        group = len(self.theirs)
-        if group == len(self.mine):
-            return value
-        value, self.mine[group] = tie(value, self.mine[group])
-        self.theirs.append(swap(self.mine[group], "tgt", 1))
-        return value
+    def trade(self):
+        self.theirs.append(swap(self.mine[-1], "tgt", 1))
 
     def traded(self, value):
         for group in range(len(self.ready), len(self.theirs)):
@@ -478,6 +492,7 @@
             12 * DEPTH * share * size * rows,
         )
         self.terms.append(terms)
+        self.done.append(self.offsets[group * mine.shape[0] + first :][:size])
         self.slabs.append(slab)
         return token
 
@@ -485,26 +500,27 @@
         if not self.todo:
             return swap(value, axis, step)
         value, self.own = tie(value, self.own)
-        other = swap(value, axis, step)
-        other, _ = tie(other, self.piece())
-        return other
+        return self.pieces(swap(value, axis, step))
+
+    def pieces(self, value):
+        while self.todo:
+            value, token = tie(value, self.piece())
+            self.tokens.append(token)
+        return value
 
     def finish(self, value):
-        while self.steps or self.coming is not None:
-            if self.coming is None:
-                self.coming = swap(self.parts, "src", self.steps.pop(0))
-            value = self.land(value)
-        while len(self.theirs) < len(self.mine):
-            value = self.trade(value)
-        self.traded(value)
-        while self.todo:
-            self.piece()
+        while self.steps or self.coming is not None or self.come is not None:
+            if self.coming is None and self.come is None:
+                self.launch()
+            value = self.join(self.land(value))
+        return self.pieces(self.traded(value))
 
 
 def shards(sources, targets, pair_active, count_src, count_tgt):
     dims, rows = sources.shape
     cols = targets.shape[1]
-    share = cols // lax.axis_size("src")
+    n_src = lax.axis_size("src")
+    share = cols // n_src
     column = (rows, LANES)
     by_row = (rows // LANES, LANES)
     by_col = (cols // LANES, LANES)
@@ -536,22 +552,20 @@
         cost_estimate=pl.CostEstimate(flops=12 * DEPTH * pairs, bytes_accessed=0, transcendentals=pairs),
     )(*hbm, pair_active)
     over_tgt = doubling(lax.axis_size("tgt"))
-    over_src = doubling(lax.axis_size("src"))
+    over_src = doubling(n_src)
     over_src = over_src[1:] + over_src[:1]
     side = Beside(half, own, over_src, rows, n_half)
     for step in range(ITERS):
+        lse = side.join(lse)
         for bit in over_tgt:
-            if step == ITERS - 1 and bit == over_tgt[0]:
-                lse = side.trade(lse)
             if bit != over_tgt[-1]:
                 other = swap(lse, "tgt", bit)
             elif step < ITERS - 1:
                 other = side.start(lse, "tgt", bit)
             else:
-                other = side.work(lse, "tgt", bit)
+                other = side.work(side.traded(lse), "tgt", bit)
             lse = merge(lse, other)
-        if step == ITERS - 2:
-            lse = side.trade(lse)
+        lse = side.traded(lse)
         if step == 0:
             lse, base, masked, kernel, top = call(
                 first_col_kernel,
@@ -565,27 +579,22 @@
                 [by_row, column], [score, kernel, top, base, lse, row_aux], 0,
             )
         if step < ITERS - 1:
-            lse = side.traded(side.land(lse))
-            lse = jnp.broadcast_to(lse, (lax.axis_size("src"), *by_col))
-            lse = lax.all_to_all(lse, "src", 0, 0, tiled=True)
+            lse = side.land(side.pieces(lse))
+            lse = lax.all_to_all(jnp.broadcast_to(lse, (n_src, *by_col)), "src", 0, 0, tiled=True)
             (lse,) = call(
                 row_kernel,
                 [by_row],
                 [by_col, by_col, column, column],
                 [score, kernel, top, base, lse, row_aux, col_aux], 0,
             )
-    lse = side.traded(lse)
-    for bit in over_src:
-        both = jnp.concatenate([lse, masked], axis=0)
-        other = side.work(both, "src", bit)
-        lse = merge(lse, other[: by_col[0]])
-        masked = jnp.concatenate([masked, other[by_col[0] :]], axis=0)
-    side.finish(lse)
+    lse = side.finish(lse)
+    both = jnp.concatenate([lse, masked], axis=0)
+    both = lax.all_to_all(jnp.broadcast_to(both, (n_src, *both.shape)), "src", 0, 0, tiled=True)
     ancestors, f, g = call(
-        functools.partial(last_kernel, pieces=len(side.slabs)),
+        functools.partial(last_kernel, pieces=side.done),
         [(dims, share), by_row, by_col],
-        [(share // LANES, LANES), (share, LANES), (share, 3 * DEPTH)],
-        [*side.slabs, *side.terms, masked, lse, col_aux, f],
+        [by_col, (share // LANES, LANES), (share, LANES), (share, 3 * DEPTH)],
+        [*side.slabs, *side.terms, both, col_aux, f, *side.tokens],
         18 * DEPTH * pairs, pairs, pin=False,
     )
     return (f.reshape(rows), g.reshape(cols), ancestors)

time: 110 us -> 93.1 us (0.85)
  starting transfers between devices: 30.8 us -> 10.2 us
  blocking collectives: 31.4 us -> 43.6 us
  waiting for transfers between devices: 21.2 us -> 13.1 us
    ppermute x16 -> x13, starting transfers between devices: 30.8 us -> 10.2 us  [swap(): lax.ppermute(value, axis, [(i, i ^ step) for i in range(lax.axis_size(axi...]
    all_to_all x3 -> x4, blocking collectives: 31.4 us -> 43.6 us  [the longest x3 33.2 us: shards(): lax.all_to_all(jnp.broadcast_to(lse, (n_src, *by_col)), 'src', 0, 0, tile...]
    ppermute x16 -> x13, waiting for transfers between devices: 21.2 us -> 13.1 us  [swap(): lax.ppermute(value, axis, [(i, i ^ step) for i in range(lax.axis_size(axi...]
  transfers between devices with their start and end apart: 16 -> 13, of which waited for: 12 -> 10; matrix products, arithmetic and copies ran while one was open for 0% -> 0% of each run, Pallas kernels for 11% -> 11%
where the time goes in v1:
time: 93.1 us; the launch traced here: 92.8 us
  blocking collectives  43.6 us (47%)
  Pallas kernels  24.3 us (26%)
  waiting for transfers between devices  13.1 us (14%)
  starting transfers between devices  10.2 us (11%)
  between operations  1.44 us (2%)
    all_to_all x3, blocking collectives, shards(): lax.all_to_all(jnp.broadcast_to(lse, (n_src, *by_col)), 'src', 0, 0, tile...  33.2 us
    pallas_call x12, Pallas kernels, call(): pl.pallas_call(kernel, out_shape=[buffer(pltpu.VMEM if pin else jax.Shape...  18.4 us
    ppermute x13, waiting for transfers between devices, swap(): lax.ppermute(value, axis, [(i, i ^ step) for i in range(lax.axis_size(axi...  13.1 us
    all_to_all x1, blocking collectives, shards(): lax.all_to_all(jnp.broadcast_to(both, (n_src, *both.shape)), 'src', 0, 0,...  10.4 us
    ppermute x13, starting transfers between devices, swap(): lax.ppermute(value, axis, [(i, i ^ step) for i in range(lax.axis_size(axi...  10.2 us
    pallas_call x1, Pallas kernels, shards(): pl.pallas_call(first_kernel, out_shape=[pltpu.VMEM(shape, jnp.float32) fo...  5.95 us
  transfers between devices with their start and end apart: 13, of which 10 were waited for; matrix products, arithmetic and copies ran while one was open for 0% of the time, Pallas kernels for 11%

profile of v1, /device:TPU:0, one launch (start us, length us, event | category | flops | bytes accessed | tf_op | source)
XLA Modules:
  0.0 92.8 jit_solution(556603003716845128)
XLA Ops:
  1.3 5.9 %shard_map.76 = (f32[512,4096]{1,0:T(8,128)S(1)}, f32[4,128]{1,0:T(4,128)S(1)}, f32[3,4,128]{2,1,0:T(4,128)S(1)}, f32[3,32,128]{2,1,0:T(8,128)S(1)}, f32[64,512]{1,0:T(8,128)S(1)}, /*index=5*/f32[1,104,128]{2,1,0:T(8,128)S(1)}) custom-call(f32[50,512]{1,0:T(8,128)} %src_hbm.1, f32[50,4096]{1,0:T(8,128)} %tgt_hbm.1, s32[8]{0:T(128)} %count_src_hbm.1, ...), custom_call_target="tpu_custom_call" | custom-call | flops 1610612736 | tf_op jit(solution)/shard_map/pallas_call | solution.py:532
  7.2 0.5 collective-permute-start
  7.7 0.8 collective-permute-done
  8.6 2.9 %collective-permute-start.1 = (f32[4,128]{1,0:T(4,128)S(1)}, f32[4,128]{1,0:T(4,128)S(1)}, u32[]{:S(2)}, u32[]{:S(2)}) collective-permute-start(f32[4,128]{1,0:T(4,128)S(1)} %multiply_add_fusion.7), channel_id=1, source_target_pairs={{0,2},{1,3},{2,0},{3,1},{4,6},{5,7},{6,4},{7,5},{8,10},{9,11},{10,... | collective-permute-start | bytes 6152 | tf_op jit(solution)/shard_map/ppermute | solution.py:391
  11.5 1.6 %collective-permute-start.2 = (f32[1,104,128]{2,1,0:T(8,128)S(1)}, f32[1,104,128]{2,1,0:T(8,128)S(1)}, u32[]{:S(2)}, u32[]{:S(2)}) collective-permute-start(f32[1,104,128]{2,1,0:T(8,128)S(1)} %get-tuple-element.82), channel_id=1, source_target_pairs={{0,8},{4,12},{8,0},{12,4},{16,24},{20,28},{24,16},{28,20},{1,9},{5... | collective-permute-start | bytes 159752 | tf_op jit(solution)/shard_map/ppermute | solution.py:391
  13.1 3.4 %shard_map.77 = (f32[32,128]{1,0:T(8,128)S(1)}, f32[4,128]{1,0:T(4,128)S(1)}, f32[4,128]{1,0:T(4,128)}, f32[512,4096]{1,0:T(8,128)S(1)}, f32[32,128]{1,0:T(8,128)S(1)}) custom-call(f32[512,4096]{1,0:T(8,128)S(1)} %get-tuple-element.68.score_ref, f32[4,128]{1,0:T(4,128)S(1)} %multiply_add_fusion.6.lse_ref, f32[3,4,128]{2,1,0:T(4,128)S(1)} %get-tuple-element.72.aux_ref.row_aux), custom_call_target="tpu_custom_call" | custom-call | tf_op jit(solution)/shard_map/pallas_call | solution.py:403
  16.5 13.4 %all_to_all.20.parts_ref = f32[8,32,128]{2,1,0:T(8,128)S(1)} all-to-all(f32[8,32,128]{2,1,0:T(8,128)S(1)} %broadcast_in_dim.12), channel_id=1, replica_groups=mesh['src'=8,'tgt'=4] {'src'}, dimensions={0} | all-to-all | bytes 262144 | tf_op jit(solution)/shard_map/all_to_all | solution.py:583
  29.9 1.1 %shard_map.78 = f32[4,128]{1,0:T(4,128)S(1)} custom-call(f32[512,4096]{1,0:T(8,128)S(1)} %get-tuple-element.68.score_ref, f32[512,4096]{1,0:T(8,128)S(1)} %get-tuple-element.73.kernel_ref, f32[32,128]{1,0:T(8,128)S(1)} %get-tuple-element.74.top_ref, f32[4,128]{1,0:T(4,128)S(1)} %get-tuple-element.75.base_ref, f32[8,32,128]{2,1,0:T(8,128)S(1)} %all_to_all.20.parts_ref, ...), custom_call_target="tpu_custom_call" | custom-call | tf_op jit(solution)/shard_map/pallas_call | solution.py:403
  31.1 1.1 %collective-permute-done.3 = f32[4,128]{1,0:T(4,128)S(1)} collective-permute-done((f32[4,128]{1,0:T(4,128)S(1)}, f32[4,128]{1,0:T(4,128)S(1)}, u32[]{:S(2)}, u32[]{:S(2)}) %collective-permute-start.3) | collective-permute-done | bytes 2080 | tf_op jit(solution)/shard_map/ppermute | solution.py:391
  32.3 1.6 %collective-permute-start.4 = (f32[4,128]{1,0:T(4,128)S(1)}, f32[4,128]{1,0:T(4,128)S(1)}, u32[]{:S(2)}, u32[]{:S(2)}) collective-permute-start(f32[4,128]{1,0:T(4,128)S(1)} %multiply_add_fusion.5), channel_id=1, source_target_pairs={{0,2},{1,3},{2,0},{3,1},{4,6},{5,7},{6,4},{7,5},{8,10},{9,11},{10,... | collective-permute-start | bytes 6152 | tf_op jit(solution)/shard_map/ppermute | solution.py:391
  34.3 1.7 %collective-permute-done.4 = f32[4,128]{1,0:T(4,128)S(1)} collective-permute-done((f32[4,128]{1,0:T(4,128)S(1)}, f32[4,128]{1,0:T(4,128)S(1)}, u32[]{:S(2)}, u32[]{:S(2)}) %collective-permute-start.4) | collective-permute-done | bytes 2080 | tf_op jit(solution)/shard_map/ppermute | solution.py:391
  35.9 1.6 %shard_map.79 = (f32[32,128]{1,0:T(8,128)S(1)}, f32[4,128]{1,0:T(4,128)}, f32[4,128]{1,0:T(4,128)}) custom-call(f32[512,4096]{1,0:T(8,128)S(1)} %get-tuple-element.68.score_ref, f32[512,4096]{1,0:T(8,128)S(1)} %get-tuple-element.73.kernel_ref, f32[32,128]{1,0:T(8,128)S(1)} %get-tuple-element.74.top_ref, f32[4,128]{1,0:T(4,128)S(1)} %get-tuple-element.75.base_ref, ...), custom_call_target="tpu_custom_call" | custom-call | tf_op jit(solution)/shard_map/pallas_call | solution.py:403
  37.6 3.6 %collective-permute-done.5 = f32[2,104,128]{2,1,0:T(8,128)S(1)} collective-permute-done((f32[2,104,128]{2,1,0:T(8,128)S(1)}, f32[2,104,128]{2,1,0:T(8,128)S(1)}, u32[]{:S(2)}, u32[]{:S(2)}) %collective-permute-start.5) | collective-permute-done | bytes 106528 | tf_op jit(solution)/shard_map/ppermute | solution.py:391
  41.1 10.1 %all_to_all.21.parts_ref = f32[8,32,128]{2,1,0:T(8,128)S(1)} all-to-all(f32[8,32,128]{2,1,0:T(8,128)S(1)} %broadcast_in_dim.13), channel_id=1, replica_groups=mesh['src'=8,'tgt'=4] {'src'}, dimensions={0} | all-to-all | bytes 262144 | tf_op jit(solution)/shard_map/all_to_all | solution.py:583
  51.2 1.1 %shard_map.80 = f32[4,128]{1,0:T(4,128)S(1)} custom-call(f32[512,4096]{1,0:T(8,128)S(1)} %get-tuple-element.68.score_ref, f32[512,4096]{1,0:T(8,128)S(1)} %get-tuple-element.73.kernel_ref, f32[32,128]{1,0:T(8,128)S(1)} %get-tuple-element.74.top_ref, f32[4,128]{1,0:T(4,128)S(1)} %get-tuple-element.75.base_ref, f32[8,32,128]{2,1,0:T(8,128)S(1)} %all_to_all.21.parts_ref, ...), custom_call_target="tpu_custom_call" | custom-call | tf_op jit(solution)/shard_map/pallas_call | solution.py:403
  52.4 1.1 %collective-permute-done.6 = f32[4,128]{1,0:T(4,128)S(1)} collective-permute-done((f32[4,128]{1,0:T(4,128)S(1)}, f32[4,128]{1,0:T(4,128)S(1)}, u32[]{:S(2)}, u32[]{:S(2)}) %collective-permute-start.6) | collective-permute-done | bytes 2080 | tf_op jit(solution)/shard_map/ppermute | solution.py:391
  53.5 0.6 collective-permute-start.7
  54.5 2.7 %collective-permute-done.7 = f32[4,128]{1,0:T(4,128)S(1)} collective-permute-done((f32[4,128]{1,0:T(4,128)S(1)}, f32[4,128]{1,0:T(4,128)S(1)}, u32[]{:S(2)}, u32[]{:S(2)}) %collective-permute-start.7) | collective-permute-done | bytes 2080 | tf_op jit(solution)/shard_map/ppermute | solution.py:391
  57.2 1.6 %shard_map.83 = (f32[32,128]{1,0:T(8,128)S(1)}, f32[4,128]{1,0:T(4,128)}, f32[4,128]{1,0:T(4,128)}) custom-call(f32[512,4096]{1,0:T(8,128)S(1)} %get-tuple-element.68.score_ref, f32[512,4096]{1,0:T(8,128)S(1)} %get-tuple-element.73.kernel_ref, f32[32,128]{1,0:T(8,128)S(1)} %get-tuple-element.74.top_ref, f32[4,128]{1,0:T(4,128)S(1)} %get-tuple-element.75.base_ref, ...), custom_call_target="tpu_custom_call" | custom-call | tf_op jit(solution)/shard_map/pallas_call | solution.py:403
  58.8 1.0 %shard_map.81 = (f32[512,1024]{1,0:T(8,128)S(1)}, bf16[1024,192]{1,0:T(8,128)(2,1)S(1)}, f32[8,128]{1,0:T(8,128)S(1)}) custom-call(f32[64,512]{1,0:T(8,128)S(1)} %get-tuple-element.108.own_ref, f32[4,104,128]{2,1,0:T(8,128)S(1)} %pad_maximum_fusion.mine_ref, f32[4,104,128]{2,1,0:T(8,128)S(1)} %collective-permute-done.8.theirs_ref), custom_call_target="tpu_custom_call" | custom-call | flops 402653184 | tf_op jit(solution)/shard_map/pallas_call | solution.py:403
  59.8 1.0 %shard_map.82 = (f32[512,1024]{1,0:T(8,128)S(1)}, bf16[1024,192]{1,0:T(8,128)(2,1)S(1)}, f32[8,128]{1,0:T(8,128)S(1)}) custom-call(f32[64,512]{1,0:T(8,128)S(1)} %get-tuple-element.108.own_ref, f32[4,104,128]{2,1,0:T(8,128)S(1)} %pad_maximum_fusion.mine_ref, f32[4,104,128]{2,1,0:T(8,128)S(1)} %collective-permute-done.8.theirs_ref), custom_call_target="tpu_custom_call" | custom-call | flops 402653184 | tf_op jit(solution)/shard_map/pallas_call | solution.py:403
  60.8 1.0 %collective-permute-done.9.mine_ref = f32[4,104,128]{2,1,0:T(8,128)S(1)} collective-permute-done((f32[4,104,128]{2,1,0:T(8,128)S(1)}, f32[4,104,128]{2,1,0:T(8,128)S(1)}, u32[]{:S(2)}, u32[]{:S(2)}) %collective-permute-start.9) | collective-permute-done | bytes 213024 | tf_op jit(solution)/shard_map/ppermute | solution.py:391
  61.8 9.7 %all_to_all.22.parts_ref = f32[8,32,128]{2,1,0:T(8,128)S(1)} all-to-all(f32[8,32,128]{2,1,0:T(8,128)S(1)} %broadcast_in_dim.14), channel_id=1, replica_groups=mesh['src'=8,'tgt'=4] {'src'}, dimensions={0} | all-to-all | bytes 262144 | tf_op jit(solution)/shard_map/all_to_all | solution.py:583
  71.5 1.1 %shard_map.84 = f32[4,128]{1,0:T(4,128)S(1)} custom-call(f32[512,4096]{1,0:T(8,128)S(1)} %get-tuple-element.68.score_ref, f32[512,4096]{1,0:T(8,128)S(1)} %get-tuple-element.73.kernel_ref, f32[32,128]{1,0:T(8,128)S(1)} %get-tuple-element.74.top_ref, f32[4,128]{1,0:T(4,128)S(1)} %get-tuple-element.75.base_ref, f32[8,32,128]{2,1,0:T(8,128)S(1)} %all_to_all.22.parts_ref, ...), custom_call_target="tpu_custom_call" | custom-call | tf_op jit(solution)/shard_map/pallas_call | solution.py:403
  72.7 0.5 collective-permute-start.11
  73.2 0.6 collective-permute-done.10
  74.3 1.5 %collective-permute-start.12 = (f32[4,128]{1,0:T(4,128)S(1)}, f32[4,128]{1,0:T(4,128)S(1)}, u32[]{:S(2)}, u32[]{:S(2)}) collective-permute-start(f32[4,128]{1,0:T(4,128)S(1)} %multiply_add_fusion.1), channel_id=1, source_target_pairs={{0,2},{1,3},{2,0},{3,1},{4,6},{5,7},{6,4},{7,5},{8,10},{9,11},{10,... | collective-permute-start | bytes 6152 | tf_op jit(solution)/shard_map/ppermute | solution.py:391
  75.8 1.0 %shard_map.85 = (f32[512,1024]{1,0:T(8,128)S(1)}, bf16[1024,192]{1,0:T(8,128)(2,1)S(1)}, f32[8,128]{1,0:T(8,128)S(1)}) custom-call(f32[64,512]{1,0:T(8,128)S(1)} %get-tuple-element.108.own_ref, f32[4,104,128]{2,1,0:T(8,128)S(1)} %collective-permute-done.9.mine_ref, f32[4,104,128]{2,1,0:T(8,128)S(1)} %collective-permute-done.11.theirs_ref), custom_call_target="tpu_custom_call" | custom-call | flops 402653184 | tf_op jit(solution)/shard_map/pallas_call | solution.py:403
  76.8 1.0 %shard_map.86 = (f32[512,1024]{1,0:T(8,128)S(1)}, bf16[1024,192]{1,0:T(8,128)(2,1)S(1)}, f32[8,128]{1,0:T(8,128)S(1)}) custom-call(f32[64,512]{1,0:T(8,128)S(1)} %get-tuple-element.108.own_ref, f32[4,104,128]{2,1,0:T(8,128)S(1)} %collective-permute-done.9.mine_ref, f32[4,104,128]{2,1,0:T(8,128)S(1)} %collective-permute-done.11.theirs_ref), custom_call_target="tpu_custom_call" | custom-call | flops 402653184 | tf_op jit(solution)/shard_map/pallas_call | solution.py:403
  77.9 1.0 %shard_map.87 = (f32[32,128]{1,0:T(8,128)S(1)}, f32[4,128]{1,0:T(4,128)S(1)}, f32[4,128]{1,0:T(4,128)S(1)}) custom-call(f32[512,4096]{1,0:T(8,128)S(1)} %get-tuple-element.68.score_ref, f32[512,4096]{1,0:T(8,128)S(1)} %get-tuple-element.73.kernel_ref, f32[32,128]{1,0:T(8,128)S(1)} %get-tuple-element.74.top_ref, f32[4,128]{1,0:T(4,128)S(1)} %get-tuple-element.75.base_ref, ...), custom_call_target="tpu_custom_call" | custom-call | tf_op jit(solution)/shard_map/pallas_call | solution.py:403
  79.0 10.4 %all_to_all.23.refs_8_ = f32[8,36,128]{2,1,0:T(8,128)S(1)} all-to-all(f32[8,36,128]{2,1,0:T(8,128)S(1)} %broadcast_in_dim.15), channel_id=1, replica_groups=mesh['src'=8,'tgt'=4] {'src'}, dimensions={0} | all-to-all | bytes 294912 | tf_op jit(solution)/shard_map/all_to_all | solution.py:592
  89.3 3.5 %shard_map.88 = (f32[50,512]{1,0:T(8,128)}, f32[4,128]{1,0:T(4,128)}, f32[32,128]{1,0:T(8,128)}) custom-call(f32[512,1024]{1,0:T(8,128)S(1)} %get-tuple-element.95.refs_0_, f32[512,1024]{1,0:T(8,128)S(1)} %get-tuple-element.96.refs_1_, f32[512,1024]{1,0:T(8,128)S(1)} %get-tuple-element.110.refs_2_, f32[512,1024]{1,0:T(8,128)S(1)} %get-tuple-element.111.refs_3_, ...), custom_call_target="tpu_custom_call" | custom-call | flops 2415919104 | tf_op jit(solution)/shard_map/pallas_call | solution.py:403
  (26 shorter events, 1.6 us)
Async XLA Ops:
  7.2 1.3 %collective-permute-start = (f32[4,128]{1,0:T(4,128)S(1)}, f32[4,128]{1,0:T(4,128)S(1)}, u32[]{:S(2)}, u32[]{:S(2)}) collective-permute-start(f32[4,128]{1,0:T(4,128)S(1)} %get-tuple-element.69), channel_id=1, source_target_pairs={{0,1},{1,0},{2,3},{3,2},{4,5},{5,4},{6,7},{7,6},{8,9},{9,8},{10,11... | collective-permute-start | bytes 6152 | tf_op jit(solution)/shard_map/ppermute | solution.py:391
  8.6 4.5 %collective-permute-start.1 = (f32[4,128]{1,0:T(4,128)S(1)}, f32[4,128]{1,0:T(4,128)S(1)}, u32[]{:S(2)}, u32[]{:S(2)}) collective-permute-start(f32[4,128]{1,0:T(4,128)S(1)} %multiply_add_fusion.7), channel_id=1, source_target_pairs={{0,2},{1,3},{2,0},{3,1},{4,6},{5,7},{6,4},{7,5},{8,10},{9,11},{10,... | collective-permute-start | bytes 6152 | tf_op jit(solution)/shard_map/ppermute | solution.py:391
  11.5 5.0 %collective-permute-start.2 = (f32[1,104,128]{2,1,0:T(8,128)S(1)}, f32[1,104,128]{2,1,0:T(8,128)S(1)}, u32[]{:S(2)}, u32[]{:S(2)}) collective-permute-start(f32[1,104,128]{2,1,0:T(8,128)S(1)} %get-tuple-element.82), channel_id=1, source_target_pairs={{0,8},{4,12},{8,0},{12,4},{16,24},{20,28},{24,16},{28,20},{1,9},{5... | collective-permute-start | bytes 159752 | tf_op jit(solution)/shard_map/ppermute | solution.py:391
  31.0 1.2 %collective-permute-start.3 = (f32[4,128]{1,0:T(4,128)S(1)}, f32[4,128]{1,0:T(4,128)S(1)}, u32[]{:S(2)}, u32[]{:S(2)}) collective-permute-start(f32[4,128]{1,0:T(4,128)S(1)} %shard_map.78), channel_id=1, source_target_pairs={{0,1},{1,0},{2,3},{3,2},{4,5},{5,4},{6,7},{7,6},{8,9},{9,8},{10,11... | collective-permute-start | bytes 6152 | tf_op jit(solution)/shard_map/ppermute | solution.py:391
  32.3 3.6 %collective-permute-start.4 = (f32[4,128]{1,0:T(4,128)S(1)}, f32[4,128]{1,0:T(4,128)S(1)}, u32[]{:S(2)}, u32[]{:S(2)}) collective-permute-start(f32[4,128]{1,0:T(4,128)S(1)} %multiply_add_fusion.5), channel_id=1, source_target_pairs={{0,2},{1,3},{2,0},{3,1},{4,6},{5,7},{6,4},{7,5},{8,10},{9,11},{10,... | collective-permute-start | bytes 6152 | tf_op jit(solution)/shard_map/ppermute | solution.py:391
  33.9 7.2 %collective-permute-start.5 = (f32[2,104,128]{2,1,0:T(8,128)S(1)}, f32[2,104,128]{2,1,0:T(8,128)S(1)}, u32[]{:S(2)}, u32[]{:S(2)}) collective-permute-start(f32[2,104,128]{2,1,0:T(8,128)S(1)} %pad_maximum_fusion.1), channel_id=1, source_target_pairs={{0,16},{4,20},{8,24},{12,28},{16,0},{20,4},{24,8},{28,12},{1,17},{... | collective-permute-start | bytes 319496 | tf_op jit(solution)/shard_map/ppermute | solution.py:391
  52.3 1.2 %collective-permute-start.6 = (f32[4,128]{1,0:T(4,128)S(1)}, f32[4,128]{1,0:T(4,128)S(1)}, u32[]{:S(2)}, u32[]{:S(2)}) collective-permute-start(f32[4,128]{1,0:T(4,128)S(1)} %shard_map.80), channel_id=1, source_target_pairs={{0,1},{1,0},{2,3},{3,2},{4,5},{5,4},{6,7},{7,6},{8,9},{9,8},{10,11... | collective-permute-start | bytes 6152 | tf_op jit(solution)/shard_map/ppermute | solution.py:391
  53.5 3.6 %collective-permute-start.7 = (f32[4,128]{1,0:T(4,128)S(1)}, f32[4,128]{1,0:T(4,128)S(1)}, u32[]{:S(2)}, u32[]{:S(2)}) collective-permute-start(f32[4,128]{1,0:T(4,128)S(1)} %multiply_add_fusion.3), channel_id=1, source_target_pairs={{0,2},{1,3},{2,0},{3,1},{4,6},{5,7},{6,4},{7,5},{8,10},{9,11},{10,... | collective-permute-start | bytes 6152 | tf_op jit(solution)/shard_map/ppermute | solution.py:391
  54.1 3.1 %collective-permute-start.8 = (f32[4,104,128]{2,1,0:T(8,128)S(1)}, f32[4,104,128]{2,1,0:T(8,128)S(1)}, u32[]{:S(2)}, u32[]{:S(2)}) collective-permute-start(f32[4,104,128]{2,1,0:T(8,128)S(1)} %pad_maximum_fusion.mine_ref), channel_id=1, source_target_pairs={{0,1},{1,0},{2,3},{3,2},{4,5},{5,4},{6,7},{7,6},{8,9},{9,8},{10,11... | collective-permute-start | bytes 638984 | tf_op jit(solution)/shard_map/ppermute | solution.py:391
  54.1 7.7 %collective-permute-start.9 = (f32[4,104,128]{2,1,0:T(8,128)S(1)}, f32[4,104,128]{2,1,0:T(8,128)S(1)}, u32[]{:S(2)}, u32[]{:S(2)}) collective-permute-start(f32[4,104,128]{2,1,0:T(8,128)S(1)} %pad_maximum_fusion.mine_ref), channel_id=1, source_target_pairs={{0,4},{4,0},{8,12},{12,8},{16,20},{20,16},{24,28},{28,24},{1,5},{5... | collective-permute-start | bytes 638984 | tf_op jit(solution)/shard_map/ppermute | solution.py:391
  72.6 1.2 %collective-permute-start.10 = (f32[4,128]{1,0:T(4,128)S(1)}, f32[4,128]{1,0:T(4,128)S(1)}, u32[]{:S(2)}, u32[]{:S(2)}) collective-permute-start(f32[4,128]{1,0:T(4,128)S(1)} %shard_map.84), channel_id=1, source_target_pairs={{0,1},{1,0},{2,3},{3,2},{4,5},{5,4},{6,7},{7,6},{8,9},{9,8},{10,11... | collective-permute-start | bytes 6152 | tf_op jit(solution)/shard_map/ppermute | solution.py:391
  72.7 1.6 %collective-permute-start.11 = (f32[4,104,128]{2,1,0:T(8,128)S(1)}, f32[4,104,128]{2,1,0:T(8,128)S(1)}, u32[]{:S(2)}, u32[]{:S(2)}) collective-permute-start(f32[4,104,128]{2,1,0:T(8,128)S(1)} %collective-permute-done.9.mine_ref), channel_id=1, source_target_pairs={{0,1},{1,0},{2,3},{3,2},{4,5},{5,4},{6,7},{7,6},{8,9},{9,8},{10,11... | collective-permute-start | bytes 638984 | tf_op jit(solution)/shard_map/ppermute | solution.py:391
  74.3 3.6 %collective-permute-start.12 = (f32[4,128]{1,0:T(4,128)S(1)}, f32[4,128]{1,0:T(4,128)S(1)}, u32[]{:S(2)}, u32[]{:S(2)}) collective-permute-start(f32[4,128]{1,0:T(4,128)S(1)} %multiply_add_fusion.1), channel_id=1, source_target_pairs={{0,2},{1,3},{2,0},{3,1},{4,6},{5,7},{6,4},{7,5},{8,10},{9,11},{10,... | collective-permute-start | bytes 6152 | tf_op jit(solution)/shard_map/ppermute | solution.py:391

commit v2 on v1

--- a/solution.py
+++ b/solution.py
@@ -416,104 +416,84 @@
 
 
 class Beside:
-    def __init__(self, half, own, steps, rows, n_half):
-        self.parts = half
+    def __init__(self, half, own, bits, rows, n_half):
         self.own = own
-        self.steps = list(steps)
-        self.coming = None
-        self.come = None
+        self.rows = rows
+        self.n_half = n_half
+        self.blocks = {0: half}
+        self.coming = {}
+        if len(bits) >= 3:
+            z, w, x = bits[:3]
+            self.fetches = [[(0, z), (0, w), (0, x)], [(z, x), (w, z)], [(w, x), (w ^ z, x)], []]
+            self.groups = [[], [0, z, w, x], [z ^ x, w ^ z], [w ^ x, w ^ z ^ x]]
+            self.bits = bits[3:]
+        else:
+            self.fetches = [[]] * ITERS
+            self.groups = [[]] * (ITERS - 1) + [[0]]
+            self.bits = bits
         self.mine = []
         self.theirs = []
-        self.ready = []
+        self.offsets = []
         self.todo = []
+        self.tokens = []
+        self.slabs = []
         self.terms = []
-        self.tokens = []
         self.done = []
-        self.offsets = [0]
-        for bit in steps:
-            self.offsets += [offset ^ bit for offset in self.offsets]
-        self.rows = rows
-        self.n_half = n_half
-        self.slabs = []
-
-    def launch(self):
-        self.coming = swap(self.parts, "src", self.steps.pop(0))
-        if not self.steps:
-            self.mine = [self.parts]
-            self.trade()
-
-    def start(self, value, axis, step):
-        if self.coming is not None or not self.steps:
-            return swap(value, axis, step)
-        value, self.parts = tie(value, self.parts)
-        other = swap(value, axis, step)
-        self.launch()
-        return other
+
+    def start(self, step, value, exchange):
+        used = sorted({offset for offset, _ in self.fetches[step]} | set(self.groups[step]))
+        if step and used:
+            value, *held = tie(value, *[self.blocks[offset] for offset in used])
+            self.blocks.update(zip(used, held))
+        others = exchange(value)
+        for offset, bit in self.fetches[step]:
+            self.coming[offset ^ bit] = swap(self.blocks[offset], "src", bit)
+        if self.groups[step]:
+            held = [self.blocks[offset] for offset in self.groups[step]]
+            self.add(held[0] if len(held) == 1 else jnp.concatenate(held, axis=0), self.groups[step])
+        return others
+
+    def add(self, mine, offsets):
+        group = len(self.mine)
+        self.mine.append(mine)
+        self.theirs.append(swap(mine, "tgt", 1))
+        self.offsets.append(offsets)
+        self.todo += [(group, first, min(2, len(offsets))) for first in range(0, len(offsets), 2)]
 
     def land(self, value):
-        if self.coming is not None:
-            value, self.come = tie(value, self.coming)
-            self.coming = None
-        return value
-
-    def join(self, value):
-        if self.come is None:
-            return value
-        value, parts, come = tie(value, self.parts, self.come)
-        self.come = None
-        if self.steps:
-            self.parts = jnp.concatenate([parts, come], axis=0)
-        else:
-            self.mine.append(come)
-            self.trade()
-        return value
-
-    def trade(self):
-        self.theirs.append(swap(self.mine[-1], "tgt", 1))
-
-    def traded(self, value):
-        for group in range(len(self.ready), len(self.theirs)):
-            value, self.theirs[group] = tie(value, self.theirs[group])
-            self.ready.append(group)
-            size = max(self.mine[group].shape[0] // 2, 1)
-            self.todo += [(group, first, size) for first in range(0, self.mine[group].shape[0], size)]
+        if self.coming:
+            value, *held = tie(value, *self.coming.values())
+            self.blocks.update(zip(self.coming, held))
+            self.coming = {}
         return value
 
     def piece(self):
         group, first, size = self.todo.pop(0)
-        mine, theirs = self.mine[group], self.theirs[group]
         share = self.own.shape[1]
         rows = self.rows
         slab, terms, token = call(
             functools.partial(slab_kernel, first=first, n_half=self.n_half),
             [(share, size * rows), ((size * rows, 3 * DEPTH), jnp.bfloat16), (8, LANES)],
             [(DEPTH, rows), ((share, 6 * DEPTH), jnp.bfloat16), (share // LANES, LANES), (share, LANES)],
-            [self.own, mine, theirs],
+            [self.own, self.mine[group], self.theirs[group]],
             12 * DEPTH * share * size * rows,
         )
         self.terms.append(terms)
-        self.done.append(self.offsets[group * mine.shape[0] + first :][:size])
         self.slabs.append(slab)
+        self.done.append(self.offsets[group][first : first + size])
         return token
 
-    def work(self, value, axis, step):
-        if not self.todo:
-            return swap(value, axis, step)
-        value, self.own = tie(value, self.own)
-        return self.pieces(swap(value, axis, step))
-
-    def pieces(self, value):
-        while self.todo:
+    def pieces(self, value, most):
+        for _ in range(min(most, len(self.todo))):
             value, token = tie(value, self.piece())
             self.tokens.append(token)
         return value
 
     def finish(self, value):
-        while self.steps or self.coming is not None or self.come is not None:
-            if self.coming is None and self.come is None:
-                self.launch()
-            value = self.join(self.land(value))
-        return self.pieces(self.traded(value))
+        for bit in self.bits:
+            for mine, offsets in list(zip(self.mine, self.offsets)):
+                self.add(swap(mine, "src", bit), [offset ^ bit for offset in offsets])
+        return self.pieces(value, len(self.todo))
 
 
 def shards(sources, targets, pair_active, count_src, count_tgt):
@@ -555,17 +535,23 @@
     over_src = doubling(n_src)
     over_src = over_src[1:] + over_src[:1]
     side = Beside(half, own, over_src, rows, n_half)
+    near = [bit for bit in (2, 3, 1) if bit < lax.axis_size("tgt")]
+
+    def exchange(value):
+        return [swap(value, "tgt", bit) for bit in near]
+
+    def combine(value, others):
+        values = dict(zip(near, others))
+        value = merge(value, values[1])
+        return merge(value, merge(values[2], values[3])) if 2 in values else value
+
     for step in range(ITERS):
-        lse = side.join(lse)
-        for bit in over_tgt:
-            if bit != over_tgt[-1]:
-                other = swap(lse, "tgt", bit)
-            elif step < ITERS - 1:
-                other = side.start(lse, "tgt", bit)
-            else:
-                other = side.work(side.traded(lse), "tgt", bit)
-            lse = merge(lse, other)
-        lse = side.traded(lse)
+        others = side.start(step, lse, exchange)
+        if step == ITERS - 1:
+            others[0] = side.pieces(others[0], 1)
+        lse = combine(lse, others)
+        for bit in over_tgt[2:]:
+            lse = merge(lse, swap(lse, "tgt", bit))
         if step == 0:
             lse, base, masked, kernel, top = call(
                 first_col_kernel,
@@ -579,7 +565,7 @@
                 [by_row, column], [score, kernel, top, base, lse, row_aux], 0,
             )
         if step < ITERS - 1:
-            lse = side.land(side.pieces(lse))
+            lse = side.land(side.pieces(lse, step))
             lse = lax.all_to_all(jnp.broadcast_to(lse, (n_src, *by_col)), "src", 0, 0, tiled=True)
             (lse,) = call(
                 row_kernel,

time: 93.1 us -> 99.3 us (1.067); the launches traced: 92.8 us -> 101 us
  starting transfers between devices: 10.2 us -> 22.1 us
  local copies, waits for them, and re-layouts: 0.04 us -> 11.4 us
  blocking collectives: 43.6 us -> 33 us
  waiting for transfers between devices: 13.1 us -> 6.15 us
  Pallas kernels: 24.3 us -> 26.9 us
    all_to_all x3 -> x2, blocking collectives: 33.2 us -> 22.4 us  [shards(): lax.all_to_all(jnp.broadcast_to(lse, (n_src, *by_col)), 'src', 0, 0, tile...]
    unnamed x0 -> x39, local copies, waits for them, and re-layouts: none -> 10.6 us
    ppermute x13 -> x22, waiting for transfers between devices: 13.1 us -> 2.83 us  [swap(): lax.ppermute(value, axis, [(i, i ^ step) for i in range(lax.axis_size(axi...]
    ppermute x13 -> x22, starting transfers between devices: 10.2 us -> 18.7 us  [swap(): lax.ppermute(value, axis, [(i, i ^ step) for i in range(lax.axis_size(axi...]
    all_to_all x0 -> x1, starting transfers between devices: none -> 3.37 us  [shards(): lax.all_to_all(jnp.broadcast_to(lse, (n_src, *by_col)), 'src', 0, 0, tile...]
    all_to_all x0 -> x1, waiting for transfers between devices: none -> 3.32 us  [shards(): lax.all_to_all(jnp.broadcast_to(lse, (n_src, *by_col)), 'src', 0, 0, tile...]
    pallas_call x12, Pallas kernels: 18.4 us -> 21 us  [call(): pl.pallas_call(kernel, out_shape=[buffer(pltpu.VMEM if pin else jax.Shape...]
  transfers between devices with their start and end apart: 13 -> 23, of which waited for: 10 -> 6; matrix products, arithmetic and copies ran while one was open for 0% -> 0% of each run, Pallas kernels for 11% -> 10%
where the time goes in v2:
time: 99.3 us; the launch traced here: 101 us
  blocking collectives  33 us (33%)
  Pallas kernels  26.9 us (27%)
  starting transfers between devices  22.1 us (22%)
  local copies, waits for them, and re-layouts  11.4 us (11%)
  waiting for transfers between devices  6.15 us (6%)
  between operations  1.61 us (2%)
    all_to_all x2, blocking collectives, shards(): lax.all_to_all(jnp.broadcast_to(lse, (n_src, *by_col)), 'src', 0, 0, tile...  22.4 us
    pallas_call x12, Pallas kernels, call(): pl.pallas_call(kernel, out_shape=[buffer(pltpu.VMEM if pin else jax.Shape...  21 us
    ppermute x22, starting transfers between devices, swap(): lax.ppermute(value, axis, [(i, i ^ step) for i in range(lax.axis_size(axi...  18.7 us
    all_to_all x1, blocking collectives, shards(): lax.all_to_all(jnp.broadcast_to(both, (n_src, *both.shape)), 'src', 0, 0,...  10.7 us
    unnamed x39, local copies, waits for them, and re-layouts  10.6 us
    pallas_call x1, Pallas kernels, shards(): pl.pallas_call(first_kernel, out_shape=[pltpu.VMEM(shape, jnp.float32) fo...  5.95 us
    all_to_all x1, starting transfers between devices, shards(): lax.all_to_all(jnp.broadcast_to(lse, (n_src, *by_col)), 'src', 0, 0, tile...  3.37 us
    all_to_all x1, waiting for transfers between devices, shards(): lax.all_to_all(jnp.broadcast_to(lse, (n_src, *by_col)), 'src', 0, 0, tile...  3.32 us
  transfers between devices with their start and end apart: 23, of which 6 were waited for; matrix products, arithmetic and copies ran while one was open for 0% of the time, Pallas kernels for 10%

profile of v2, /device:TPU:0, one launch (start us, length us, event | category | flops | bytes accessed | tf_op | source)
XLA Modules:
  0.0 101.3 jit_solution(14444189582401903509)
XLA Ops:
  1.3 5.9 %shard_map.76 = (f32[512,4096]{1,0:T(8,128)S(1)}, f32[4,128]{1,0:T(4,128)S(1)}, f32[3,4,128]{2,1,0:T(4,128)S(1)}, f32[3,32,128]{2,1,0:T(8,128)S(1)}, f32[64,512]{1,0:T(8,128)S(1)}, /*index=5*/f32[1,104,128]{2,1,0:T(8,128)S(1)}) custom-call(f32[50,512]{1,0:T(8,128)} %src_hbm.1, f32[50,4096]{1,0:T(8,128)} %tgt_hbm.1, s32[8]{0:T(128)} %count_src_hbm.1, ...), custom_call_target="tpu_custom_call" | custom-call | flops 1610612736 | tf_op jit(solution)/shard_map/pallas_call | solution.py:512
  7.8 2.6 %collective-permute-start.1 = (f32[4,128]{1,0:T(4,128)S(1)}, f32[4,128]{1,0:T(4,128)S(1)}, u32[]{:S(2)}, u32[]{:S(2)}) collective-permute-start(f32[4,128]{1,0:T(4,128)S(1)} %get-tuple-element.65), channel_id=1, source_target_pairs={{0,2},{1,3},{2,0},{3,1},{4,6},{5,7},{6,4},{7,5},{8,10},{9,11},{10,... | collective-permute-start | bytes 6152 | tf_op jit(solution)/shard_map/ppermute | solution.py:391
  10.4 1.8 %collective-permute-start.3 = (f32[1,104,128]{2,1,0:T(8,128)S(1)}, f32[1,104,128]{2,1,0:T(8,128)S(1)}, u32[]{:S(2)}, u32[]{:S(2)}) collective-permute-start(f32[1,104,128]{2,1,0:T(8,128)S(1)} %get-tuple-element.77), channel_id=1, source_target_pairs={{0,8},{4,12},{8,0},{12,4},{16,24},{20,28},{24,16},{28,20},{1,9},{5... | collective-permute-start | bytes 159752 | tf_op jit(solution)/shard_map/ppermute | solution.py:391
  12.2 2.6 %collective-permute-start.4 = (f32[1,104,128]{2,1,0:T(8,128)S(1)}, f32[1,104,128]{2,1,0:T(8,128)S(1)}, u32[]{:S(2)}, u32[]{:S(2)}) collective-permute-start(f32[1,104,128]{2,1,0:T(8,128)S(1)} %get-tuple-element.77), channel_id=1, source_target_pairs={{0,16},{4,20},{8,24},{12,28},{16,0},{20,4},{24,8},{28,12},{1,17},{... | collective-permute-start | bytes 159752 | tf_op jit(solution)/shard_map/ppermute | solution.py:391
  14.8 1.5 %collective-permute-start.5 = (f32[1,104,128]{2,1,0:T(8,128)S(1)}, f32[1,104,128]{2,1,0:T(8,128)S(1)}, u32[]{:S(2)}, u32[]{:S(2)}) collective-permute-start(f32[1,104,128]{2,1,0:T(8,128)S(1)} %get-tuple-element.77), channel_id=1, source_target_pairs={{0,4},{4,0},{8,12},{12,8},{16,20},{20,16},{24,28},{28,24},{1,5},{5... | collective-permute-start | bytes 159752 | tf_op jit(solution)/shard_map/ppermute | solution.py:391
  16.3 3.4 %shard_map.77 = (f32[32,128]{1,0:T(8,128)S(1)}, f32[4,128]{1,0:T(4,128)S(1)}, f32[4,128]{1,0:T(4,128)}, f32[512,4096]{1,0:T(8,128)S(1)}, f32[32,128]{1,0:T(8,128)S(1)}) custom-call(f32[512,4096]{1,0:T(8,128)S(1)} %get-tuple-element.64.score_ref, f32[4,128]{1,0:T(4,128)S(1)} %multiply_add_fusion.3.lse_ref, f32[3,4,128]{2,1,0:T(4,128)S(1)} %get-tuple-element.66.aux_ref.row_aux), custom_call_target="tpu_custom_call" | custom-call | tf_op jit(solution)/shard_map/pallas_call | solution.py:403
  19.8 10.4 %all_to_all.20.parts_ref = f32[8,32,128]{2,1,0:T(8,128)S(1)} all-to-all(f32[8,32,128]{2,1,0:T(8,128)S(1)} %broadcast_in_dim.12), channel_id=1, replica_groups=mesh['src'=8,'tgt'=4] {'src'}, dimensions={0} | all-to-all | bytes 262144 | tf_op jit(solution)/shard_map/all_to_all | solution.py:569
  30.2 1.1 %shard_map.78 = f32[4,128]{1,0:T(4,128)S(1)} custom-call(f32[512,4096]{1,0:T(8,128)S(1)} %get-tuple-element.64.score_ref, f32[512,4096]{1,0:T(8,128)S(1)} %get-tuple-element.67.kernel_ref, f32[32,128]{1,0:T(8,128)S(1)} %get-tuple-element.68.top_ref, f32[4,128]{1,0:T(4,128)S(1)} %get-tuple-element.69.base_ref, f32[8,32,128]{2,1,0:T(8,128)S(1)} %all_to_all.20.parts_ref, ...), custom_call_target="tpu_custom_call" | custom-call | tf_op jit(solution)/shard_map/pallas_call | solution.py:403
  31.4 1.6 %collective-permute-start.8 = (f32[4,128]{1,0:T(4,128)S(1)}, f32[4,128]{1,0:T(4,128)S(1)}, u32[]{:S(2)}, u32[]{:S(2)}) collective-permute-start(f32[4,128]{1,0:T(4,128)S(1)} %shard_map.78), channel_id=1, source_target_pairs={{0,2},{1,3},{2,0},{3,1},{4,6},{5,7},{6,4},{7,5},{8,10},{9,11},{10,... | collective-permute-start | bytes 6152 | tf_op jit(solution)/shard_map/ppermute | solution.py:391
  33.5 1.1 %collective-permute-start.11 = (f32[1,104,128]{2,1,0:T(8,128)S(1)}, f32[1,104,128]{2,1,0:T(8,128)S(1)}, u32[]{:S(2)}, u32[]{:S(2)}) collective-permute-start(f32[1,104,128]{2,1,0:T(8,128)S(1)} %collective-permute-done.4), channel_id=1, source_target_pairs={{0,8},{4,12},{8,0},{12,4},{16,24},{20,28},{24,16},{28,20},{1,9},{5... | collective-permute-start | bytes 159752 | tf_op jit(solution)/shard_map/ppermute | solution.py:391
  35.0 0.9 collective-permute-done.9
  36.0 1.6 %shard_map.81 = (f32[32,128]{1,0:T(8,128)S(1)}, f32[4,128]{1,0:T(4,128)}, f32[4,128]{1,0:T(4,128)}) custom-call(f32[512,4096]{1,0:T(8,128)S(1)} %get-tuple-element.64.score_ref, f32[512,4096]{1,0:T(8,128)S(1)} %get-tuple-element.67.kernel_ref, f32[32,128]{1,0:T(8,128)S(1)} %get-tuple-element.68.top_ref, f32[4,128]{1,0:T(4,128)S(1)} %get-tuple-element.69.base_ref, ...), custom_call_target="tpu_custom_call" | custom-call | tf_op jit(solution)/shard_map/pallas_call | solution.py:403
  37.7 1.0 shard_map.79
  40.0 3.4 %all-to-all-start.1 = ((f32[8,32,128]{2,1,0:T(8,128)}), f32[8,32,128]{2,1,0:T(8,128)S(1)}, u32[]{:S(2)}, u32[]{:S(2)}) async-start(f32[8,32,128]{2,1,0:T(8,128)} %broadcast_in_dim.13), calls=%async_computation.1 | async-start | bytes 262144 | tf_op jit(solution)/shard_map/all_to_all | solution.py:569
  45.2 1.0 shard_map.80
  46.3 1.3 %copy-done.5 = f32[512,1024]{1,0:T(8,128)} copy-done((f32[512,1024]{1,0:T(8,128)}, f32[512,1024]{1,0:T(8,128)S(1)}, u32[]{:S(2)}) %copy-start.5) | copy-done | bytes 2097176
  47.6 3.3 %all-to-all-done.1.parts_ref = f32[8,32,128]{2,1,0:T(8,128)S(1)} async-done(((f32[8,32,128]{2,1,0:T(8,128)}), f32[8,32,128]{2,1,0:T(8,128)S(1)}, u32[]{:S(2)}, u32[]{:S(2)}) %all-to-all-start.1) | async-done | bytes 131104 | tf_op jit(solution)/shard_map/all_to_all | solution.py:569
  50.9 3.4 %copy-done.1 = f32[512,4096]{1,0:T(8,128)S(1)} copy-done((f32[512,4096]{1,0:T(8,128)S(1)}, f32[512,4096]{1,0:T(8,128)}, u32[]{:S(2)}) %copy-start.1) | copy-done | bytes 8388632
  54.3 3.4 %copy-done.3 = f32[512,4096]{1,0:T(8,128)S(1)} copy-done((f32[512,4096]{1,0:T(8,128)S(1)}, f32[512,4096]{1,0:T(8,128)}, u32[]{:S(2)}) %copy-start.3) | copy-done | bytes 8388632
  57.7 1.2 %shard_map.82 = f32[4,128]{1,0:T(4,128)S(1)} custom-call(f32[512,4096]{1,0:T(8,128)S(1)} %copy-done.1, f32[512,4096]{1,0:T(8,128)S(1)} %copy-done.3, f32[32,128]{1,0:T(8,128)S(1)} %get-tuple-element.68.top_ref, f32[4,128]{1,0:T(4,128)S(1)} %get-tuple-element.69.base_ref, f32[8,32,128]{2,1,0:T(8,128)S(1)} %all-to-all-done.1.parts_ref, ...), custom_call_target="tpu_custom_call" | custom-call | tf_op jit(solution)/shard_map/pallas_call | solution.py:403
  59.6 1.2 %collective-permute-start.15 = (f32[4,128]{1,0:T(4,128)S(1)}, f32[4,128]{1,0:T(4,128)S(1)}, u32[]{:S(2)}, u32[]{:S(2)}) collective-permute-start(f32[4,128]{1,0:T(4,128)S(1)} %shard_map.82), channel_id=1, source_target_pairs={{0,3},{1,2},{2,1},{3,0},{4,7},{5,6},{6,5},{7,4},{8,11},{9,10},{10,... | collective-permute-start | bytes 6152 | tf_op jit(solution)/shard_map/ppermute | solution.py:391
  61.4 1.7 %collective-permute-start.16 = (f32[1,104,128]{2,1,0:T(8,128)S(1)}, f32[1,104,128]{2,1,0:T(8,128)S(1)}, u32[]{:S(2)}, u32[]{:S(2)}) collective-permute-start(f32[1,104,128]{2,1,0:T(8,128)S(1)} %collective-permute-done.4), channel_id=1, source_target_pairs={{0,4},{4,0},{8,12},{12,8},{16,20},{20,16},{24,28},{28,24},{1,5},{5... | collective-permute-start | bytes 159752 | tf_op jit(solution)/shard_map/ppermute | solution.py:391
  63.1 1.6 %shard_map.84 = (f32[32,128]{1,0:T(8,128)S(1)}, f32[4,128]{1,0:T(4,128)}, f32[4,128]{1,0:T(4,128)}) custom-call(f32[512,4096]{1,0:T(8,128)S(1)} %copy-done.1, f32[512,4096]{1,0:T(8,128)S(1)} %copy-done.4, f32[32,128]{1,0:T(8,128)S(1)} %get-tuple-element.68.top_ref, f32[4,128]{1,0:T(4,128)S(1)} %get-tuple-element.69.base_ref, ...), custom_call_target="tpu_custom_call" | custom-call | tf_op jit(solution)/shard_map/pallas_call | solution.py:403
  64.7 1.0 shard_map.83
  66.2 11.9 %all_to_all.21.parts_ref = f32[8,32,128]{2,1,0:T(8,128)S(1)} all-to-all(f32[8,32,128]{2,1,0:T(8,128)S(1)} %broadcast_in_dim.14), channel_id=1, replica_groups=mesh['src'=8,'tgt'=4] {'src'}, dimensions={0} | all-to-all | bytes 262144 | tf_op jit(solution)/shard_map/all_to_all | solution.py:569
  78.1 1.1 %shard_map.85 = f32[4,128]{1,0:T(4,128)S(1)} custom-call(f32[512,4096]{1,0:T(8,128)S(1)} %bitcast.3, f32[512,4096]{1,0:T(8,128)S(1)} %copy-done.4, f32[32,128]{1,0:T(8,128)S(1)} %get-tuple-element.68.top_ref, f32[4,128]{1,0:T(4,128)S(1)} %get-tuple-element.69.base_ref, f32[8,32,128]{2,1,0:T(8,128)S(1)} %all_to_all.21.parts_ref, ...), custom_call_target="tpu_custom_call" | custom-call | tf_op jit(solution)/shard_map/pallas_call | solution.py:403
  79.3 1.1 %collective-permute-start.20 = (f32[4,128]{1,0:T(4,128)S(1)}, f32[4,128]{1,0:T(4,128)S(1)}, u32[]{:S(2)}, u32[]{:S(2)}) collective-permute-start(f32[4,128]{1,0:T(4,128)S(1)} %shard_map.85), channel_id=1, source_target_pairs={{0,2},{1,3},{2,0},{3,1},{4,6},{5,7},{6,4},{7,5},{8,10},{9,11},{10,... | collective-permute-start | bytes 6152 | tf_op jit(solution)/shard_map/ppermute | solution.py:391
  80.6 0.9 collective-permute-start.21
  81.5 1.0 shard_map.86
  83.6 3.6 %shard_map.87 = (f32[32,128]{1,0:T(8,128)S(1)}, f32[4,128]{1,0:T(4,128)S(1)}, f32[4,128]{1,0:T(4,128)S(1)}) custom-call(f32[512,4096]{1,0:T(8,128)S(1)} %bitcast.3, f32[512,4096]{1,0:T(8,128)S(1)} %copy-done.4, f32[32,128]{1,0:T(8,128)S(1)} %get-tuple-element.68.top_ref, f32[4,128]{1,0:T(4,128)S(1)} %get-tuple-element.69.base_ref, ...), custom_call_target="tpu_custom_call" | custom-call | tf_op jit(solution)/shard_map/pallas_call | solution.py:403
  87.2 10.7 %all_to_all.22.refs_8_ = f32[8,36,128]{2,1,0:T(8,128)S(1)} all-to-all(f32[8,36,128]{2,1,0:T(8,128)S(1)} %broadcast_in_dim.15), channel_id=1, replica_groups=mesh['src'=8,'tgt'=4] {'src'}, dimensions={0} | all-to-all | bytes 294912 | tf_op jit(solution)/shard_map/all_to_all | solution.py:578
  97.9 3.4 %shard_map.88 = (f32[50,512]{1,0:T(8,128)}, f32[4,128]{1,0:T(4,128)}, f32[32,128]{1,0:T(8,128)}) custom-call(f32[512,1024]{1,0:T(8,128)S(1)} %get-tuple-element.81.refs_0_, f32[512,1024]{1,0:T(8,128)S(1)} %copy-done.6, f32[512,1024]{1,0:T(8,128)S(1)} %get-tuple-element.92.refs_2_, f32[512,1024]{1,0:T(8,128)S(1)} %get-tuple-element.105.refs_3_, ...), custom_call_target="tpu_custom_call" | custom-call | flops 2415919104 | tf_op jit(solution)/shard_map/pallas_call | solution.py:403
  (82 shorter events, 7.9 us)
Async XLA Ops:
  7.2 28.8 %copy-start = (f32[512,4096]{1,0:T(8,128)}, f32[512,4096]{1,0:T(8,128)S(1)}, u32[]{:S(2)}) copy-start(f32[512,4096]{1,0:T(8,128)S(1)} %get-tuple-element.64.score_ref) | copy-start | bytes 25165828
  7.2 7.6 %collective-permute-start = (f32[4,128]{1,0:T(4,128)S(1)}, f32[4,128]{1,0:T(4,128)S(1)}, u32[]{:S(2)}, u32[]{:S(2)}) collective-permute-start(f32[4,128]{1,0:T(4,128)S(1)} %get-tuple-element.65), channel_id=1, source_target_pairs={{0,1},{1,0},{2,3},{3,2},{4,5},{5,4},{6,7},{7,6},{8,9},{9,8},{10,11... | collective-permute-start | bytes 6152 | tf_op jit(solution)/shard_map/ppermute | solution.py:391
  7.8 8.5 %collective-permute-start.1 = (f32[4,128]{1,0:T(4,128)S(1)}, f32[4,128]{1,0:T(4,128)S(1)}, u32[]{:S(2)}, u32[]{:S(2)}) collective-permute-start(f32[4,128]{1,0:T(4,128)S(1)} %get-tuple-element.65), channel_id=1, source_target_pairs={{0,2},{1,3},{2,0},{3,1},{4,6},{5,7},{6,4},{7,5},{8,10},{9,11},{10,... | collective-permute-start | bytes 6152 | tf_op jit(solution)/shard_map/ppermute | solution.py:391
  10.4 5.9 %collective-permute-start.2 = (f32[4,128]{1,0:T(4,128)S(1)}, f32[4,128]{1,0:T(4,128)S(1)}, u32[]{:S(2)}, u32[]{:S(2)}) collective-permute-start(f32[4,128]{1,0:T(4,128)S(1)} %get-tuple-element.65), channel_id=1, source_target_pairs={{0,3},{1,2},{2,1},{3,0},{4,7},{5,6},{6,5},{7,4},{8,11},{9,10},{10,... | collective-permute-start | bytes 6152 | tf_op jit(solution)/shard_map/ppermute | solution.py:391
  10.4 9.3 %collective-permute-start.3 = (f32[1,104,128]{2,1,0:T(8,128)S(1)}, f32[1,104,128]{2,1,0:T(8,128)S(1)}, u32[]{:S(2)}, u32[]{:S(2)}) collective-permute-start(f32[1,104,128]{2,1,0:T(8,128)S(1)} %get-tuple-element.77), channel_id=1, source_target_pairs={{0,8},{4,12},{8,0},{12,4},{16,24},{20,28},{24,16},{28,20},{1,9},{5... | collective-permute-start | bytes 159752 | tf_op jit(solution)/shard_map/ppermute | solution.py:391
  12.2 7.5 %collective-permute-start.4 = (f32[1,104,128]{2,1,0:T(8,128)S(1)}, f32[1,104,128]{2,1,0:T(8,128)S(1)}, u32[]{:S(2)}, u32[]{:S(2)}) collective-permute-start(f32[1,104,128]{2,1,0:T(8,128)S(1)} %get-tuple-element.77), channel_id=1, source_target_pairs={{0,16},{4,20},{8,24},{12,28},{16,0},{20,4},{24,8},{28,12},{1,17},{... | collective-permute-start | bytes 159752 | tf_op jit(solution)/shard_map/ppermute | solution.py:391
  14.8 5.0 %collective-permute-start.5 = (f32[1,104,128]{2,1,0:T(8,128)S(1)}, f32[1,104,128]{2,1,0:T(8,128)S(1)}, u32[]{:S(2)}, u32[]{:S(2)}) collective-permute-start(f32[1,104,128]{2,1,0:T(8,128)S(1)} %get-tuple-element.77), channel_id=1, source_target_pairs={{0,4},{4,0},{8,12},{12,8},{16,20},{20,16},{24,28},{28,24},{1,5},{5... | collective-permute-start | bytes 159752 | tf_op jit(solution)/shard_map/ppermute | solution.py:391
  19.7 16.3 %copy-start.2 = (f32[512,4096]{1,0:T(8,128)}, f32[512,4096]{1,0:T(8,128)S(1)}, u32[]{:S(2)}) copy-start(f32[512,4096]{1,0:T(8,128)S(1)} %get-tuple-element.67.kernel_ref) | copy-start | bytes 25165828
  31.3 3.3 %collective-permute-start.7 = (f32[4,128]{1,0:T(4,128)S(1)}, f32[4,128]{1,0:T(4,128)S(1)}, u32[]{:S(2)}, u32[]{:S(2)}) collective-permute-start(f32[4,128]{1,0:T(4,128)S(1)} %shard_map.78), channel_id=1, source_target_pairs={{0,1},{1,0},{2,3},{3,2},{4,5},{5,4},{6,7},{7,6},{8,9},{9,8},{10,11... | collective-permute-start | bytes 6152 | tf_op jit(solution)/shard_map/ppermute | solution.py:391
  31.4 3.7 %collective-permute-start.8 = (f32[4,128]{1,0:T(4,128)S(1)}, f32[4,128]{1,0:T(4,128)S(1)}, u32[]{:S(2)}, u32[]{:S(2)}) collective-permute-start(f32[4,128]{1,0:T(4,128)S(1)} %shard_map.78), channel_id=1, source_target_pairs={{0,2},{1,3},{2,0},{3,1},{4,6},{5,7},{6,4},{7,5},{8,10},{9,11},{10,... | collective-permute-start | bytes 6152 | tf_op jit(solution)/shard_map/ppermute | solution.py:391
  33.0 3.0 %collective-permute-start.9 = (f32[4,128]{1,0:T(4,128)S(1)}, f32[4,128]{1,0:T(4,128)S(1)}, u32[]{:S(2)}, u32[]{:S(2)}) collective-permute-start(f32[4,128]{1,0:T(4,128)S(1)} %shard_map.78), channel_id=1, source_target_pairs={{0,3},{1,2},{2,1},{3,0},{4,7},{5,6},{6,5},{7,4},{8,11},{9,10},{10,... | collective-permute-start | bytes 6152 | tf_op jit(solution)/shard_map/ppermute | solution.py:391
  33.3 5.4 %collective-permute-start.10 = (f32[1,104,128]{2,1,0:T(8,128)S(1)}, f32[1,104,128]{2,1,0:T(8,128)S(1)}, u32[]{:S(2)}, u32[]{:S(2)}) collective-permute-start(f32[1,104,128]{2,1,0:T(8,128)S(1)} %collective-permute-done.3), channel_id=1, source_target_pairs={{0,4},{4,0},{8,12},{12,8},{16,20},{20,16},{24,28},{28,24},{1,5},{5... | collective-permute-start | bytes 159752 | tf_op jit(solution)/shard_map/ppermute | solution.py:391
  33.5 5.2 %collective-permute-start.11 = (f32[1,104,128]{2,1,0:T(8,128)S(1)}, f32[1,104,128]{2,1,0:T(8,128)S(1)}, u32[]{:S(2)}, u32[]{:S(2)}) collective-permute-start(f32[1,104,128]{2,1,0:T(8,128)S(1)} %collective-permute-done.4), channel_id=1, source_target_pairs={{0,8},{4,12},{8,0},{12,4},{16,24},{20,28},{24,16},{28,20},{1,9},{5... | collective-permute-start | bytes 159752 | tf_op jit(solution)/shard_map/ppermute | solution.py:391
  34.6 3.0 %collective-permute-start.6 = (f32[4,104,128]{2,1,0:T(8,128)S(1)}, f32[4,104,128]{2,1,0:T(8,128)S(1)}, u32[]{:S(2)}, u32[]{:S(2)}) collective-permute-start(f32[4,104,128]{2,1,0:T(8,128)S(1)} %constant_dynamic-update-slice_fusion.mine_ref), channel_id=1, source_target_pairs={{0,1},{1,0},{2,3},{3,2},{4,5},{5,4},{6,7},{7,6},{8,9},{9,8},{10,11... | collective-permute-start | bytes 638984 | tf_op jit(solution)/shard_map/ppermute | solution.py:391
  40.0 10.9 %all-to-all-start.1 = ((f32[8,32,128]{2,1,0:T(8,128)}), f32[8,32,128]{2,1,0:T(8,128)S(1)}, u32[]{:S(2)}, u32[]{:S(2)}) async-start(f32[8,32,128]{2,1,0:T(8,128)} %broadcast_in_dim.13), calls=%async_computation.1 | async-start | bytes 262144 | tf_op jit(solution)/shard_map/all_to_all | solution.py:569
  50.9 3.4 %copy-start.1 = (f32[512,4096]{1,0:T(8,128)S(1)}, f32[512,4096]{1,0:T(8,128)}, u32[]{:S(2)}) copy-start(f32[512,4096]{1,0:T(8,128)} %copy-done) | copy-start | bytes 25165828
  54.3 3.4 %copy-start.3 = (f32[512,4096]{1,0:T(8,128)S(1)}, f32[512,4096]{1,0:T(8,128)}, u32[]{:S(2)}) copy-start(f32[512,4096]{1,0:T(8,128)} %copy-done.2) | copy-start | bytes 25165828
  57.7 3.2 %copy-start.12 = (f32[1,104,128]{2,1,0:T(8,128)S(1)}, f32[1,104,128]{2,1,0:T(8,128)}, u32[]{:S(2)}) copy-start(f32[1,104,128]{2,1,0:T(8,128)} %copy-done.11) | copy-start | bytes 159748
  57.7 5.4 %copy-start.4 = (f32[512,4096]{1,0:T(8,128)S(1)}, f32[512,4096]{1,0:T(8,128)}, u32[]{:S(2)}) copy-start(f32[512,4096]{1,0:T(8,128)} %copy-done.2) | copy-start | bytes 25165828
  58.9 2.5 %collective-permute-start.13 = (f32[4,128]{1,0:T(4,128)S(1)}, f32[4,128]{1,0:T(4,128)S(1)}, u32[]{:S(2)}, u32[]{:S(2)}) collective-permute-start(f32[4,128]{1,0:T(4,128)S(1)} %shard_map.82), channel_id=1, source_target_pairs={{0,1},{1,0},{2,3},{3,2},{4,5},{5,4},{6,7},{7,6},{8,9},{9,8},{10,11... | collective-permute-start | bytes 6152 | tf_op jit(solution)/shard_map/ppermute | solution.py:391
  59.0 4.1 %collective-permute-start.14 = (f32[4,128]{1,0:T(4,128)S(1)}, f32[4,128]{1,0:T(4,128)S(1)}, u32[]{:S(2)}, u32[]{:S(2)}) collective-permute-start(f32[4,128]{1,0:T(4,128)S(1)} %shard_map.82), channel_id=1, source_target_pairs={{0,2},{1,3},{2,0},{3,1},{4,6},{5,7},{6,4},{7,5},{8,10},{9,11},{10,... | collective-permute-start | bytes 6152 | tf_op jit(solution)/shard_map/ppermute | solution.py:391
  59.6 3.4 %collective-permute-start.15 = (f32[4,128]{1,0:T(4,128)S(1)}, f32[4,128]{1,0:T(4,128)S(1)}, u32[]{:S(2)}, u32[]{:S(2)}) collective-permute-start(f32[4,128]{1,0:T(4,128)S(1)} %shard_map.82), channel_id=1, source_target_pairs={{0,3},{1,2},{2,1},{3,0},{4,7},{5,6},{6,5},{7,4},{8,11},{9,10},{10,... | collective-permute-start | bytes 6152 | tf_op jit(solution)/shard_map/ppermute | solution.py:391
  60.9 5.3 %collective-permute-start.17 = (f32[1,104,128]{2,1,0:T(8,128)S(1)}, f32[1,104,128]{2,1,0:T(8,128)S(1)}, u32[]{:S(2)}, u32[]{:S(2)}) collective-permute-start(f32[1,104,128]{2,1,0:T(8,128)S(1)} %copy-done.12), channel_id=1, source_target_pairs={{0,4},{4,0},{8,12},{12,8},{16,20},{20,16},{24,28},{28,24},{1,5},{5... | collective-permute-start | bytes 159752 | tf_op jit(solution)/shard_map/ppermute | solution.py:391
  61.2 3.5 %collective-permute-start.12 = (f32[2,104,128]{2,1,0:T(8,128)S(1)}, f32[2,104,128]{2,1,0:T(8,128)S(1)}, u32[]{:S(2)}, u32[]{:S(2)}) collective-permute-start(f32[2,104,128]{2,1,0:T(8,128)S(1)} %constant_dynamic-update-slice_fusion.4.mine_ref), channel_id=1, source_target_pairs={{0,1},{1,0},{2,3},{3,2},{4,5},{5,4},{6,7},{7,6},{8,9},{9,8},{10,11... | collective-permute-start | bytes 319496 | tf_op jit(solution)/shard_map/ppermute | solution.py:391
  61.4 4.8 %collective-permute-start.16 = (f32[1,104,128]{2,1,0:T(8,128)S(1)}, f32[1,104,128]{2,1,0:T(8,128)S(1)}, u32[]{:S(2)}, u32[]{:S(2)}) collective-permute-start(f32[1,104,128]{2,1,0:T(8,128)S(1)} %collective-permute-done.4), channel_id=1, source_target_pairs={{0,4},{4,0},{8,12},{12,8},{16,20},{20,16},{24,28},{28,24},{1,5},{5... | collective-permute-start | bytes 159752 | tf_op jit(solution)/shard_map/ppermute | solution.py:391
  63.0 15.1 %slice-start = ((s8[8388608]{0:T(1024)(128)(4,1)}), s8[4194304]{0:T(1024)(128)(4,1)S(1)}, s32[]{:S(2)}) async-start(s8[8388608]{0:T(1024)(128)(4,1)} %bitcast.2), calls=%async_computation.4 | async-start | bytes 8388608
  63.1 15.0 %slice-start.1 = ((s8[8388608]{0:T(1024)(128)(4,1)}), s8[4194304]{0:T(1024)(128)(4,1)S(1)}, s32[]{:S(2)}) async-start(s8[8388608]{0:T(1024)(128)(4,1)} %bitcast.2), calls=%async_computation.5 | async-start | bytes 8388608
  79.2 2.3 %collective-permute-start.18 = (f32[2,104,128]{2,1,0:T(8,128)S(1)}, f32[2,104,128]{2,1,0:T(8,128)S(1)}, u32[]{:S(2)}, u32[]{:S(2)}) collective-permute-start(f32[2,104,128]{2,1,0:T(8,128)S(1)} %constant_dynamic-update-slice_fusion.6.mine_ref), channel_id=1, source_target_pairs={{0,1},{1,0},{2,3},{3,2},{4,5},{5,4},{6,7},{7,6},{8,9},{9,8},{10,11... | collective-permute-start | bytes 319496 | tf_op jit(solution)/shard_map/ppermute | solution.py:391
  79.3 3.7 %collective-permute-start.20 = (f32[4,128]{1,0:T(4,128)S(1)}, f32[4,128]{1,0:T(4,128)S(1)}, u32[]{:S(2)}, u32[]{:S(2)}) collective-permute-start(f32[4,128]{1,0:T(4,128)S(1)} %shard_map.85), channel_id=1, source_target_pairs={{0,2},{1,3},{2,0},{3,1},{4,6},{5,7},{6,4},{7,5},{8,10},{9,11},{10,... | collective-permute-start | bytes 6152 | tf_op jit(solution)/shard_map/ppermute | solution.py:391
  80.4 2.6 %collective-permute-start.19 = (f32[4,128]{1,0:T(4,128)S(1)}, f32[4,128]{1,0:T(4,128)S(1)}, u32[]{:S(2)}, u32[]{:S(2)}) collective-permute-start(f32[4,128]{1,0:T(4,128)S(1)} %shard_map.85), channel_id=1, source_target_pairs={{0,1},{1,0},{2,3},{3,2},{4,5},{5,4},{6,7},{7,6},{8,9},{9,8},{10,11... | collective-permute-start | bytes 6152 | tf_op jit(solution)/shard_map/ppermute | solution.py:391
  80.6 3.0 %collective-permute-start.21 = (f32[4,128]{1,0:T(4,128)S(1)}, f32[4,128]{1,0:T(4,128)S(1)}, u32[]{:S(2)}, u32[]{:S(2)}) collective-permute-start(f32[4,128]{1,0:T(4,128)S(1)} %shard_map.85), channel_id=1, source_target_pairs={{0,3},{1,2},{2,1},{3,0},{4,7},{5,6},{6,5},{7,4},{8,11},{9,10},{10,... | collective-permute-start | bytes 6152 | tf_op jit(solution)/shard_map/ppermute | solution.py:391
  83.6 14.3 %copy-start.6 = (f32[512,1024]{1,0:T(8,128)S(1)}, f32[512,1024]{1,0:T(8,128)}, u32[]{:S(2)}) copy-start(f32[512,1024]{1,0:T(8,128)} %copy-done.5) | copy-start | bytes 6291460
  (8 other events, 13.1 us)

commit v3 on v2

--- a/solution.py
+++ b/solution.py
@@ -483,6 +483,10 @@
         self.done.append(self.offsets[group][first : first + size])
         return token
 
+    def hold(self, value):
+        value, self.own = tie(value, self.own)
+        return value
+
     def pieces(self, value, most):
         for _ in range(min(most, len(self.todo))):
             value, token = tie(value, self.piece())
@@ -493,7 +497,7 @@
         for bit in self.bits:
             for mine, offsets in list(zip(self.mine, self.offsets)):
                 self.add(swap(mine, "src", bit), [offset ^ bit for offset in offsets])
-        return self.pieces(value, len(self.todo))
+        return self.pieces(self.hold(value), len(self.todo))
 
 
 def shards(sources, targets, pair_active, count_src, count_tgt):
@@ -546,6 +550,8 @@
         return merge(value, merge(values[2], values[3])) if 2 in values else value
 
     for step in range(ITERS):
+        if step == ITERS - 1:
+            lse = side.hold(lse)
         others = side.start(step, lse, exchange)
         if step == ITERS - 1:
             others[0] = side.pieces(others[0], 1)
@@ -565,7 +571,7 @@
                 [by_row, column], [score, kernel, top, base, lse, row_aux], 0,
             )
         if step < ITERS - 1:
-            lse = side.land(side.pieces(lse, step))
+            lse = side.land(side.pieces(side.hold(lse), step))
             lse = lax.all_to_all(jnp.broadcast_to(lse, (n_src, *by_col)), "src", 0, 0, tiled=True)
             (lse,) = call(
                 row_kernel,

time: 99.3 us -> 88.6 us (0.89); the launches traced: 101 us -> 88.3 us
  local copies, waits for them, and re-layouts: 11.4 us -> 0.08 us
  blocking collectives: 33 us -> 41.1 us
  waiting for transfers between devices: 6.15 us -> 2.52 us
  starting transfers between devices: 22.1 us -> 18.7 us
  Pallas kernels: 26.9 us -> 24.4 us
    unnamed x39 -> x5, local copies, waits for them, and re-layouts: 10.6 us -> 0.02 us
    all_to_all x2 -> x3, blocking collectives: 22.4 us -> 30.4 us  [shards(): lax.all_to_all(jnp.broadcast_to(lse, (n_src, *by_col)), 'src', 0, 0, tile...]
    all_to_all x1 -> x0, starting transfers between devices: 3.37 us -> none  [shards(): lax.all_to_all(jnp.broadcast_to(lse, (n_src, *by_col)), 'src', 0, 0, tile...]
    all_to_all x1 -> x0, waiting for transfers between devices: 3.32 us -> none  [shards(): lax.all_to_all(jnp.broadcast_to(lse, (n_src, *by_col)), 'src', 0, 0, tile...]
    pallas_call x12, Pallas kernels: 21 us -> 18.4 us  [call(): pl.pallas_call(kernel, out_shape=[buffer(pltpu.VMEM if pin else jax.Shape...]
  transfers between devices with their start and end apart: 23 -> 22, of which waited for: 6 -> 5; matrix products, arithmetic and copies ran while one was open for 0% -> 0% of each run, Pallas kernels for 10% -> 12%
where the time goes in v3:
time: 88.6 us; the launch traced here: 88.3 us
  blocking collectives  41.1 us (46%)
  Pallas kernels  24.4 us (28%)
  starting transfers between devices  18.7 us (21%)
  waiting for transfers between devices  2.52 us (3%)
  between operations  1.53 us (2%)
    all_to_all x3, blocking collectives, shards(): lax.all_to_all(jnp.broadcast_to(lse, (n_src, *by_col)), 'src', 0, 0, tile...  30.4 us
    ppermute x22, starting transfers between devices, swap(): lax.ppermute(value, axis, [(i, i ^ step) for i in range(lax.axis_size(axi...  18.7 us
    pallas_call x12, Pallas kernels, call(): pl.pallas_call(kernel, out_shape=[buffer(pltpu.VMEM if pin else jax.Shape...  18.4 us
    all_to_all x1, blocking collectives, shards(): lax.all_to_all(jnp.broadcast_to(both, (n_src, *both.shape)), 'src', 0, 0,...  10.7 us
    pallas_call x1, Pallas kernels, shards(): pl.pallas_call(first_kernel, out_shape=[pltpu.VMEM(shape, jnp.float32) fo...  5.95 us
    ppermute x22, waiting for transfers between devices, swap(): lax.ppermute(value, axis, [(i, i ^ step) for i in range(lax.axis_size(axi...  2.52 us
  transfers between devices with their start and end apart: 22, of which 5 were waited for; matrix products, arithmetic and copies ran while one was open for 0% of the time, Pallas kernels for 12%

profile of v3, /device:TPU:0, one launch (start us, length us, event | category | flops | bytes accessed | tf_op | source)
XLA Modules:
  0.0 88.3 jit_solution(15621694406056788178)
XLA Ops:
  1.3 5.9 %shard_map.76 = (f32[512,4096]{1,0:T(8,128)S(1)}, f32[4,128]{1,0:T(4,128)S(1)}, f32[3,4,128]{2,1,0:T(4,128)S(1)}, f32[3,32,128]{2,1,0:T(8,128)S(1)}, f32[64,512]{1,0:T(8,128)S(1)}, /*index=5*/f32[1,104,128]{2,1,0:T(8,128)S(1)}) custom-call(f32[50,512]{1,0:T(8,128)} %src_hbm.1, f32[50,4096]{1,0:T(8,128)} %tgt_hbm.1, s32[8]{0:T(128)} %count_src_hbm.1, ...), custom_call_target="tpu_custom_call" | custom-call | flops 1610612736 | tf_op jit(solution)/shard_map/pallas_call | solution.py:516
  7.2 0.5 collective-permute-start
  7.7 2.6 %collective-permute-start.1 = (f32[4,128]{1,0:T(4,128)S(1)}, f32[4,128]{1,0:T(4,128)S(1)}, u32[]{:S(2)}, u32[]{:S(2)}) collective-permute-start(f32[4,128]{1,0:T(4,128)S(1)} %get-tuple-element.73), channel_id=1, source_target_pairs={{0,2},{1,3},{2,0},{3,1},{4,6},{5,7},{6,4},{7,5},{8,10},{9,11},{10,... | collective-permute-start | bytes 6152 | tf_op jit(solution)/shard_map/ppermute | solution.py:391
  10.4 1.8 %collective-permute-start.3 = (f32[1,104,128]{2,1,0:T(8,128)S(1)}, f32[1,104,128]{2,1,0:T(8,128)S(1)}, u32[]{:S(2)}, u32[]{:S(2)}) collective-permute-start(f32[1,104,128]{2,1,0:T(8,128)S(1)} %get-tuple-element.91), channel_id=1, source_target_pairs={{0,8},{4,12},{8,0},{12,4},{16,24},{20,28},{24,16},{28,20},{1,9},{5... | collective-permute-start | bytes 159752 | tf_op jit(solution)/shard_map/ppermute | solution.py:391
  12.2 2.6 %collective-permute-start.4 = (f32[1,104,128]{2,1,0:T(8,128)S(1)}, f32[1,104,128]{2,1,0:T(8,128)S(1)}, u32[]{:S(2)}, u32[]{:S(2)}) collective-permute-start(f32[1,104,128]{2,1,0:T(8,128)S(1)} %get-tuple-element.91), channel_id=1, source_target_pairs={{0,16},{4,20},{8,24},{12,28},{16,0},{20,4},{24,8},{28,12},{1,17},{... | collective-permute-start | bytes 159752 | tf_op jit(solution)/shard_map/ppermute | solution.py:391
  14.8 1.5 %collective-permute-start.5 = (f32[1,104,128]{2,1,0:T(8,128)S(1)}, f32[1,104,128]{2,1,0:T(8,128)S(1)}, u32[]{:S(2)}, u32[]{:S(2)}) collective-permute-start(f32[1,104,128]{2,1,0:T(8,128)S(1)} %get-tuple-element.91), channel_id=1, source_target_pairs={{0,4},{4,0},{8,12},{12,8},{16,20},{20,16},{24,28},{28,24},{1,5},{5... | collective-permute-start | bytes 159752 | tf_op jit(solution)/shard_map/ppermute | solution.py:391
  16.3 3.4 %shard_map.77 = (f32[32,128]{1,0:T(8,128)S(1)}, f32[4,128]{1,0:T(4,128)S(1)}, f32[4,128]{1,0:T(4,128)}, f32[512,4096]{1,0:T(8,128)S(1)}, f32[32,128]{1,0:T(8,128)S(1)}) custom-call(f32[512,4096]{1,0:T(8,128)S(1)} %get-tuple-element.72.score_ref, f32[4,128]{1,0:T(4,128)S(1)} %multiply_add_fusion.3.lse_ref, f32[3,4,128]{2,1,0:T(4,128)S(1)} %get-tuple-element.74.aux_ref.row_aux), custom_call_target="tpu_custom_call" | custom-call | tf_op jit(solution)/shard_map/pallas_call | solution.py:403
  19.8 10.4 %all_to_all.20.parts_ref = f32[8,32,128]{2,1,0:T(8,128)S(1)} all-to-all(f32[8,32,128]{2,1,0:T(8,128)S(1)} %broadcast_in_dim.12), channel_id=1, replica_groups=mesh['src'=8,'tgt'=4] {'src'}, dimensions={0} | all-to-all | bytes 262144 | tf_op jit(solution)/shard_map/all_to_all | solution.py:575
  30.2 1.1 %shard_map.78 = f32[4,128]{1,0:T(4,128)S(1)} custom-call(f32[512,4096]{1,0:T(8,128)S(1)} %get-tuple-element.72.score_ref, f32[512,4096]{1,0:T(8,128)S(1)} %get-tuple-element.75.kernel_ref, f32[32,128]{1,0:T(8,128)S(1)} %get-tuple-element.76.top_ref, f32[4,128]{1,0:T(4,128)S(1)} %get-tuple-element.77.base_ref, f32[8,32,128]{2,1,0:T(8,128)S(1)} %all_to_all.20.parts_ref, ...), custom_call_target="tpu_custom_call" | custom-call | tf_op jit(solution)/shard_map/pallas_call | solution.py:403
  31.4 1.6 %collective-permute-start.7 = (f32[4,128]{1,0:T(4,128)S(1)}, f32[4,128]{1,0:T(4,128)S(1)}, u32[]{:S(2)}, u32[]{:S(2)}) collective-permute-start(f32[4,128]{1,0:T(4,128)S(1)} %shard_map.78), channel_id=1, source_target_pairs={{0,2},{1,3},{2,0},{3,1},{4,6},{5,7},{6,4},{7,5},{8,10},{9,11},{10,... | collective-permute-start | bytes 6152 | tf_op jit(solution)/shard_map/ppermute | solution.py:391
  33.5 1.1 %collective-permute-start.11 = (f32[1,104,128]{2,1,0:T(8,128)S(1)}, f32[1,104,128]{2,1,0:T(8,128)S(1)}, u32[]{:S(2)}, u32[]{:S(2)}) collective-permute-start(f32[1,104,128]{2,1,0:T(8,128)S(1)} %collective-permute-done.4), channel_id=1, source_target_pairs={{0,8},{4,12},{8,0},{12,4},{16,24},{20,28},{24,16},{28,20},{1,9},{5... | collective-permute-start | bytes 159752 | tf_op jit(solution)/shard_map/ppermute | solution.py:391
  35.0 0.9 %collective-permute-done.8 = f32[4,128]{1,0:T(4,128)S(1)} collective-permute-done((f32[4,128]{1,0:T(4,128)S(1)}, f32[4,128]{1,0:T(4,128)S(1)}, u32[]{:S(2)}, u32[]{:S(2)}) %collective-permute-start.8) | collective-permute-done | bytes 2080 | tf_op jit(solution)/shard_map/ppermute | solution.py:391
  36.0 1.6 %shard_map.79 = (f32[32,128]{1,0:T(8,128)S(1)}, f32[4,128]{1,0:T(4,128)}, f32[4,128]{1,0:T(4,128)}) custom-call(f32[512,4096]{1,0:T(8,128)S(1)} %get-tuple-element.72.score_ref, f32[512,4096]{1,0:T(8,128)S(1)} %get-tuple-element.75.kernel_ref, f32[32,128]{1,0:T(8,128)S(1)} %get-tuple-element.76.top_ref, f32[4,128]{1,0:T(4,128)S(1)} %get-tuple-element.77.base_ref, ...), custom_call_target="tpu_custom_call" | custom-call | tf_op jit(solution)/shard_map/pallas_call | solution.py:403
  37.6 1.0 %shard_map.80 = (f32[512,1024]{1,0:T(8,128)S(1)}, bf16[1024,192]{1,0:T(8,128)(2,1)S(1)}, f32[8,128]{1,0:T(8,128)S(1)}) custom-call(f32[64,512]{1,0:T(8,128)S(1)} %get-tuple-element.116.own_ref, f32[4,104,128]{2,1,0:T(8,128)S(1)} %constant_dynamic-update-slice_fusion.mine_ref, f32[4,104,128]{2,1,0:T(8,128)S(1)} %collective-permute-done.9.theirs_ref), custom_call_target="tpu_custom_call" | custom-call | flops 402653184 | tf_op jit(solution)/shard_map/pallas_call | solution.py:403
  38.7 10.0 %all_to_all.21.parts_ref = f32[8,32,128]{2,1,0:T(8,128)S(1)} all-to-all(f32[8,32,128]{2,1,0:T(8,128)S(1)} %broadcast_in_dim.13), channel_id=1, replica_groups=mesh['src'=8,'tgt'=4] {'src'}, dimensions={0} | all-to-all | bytes 262144 | tf_op jit(solution)/shard_map/all_to_all | solution.py:575
  48.7 1.1 %shard_map.81 = f32[4,128]{1,0:T(4,128)S(1)} custom-call(f32[512,4096]{1,0:T(8,128)S(1)} %get-tuple-element.72.score_ref, f32[512,4096]{1,0:T(8,128)S(1)} %get-tuple-element.75.kernel_ref, f32[32,128]{1,0:T(8,128)S(1)} %get-tuple-element.76.top_ref, f32[4,128]{1,0:T(4,128)S(1)} %get-tuple-element.77.base_ref, f32[8,32,128]{2,1,0:T(8,128)S(1)} %all_to_all.21.parts_ref, ...), custom_call_target="tpu_custom_call" | custom-call | tf_op jit(solution)/shard_map/pallas_call | solution.py:403
  49.8 1.2 %collective-permute-start.13 = (f32[4,128]{1,0:T(4,128)S(1)}, f32[4,128]{1,0:T(4,128)S(1)}, u32[]{:S(2)}, u32[]{:S(2)}) collective-permute-start(f32[4,128]{1,0:T(4,128)S(1)} %shard_map.81), channel_id=1, source_target_pairs={{0,2},{1,3},{2,0},{3,1},{4,6},{5,7},{6,4},{7,5},{8,10},{9,11},{10,... | collective-permute-start | bytes 6152 | tf_op jit(solution)/shard_map/ppermute | solution.py:391
  51.0 0.7 collective-permute-start.14
  52.1 1.7 %collective-permute-start.16 = (f32[1,104,128]{2,1,0:T(8,128)S(1)}, f32[1,104,128]{2,1,0:T(8,128)S(1)}, u32[]{:S(2)}, u32[]{:S(2)}) collective-permute-start(f32[1,104,128]{2,1,0:T(8,128)S(1)} %collective-permute-done.4), channel_id=1, source_target_pairs={{0,4},{4,0},{8,12},{12,8},{16,20},{20,16},{24,28},{28,24},{1,5},{5... | collective-permute-start | bytes 159752 | tf_op jit(solution)/shard_map/ppermute | solution.py:391
  54.1 1.6 %shard_map.82 = (f32[32,128]{1,0:T(8,128)S(1)}, f32[4,128]{1,0:T(4,128)}, f32[4,128]{1,0:T(4,128)}) custom-call(f32[512,4096]{1,0:T(8,128)S(1)} %get-tuple-element.72.score_ref, f32[512,4096]{1,0:T(8,128)S(1)} %get-tuple-element.75.kernel_ref, f32[32,128]{1,0:T(8,128)S(1)} %get-tuple-element.76.top_ref, f32[4,128]{1,0:T(4,128)S(1)} %get-tuple-element.77.base_ref, ...), custom_call_target="tpu_custom_call" | custom-call | tf_op jit(solution)/shard_map/pallas_call | solution.py:403
  55.7 1.0 %shard_map.83 = (f32[512,1024]{1,0:T(8,128)S(1)}, bf16[1024,192]{1,0:T(8,128)(2,1)S(1)}, f32[8,128]{1,0:T(8,128)S(1)}) custom-call(f32[64,512]{1,0:T(8,128)S(1)} %get-tuple-element.116.own_ref, f32[4,104,128]{2,1,0:T(8,128)S(1)} %constant_dynamic-update-slice_fusion.mine_ref, f32[4,104,128]{2,1,0:T(8,128)S(1)} %collective-permute-done.9.theirs_ref), custom_call_target="tpu_custom_call" | custom-call | flops 402653184 | tf_op jit(solution)/shard_map/pallas_call | solution.py:403
  56.7 1.0 %shard_map.84 = (f32[512,1024]{1,0:T(8,128)S(1)}, bf16[1024,192]{1,0:T(8,128)(2,1)S(1)}, f32[8,128]{1,0:T(8,128)S(1)}) custom-call(f32[64,512]{1,0:T(8,128)S(1)} %get-tuple-element.116.own_ref, f32[2,104,128]{2,1,0:T(8,128)S(1)} %constant_dynamic-update-slice_fusion.4.mine_ref, f32[2,104,128]{2,1,0:T(8,128)S(1)} %collective-permute-done.15.theirs_ref), custom_call_target="tpu_custom_call" | custom-call | flops 402653184 | tf_op jit(solution)/shard_map/pallas_call | solution.py:403
  57.8 10.0 %all_to_all.22.parts_ref = f32[8,32,128]{2,1,0:T(8,128)S(1)} all-to-all(f32[8,32,128]{2,1,0:T(8,128)S(1)} %broadcast_in_dim.14), channel_id=1, replica_groups=mesh['src'=8,'tgt'=4] {'src'}, dimensions={0} | all-to-all | bytes 262144 | tf_op jit(solution)/shard_map/all_to_all | solution.py:575
  67.7 1.1 %shard_map.85 = f32[4,128]{1,0:T(4,128)S(1)} custom-call(f32[512,4096]{1,0:T(8,128)S(1)} %get-tuple-element.72.score_ref, f32[512,4096]{1,0:T(8,128)S(1)} %get-tuple-element.75.kernel_ref, f32[32,128]{1,0:T(8,128)S(1)} %get-tuple-element.76.top_ref, f32[4,128]{1,0:T(4,128)S(1)} %get-tuple-element.77.base_ref, f32[8,32,128]{2,1,0:T(8,128)S(1)} %all_to_all.22.parts_ref, ...), custom_call_target="tpu_custom_call" | custom-call | tf_op jit(solution)/shard_map/pallas_call | solution.py:403
  68.9 1.0 %collective-permute-start.20 = (f32[4,128]{1,0:T(4,128)S(1)}, f32[4,128]{1,0:T(4,128)S(1)}, u32[]{:S(2)}, u32[]{:S(2)}) collective-permute-start(f32[4,128]{1,0:T(4,128)S(1)} %shard_map.85), channel_id=1, source_target_pairs={{0,2},{1,3},{2,0},{3,1},{4,6},{5,7},{6,4},{7,5},{8,10},{9,11},{10,... | collective-permute-start | bytes 6152 | tf_op jit(solution)/shard_map/ppermute | solution.py:391
  70.1 1.1 %collective-permute-start.21 = (f32[4,128]{1,0:T(4,128)S(1)}, f32[4,128]{1,0:T(4,128)S(1)}, u32[]{:S(2)}, u32[]{:S(2)}) collective-permute-start(f32[4,128]{1,0:T(4,128)S(1)} %shard_map.85), channel_id=1, source_target_pairs={{0,3},{1,2},{2,1},{3,0},{4,7},{5,6},{6,5},{7,4},{8,11},{9,10},{10,... | collective-permute-start | bytes 6152 | tf_op jit(solution)/shard_map/ppermute | solution.py:391
  71.2 1.0 %shard_map.86 = (f32[512,1024]{1,0:T(8,128)S(1)}, bf16[1024,192]{1,0:T(8,128)(2,1)S(1)}, f32[8,128]{1,0:T(8,128)S(1)}) custom-call(f32[64,512]{1,0:T(8,128)S(1)} %get-tuple-element.116.own_ref, f32[2,104,128]{2,1,0:T(8,128)S(1)} %constant_dynamic-update-slice_fusion.6.mine_ref, f32[2,104,128]{2,1,0:T(8,128)S(1)} %collective-permute-done.18.theirs_ref), custom_call_target="tpu_custom_call" | custom-call | flops 402653184 | tf_op jit(solution)/shard_map/pallas_call | solution.py:403
  72.2 0.4 collective-permute-done.20
  72.6 0.5 collective-permute-done.21
  73.1 1.0 %shard_map.87 = (f32[32,128]{1,0:T(8,128)S(1)}, f32[4,128]{1,0:T(4,128)S(1)}, f32[4,128]{1,0:T(4,128)S(1)}) custom-call(f32[512,4096]{1,0:T(8,128)S(1)} %get-tuple-element.72.score_ref, f32[512,4096]{1,0:T(8,128)S(1)} %get-tuple-element.75.kernel_ref, f32[32,128]{1,0:T(8,128)S(1)} %get-tuple-element.76.top_ref, f32[4,128]{1,0:T(4,128)S(1)} %get-tuple-element.77.base_ref, ...), custom_call_target="tpu_custom_call" | custom-call | tf_op jit(solution)/shard_map/pallas_call | solution.py:403
  74.2 10.7 %all_to_all.23.refs_8_ = f32[8,36,128]{2,1,0:T(8,128)S(1)} all-to-all(f32[8,36,128]{2,1,0:T(8,128)S(1)} %broadcast_in_dim.15), channel_id=1, replica_groups=mesh['src'=8,'tgt'=4] {'src'}, dimensions={0} | all-to-all | bytes 294912 | tf_op jit(solution)/shard_map/all_to_all | solution.py:584
  84.8 3.5 %shard_map.88 = (f32[50,512]{1,0:T(8,128)}, f32[4,128]{1,0:T(4,128)}, f32[32,128]{1,0:T(8,128)}) custom-call(f32[512,1024]{1,0:T(8,128)S(1)} %get-tuple-element.95.refs_0_, f32[512,1024]{1,0:T(8,128)S(1)} %get-tuple-element.105.refs_1_, f32[512,1024]{1,0:T(8,128)S(1)} %get-tuple-element.108.refs_2_, f32[512,1024]{1,0:T(8,128)S(1)} %get-tuple-element.122.refs_3_, ...), custom_call_target="tpu_custom_call" | custom-call | flops 2415919104 | tf_op jit(solution)/shard_map/pallas_call | solution.py:403
  (46 shorter events, 2.3 us)
Async XLA Ops:
  7.2 7.6 %collective-permute-start = (f32[4,128]{1,0:T(4,128)S(1)}, f32[4,128]{1,0:T(4,128)S(1)}, u32[]{:S(2)}, u32[]{:S(2)}) collective-permute-start(f32[4,128]{1,0:T(4,128)S(1)} %get-tuple-element.73), channel_id=1, source_target_pairs={{0,1},{1,0},{2,3},{3,2},{4,5},{5,4},{6,7},{7,6},{8,9},{9,8},{10,11... | collective-permute-start | bytes 6152 | tf_op jit(solution)/shard_map/ppermute | solution.py:391
  7.7 8.5 %collective-permute-start.1 = (f32[4,128]{1,0:T(4,128)S(1)}, f32[4,128]{1,0:T(4,128)S(1)}, u32[]{:S(2)}, u32[]{:S(2)}) collective-permute-start(f32[4,128]{1,0:T(4,128)S(1)} %get-tuple-element.73), channel_id=1, source_target_pairs={{0,2},{1,3},{2,0},{3,1},{4,6},{5,7},{6,4},{7,5},{8,10},{9,11},{10,... | collective-permute-start | bytes 6152 | tf_op jit(solution)/shard_map/ppermute | solution.py:391
  10.3 5.9 %collective-permute-start.2 = (f32[4,128]{1,0:T(4,128)S(1)}, f32[4,128]{1,0:T(4,128)S(1)}, u32[]{:S(2)}, u32[]{:S(2)}) collective-permute-start(f32[4,128]{1,0:T(4,128)S(1)} %get-tuple-element.73), channel_id=1, source_target_pairs={{0,3},{1,2},{2,1},{3,0},{4,7},{5,6},{6,5},{7,4},{8,11},{9,10},{10,... | collective-permute-start | bytes 6152 | tf_op jit(solution)/shard_map/ppermute | solution.py:391
  10.4 9.3 %collective-permute-start.3 = (f32[1,104,128]{2,1,0:T(8,128)S(1)}, f32[1,104,128]{2,1,0:T(8,128)S(1)}, u32[]{:S(2)}, u32[]{:S(2)}) collective-permute-start(f32[1,104,128]{2,1,0:T(8,128)S(1)} %get-tuple-element.91), channel_id=1, source_target_pairs={{0,8},{4,12},{8,0},{12,4},{16,24},{20,28},{24,16},{28,20},{1,9},{5... | collective-permute-start | bytes 159752 | tf_op jit(solution)/shard_map/ppermute | solution.py:391
  12.2 7.5 %collective-permute-start.4 = (f32[1,104,128]{2,1,0:T(8,128)S(1)}, f32[1,104,128]{2,1,0:T(8,128)S(1)}, u32[]{:S(2)}, u32[]{:S(2)}) collective-permute-start(f32[1,104,128]{2,1,0:T(8,128)S(1)} %get-tuple-element.91), channel_id=1, source_target_pairs={{0,16},{4,20},{8,24},{12,28},{16,0},{20,4},{24,8},{28,12},{1,17},{... | collective-permute-start | bytes 159752 | tf_op jit(solution)/shard_map/ppermute | solution.py:391
  14.8 5.0 %collective-permute-start.5 = (f32[1,104,128]{2,1,0:T(8,128)S(1)}, f32[1,104,128]{2,1,0:T(8,128)S(1)}, u32[]{:S(2)}, u32[]{:S(2)}) collective-permute-start(f32[1,104,128]{2,1,0:T(8,128)S(1)} %get-tuple-element.91), channel_id=1, source_target_pairs={{0,4},{4,0},{8,12},{12,8},{16,20},{20,16},{24,28},{28,24},{1,5},{5... | collective-permute-start | bytes 159752 | tf_op jit(solution)/shard_map/ppermute | solution.py:391
  31.3 3.3 %collective-permute-start.6 = (f32[4,128]{1,0:T(4,128)S(1)}, f32[4,128]{1,0:T(4,128)S(1)}, u32[]{:S(2)}, u32[]{:S(2)}) collective-permute-start(f32[4,128]{1,0:T(4,128)S(1)} %shard_map.78), channel_id=1, source_target_pairs={{0,1},{1,0},{2,3},{3,2},{4,5},{5,4},{6,7},{7,6},{8,9},{9,8},{10,11... | collective-permute-start | bytes 6152 | tf_op jit(solution)/shard_map/ppermute | solution.py:391
  31.4 3.7 %collective-permute-start.7 = (f32[4,128]{1,0:T(4,128)S(1)}, f32[4,128]{1,0:T(4,128)S(1)}, u32[]{:S(2)}, u32[]{:S(2)}) collective-permute-start(f32[4,128]{1,0:T(4,128)S(1)} %shard_map.78), channel_id=1, source_target_pairs={{0,2},{1,3},{2,0},{3,1},{4,6},{5,7},{6,4},{7,5},{8,10},{9,11},{10,... | collective-permute-start | bytes 6152 | tf_op jit(solution)/shard_map/ppermute | solution.py:391
  33.0 3.0 %collective-permute-start.8 = (f32[4,128]{1,0:T(4,128)S(1)}, f32[4,128]{1,0:T(4,128)S(1)}, u32[]{:S(2)}, u32[]{:S(2)}) collective-permute-start(f32[4,128]{1,0:T(4,128)S(1)} %shard_map.78), channel_id=1, source_target_pairs={{0,3},{1,2},{2,1},{3,0},{4,7},{5,6},{6,5},{7,4},{8,11},{9,10},{10,... | collective-permute-start | bytes 6152 | tf_op jit(solution)/shard_map/ppermute | solution.py:391
  33.3 5.4 %collective-permute-start.10 = (f32[1,104,128]{2,1,0:T(8,128)S(1)}, f32[1,104,128]{2,1,0:T(8,128)S(1)}, u32[]{:S(2)}, u32[]{:S(2)}) collective-permute-start(f32[1,104,128]{2,1,0:T(8,128)S(1)} %collective-permute-done.3), channel_id=1, source_target_pairs={{0,4},{4,0},{8,12},{12,8},{16,20},{20,16},{24,28},{28,24},{1,5},{5... | collective-permute-start | bytes 159752 | tf_op jit(solution)/shard_map/ppermute | solution.py:391
  33.5 5.2 %collective-permute-start.11 = (f32[1,104,128]{2,1,0:T(8,128)S(1)}, f32[1,104,128]{2,1,0:T(8,128)S(1)}, u32[]{:S(2)}, u32[]{:S(2)}) collective-permute-start(f32[1,104,128]{2,1,0:T(8,128)S(1)} %collective-permute-done.4), channel_id=1, source_target_pairs={{0,8},{4,12},{8,0},{12,4},{16,24},{20,28},{24,16},{28,20},{1,9},{5... | collective-permute-start | bytes 159752 | tf_op jit(solution)/shard_map/ppermute | solution.py:391
  34.6 3.0 %collective-permute-start.9 = (f32[4,104,128]{2,1,0:T(8,128)S(1)}, f32[4,104,128]{2,1,0:T(8,128)S(1)}, u32[]{:S(2)}, u32[]{:S(2)}) collective-permute-start(f32[4,104,128]{2,1,0:T(8,128)S(1)} %constant_dynamic-update-slice_fusion.mine_ref), channel_id=1, source_target_pairs={{0,1},{1,0},{2,3},{3,2},{4,5},{5,4},{6,7},{7,6},{8,9},{9,8},{10,11... | collective-permute-start | bytes 638984 | tf_op jit(solution)/shard_map/ppermute | solution.py:391
  49.8 2.4 %collective-permute-start.12 = (f32[4,128]{1,0:T(4,128)S(1)}, f32[4,128]{1,0:T(4,128)S(1)}, u32[]{:S(2)}, u32[]{:S(2)}) collective-permute-start(f32[4,128]{1,0:T(4,128)S(1)} %shard_map.81), channel_id=1, source_target_pairs={{0,1},{1,0},{2,3},{3,2},{4,5},{5,4},{6,7},{7,6},{8,9},{9,8},{10,11... | collective-permute-start | bytes 6152 | tf_op jit(solution)/shard_map/ppermute | solution.py:391
  49.8 4.0 %collective-permute-start.13 = (f32[4,128]{1,0:T(4,128)S(1)}, f32[4,128]{1,0:T(4,128)S(1)}, u32[]{:S(2)}, u32[]{:S(2)}) collective-permute-start(f32[4,128]{1,0:T(4,128)S(1)} %shard_map.81), channel_id=1, source_target_pairs={{0,2},{1,3},{2,0},{3,1},{4,6},{5,7},{6,4},{7,5},{8,10},{9,11},{10,... | collective-permute-start | bytes 6152 | tf_op jit(solution)/shard_map/ppermute | solution.py:391
  51.0 3.0 %collective-permute-start.14 = (f32[4,128]{1,0:T(4,128)S(1)}, f32[4,128]{1,0:T(4,128)S(1)}, u32[]{:S(2)}, u32[]{:S(2)}) collective-permute-start(f32[4,128]{1,0:T(4,128)S(1)} %shard_map.81), channel_id=1, source_target_pairs={{0,3},{1,2},{2,1},{3,0},{4,7},{5,6},{6,5},{7,4},{8,11},{9,10},{10,... | collective-permute-start | bytes 6152 | tf_op jit(solution)/shard_map/ppermute | solution.py:391
  51.7 6.0 %collective-permute-start.17 = (f32[1,104,128]{2,1,0:T(8,128)S(1)}, f32[1,104,128]{2,1,0:T(8,128)S(1)}, u32[]{:S(2)}, u32[]{:S(2)}) collective-permute-start(f32[1,104,128]{2,1,0:T(8,128)S(1)} %collective-permute-done.11), channel_id=1, source_target_pairs={{0,4},{4,0},{8,12},{12,8},{16,20},{20,16},{24,28},{28,24},{1,5},{5... | collective-permute-start | bytes 159752 | tf_op jit(solution)/shard_map/ppermute | solution.py:391
  52.0 4.7 %collective-permute-start.15 = (f32[2,104,128]{2,1,0:T(8,128)S(1)}, f32[2,104,128]{2,1,0:T(8,128)S(1)}, u32[]{:S(2)}, u32[]{:S(2)}) collective-permute-start(f32[2,104,128]{2,1,0:T(8,128)S(1)} %constant_dynamic-update-slice_fusion.4.mine_ref), channel_id=1, source_target_pairs={{0,1},{1,0},{2,3},{3,2},{4,5},{5,4},{6,7},{7,6},{8,9},{9,8},{10,11... | collective-permute-start | bytes 319496 | tf_op jit(solution)/shard_map/ppermute | solution.py:391
  52.1 5.6 %collective-permute-start.16 = (f32[1,104,128]{2,1,0:T(8,128)S(1)}, f32[1,104,128]{2,1,0:T(8,128)S(1)}, u32[]{:S(2)}, u32[]{:S(2)}) collective-permute-start(f32[1,104,128]{2,1,0:T(8,128)S(1)} %collective-permute-done.4), channel_id=1, source_target_pairs={{0,4},{4,0},{8,12},{12,8},{16,20},{20,16},{24,28},{28,24},{1,5},{5... | collective-permute-start | bytes 159752 | tf_op jit(solution)/shard_map/ppermute | solution.py:391
  68.9 2.3 %collective-permute-start.18 = (f32[2,104,128]{2,1,0:T(8,128)S(1)}, f32[2,104,128]{2,1,0:T(8,128)S(1)}, u32[]{:S(2)}, u32[]{:S(2)}) collective-permute-start(f32[2,104,128]{2,1,0:T(8,128)S(1)} %constant_dynamic-update-slice_fusion.6.mine_ref), channel_id=1, source_target_pairs={{0,1},{1,0},{2,3},{3,2},{4,5},{5,4},{6,7},{7,6},{8,9},{9,8},{10,11... | collective-permute-start | bytes 319496 | tf_op jit(solution)/shard_map/ppermute | solution.py:391
  68.9 3.7 %collective-permute-start.20 = (f32[4,128]{1,0:T(4,128)S(1)}, f32[4,128]{1,0:T(4,128)S(1)}, u32[]{:S(2)}, u32[]{:S(2)}) collective-permute-start(f32[4,128]{1,0:T(4,128)S(1)} %shard_map.85), channel_id=1, source_target_pairs={{0,2},{1,3},{2,0},{3,1},{4,6},{5,7},{6,4},{7,5},{8,10},{9,11},{10,... | collective-permute-start | bytes 6152 | tf_op jit(solution)/shard_map/ppermute | solution.py:391
  69.9 2.7 %collective-permute-start.19 = (f32[4,128]{1,0:T(4,128)S(1)}, f32[4,128]{1,0:T(4,128)S(1)}, u32[]{:S(2)}, u32[]{:S(2)}) collective-permute-start(f32[4,128]{1,0:T(4,128)S(1)} %shard_map.85), channel_id=1, source_target_pairs={{0,1},{1,0},{2,3},{3,2},{4,5},{5,4},{6,7},{7,6},{8,9},{9,8},{10,11... | collective-permute-start | bytes 6152 | tf_op jit(solution)/shard_map/ppermute | solution.py:391
  70.1 3.0 %collective-permute-start.21 = (f32[4,128]{1,0:T(4,128)S(1)}, f32[4,128]{1,0:T(4,128)S(1)}, u32[]{:S(2)}, u32[]{:S(2)}) collective-permute-start(f32[4,128]{1,0:T(4,128)S(1)} %shard_map.85), channel_id=1, source_target_pairs={{0,3},{1,2},{2,1},{3,0},{4,7},{5,6},{6,5},{7,4},{8,11},{9,10},{10,... | collective-permute-start | bytes 6152 | tf_op jit(solution)/shard_map/ppermute | solution.py:391

commit v4 on v3

--- a/solution.py
+++ b/solution.py
@@ -219,16 +219,16 @@
     fold_lanes(peak_ref, total_ref, lse_ref)
 
 
-def slab_kernel(
-    own_ref, mine_ref, theirs_ref, slab_ref, terms_out, token_ref, right_pad, terms_ref, norm_ref, col_ref,
-    *, first, n_half,
-):
-    share = own_ref.shape[1]
+def slab_kernel(own_ref, mine_ref, theirs_ref, *refs, first, n_half, prepare):
+    if prepare:
+        slab_ref, terms_out, token_ref, terms_ref, col_ref, right_pad, norm_ref = refs
+        left = own_ref[...]
+        put(norm_ref, -SCALE * jnp.sum(left * left, axis=0, keepdims=True))
+        to_sublanes(norm_ref, col_ref)
+        terms_ref[...] = jnp.concatenate(target_terms(left.T), axis=1)
+    else:
+        terms_ref, col_ref, slab_ref, terms_out, token_ref, right_pad = refs
     rows = right_pad.shape[1]
-    left = own_ref[...]
-    put(norm_ref, -SCALE * jnp.sum(left * left, axis=0, keepdims=True))
-    to_sublanes(norm_ref, col_ref)
-    terms_ref[...] = jnp.concatenate(target_terms(left.T), axis=1)
     even = lax.axis_index("tgt") % 2 == 0
     right_pad[...] = jnp.zeros(right_pad.shape, jnp.float32)
     for b in range(slab_ref.shape[1] // rows):
@@ -245,7 +245,7 @@
         cross = jnp.dot(terms_ref[...], terms, preferred_element_type=jnp.float32)
         here = slice(b * rows, (b + 1) * rows)
         slab_ref[:, here] = cross + (wide(col_ref[...], rows) + norm)
-        terms_out[here, :] = jnp.concatenate(split(right.T), axis=1)
+        terms_out[here, :] = jnp.concatenate(split(right.T)[:2], axis=1)
     token_ref[...] = jnp.zeros(token_ref.shape, jnp.float32)
 
 
@@ -298,7 +298,7 @@
     masked_ref[...] = jnp.where(aux_ref[2] > 0, f, NEG)
 
 
-def first_col_kernel(score_ref, lse_ref, aux_ref, out_ref, f_ref, masked_ref, kernel_ref, top_ref, col_ref):
+def first_col_kernel(score_ref, lse_ref, aux_ref, out_ref, f_ref, kernel_ref, top_ref, masked_ref, col_ref):
     set_f(lse_ref, aux_ref, f_ref, masked_ref)
     to_sublanes(f_ref, col_ref)
     col_lse(score_ref, col_ref, out_ref, kernel_ref, top_ref)
@@ -379,7 +379,7 @@
         else:
             sum_ref[...] += sums
     sums = sum_ref[...].T
-    out_ref[...] = (sums[0:DEPTH] + sums[DEPTH : 2 * DEPTH] + sums[2 * DEPTH :])[0 : out_ref.shape[0]]
+    out_ref[...] = (sums[0:DEPTH] + sums[DEPTH :])[0 : out_ref.shape[0]]
 
 
 def merge(one, two):
@@ -431,6 +431,7 @@
             self.fetches = [[]] * ITERS
             self.groups = [[]] * (ITERS - 1) + [[0]]
             self.bits = bits
+        self.ready = None
         self.mine = []
         self.theirs = []
         self.offsets = []
@@ -471,13 +472,16 @@
         group, first, size = self.todo.pop(0)
         share = self.own.shape[1]
         rows = self.rows
-        slab, terms, token = call(
-            functools.partial(slab_kernel, first=first, n_half=self.n_half),
-            [(share, size * rows), ((size * rows, 3 * DEPTH), jnp.bfloat16), (8, LANES)],
-            [(DEPTH, rows), ((share, 6 * DEPTH), jnp.bfloat16), (share // LANES, LANES), (share, LANES)],
-            [self.own, self.mine[group], self.theirs[group]],
+        prepare = self.ready is None
+        slab, terms, token, *ready = call(
+            functools.partial(slab_kernel, first=first, n_half=self.n_half, prepare=prepare),
+            [(share, size * rows), ((size * rows, 2 * DEPTH), jnp.bfloat16), (8, LANES)]
+            + [((share, 6 * DEPTH), jnp.bfloat16), (share, LANES)] * prepare,
+            [(DEPTH, rows)] + [(share // LANES, LANES)] * prepare,
+            [self.own, self.mine[group], self.theirs[group], *(self.ready or [])],
             12 * DEPTH * share * size * rows,
         )
+        self.ready = ready or self.ready
         self.terms.append(terms)
         self.slabs.append(slab)
         self.done.append(self.offsets[group][first : first + size])
@@ -559,17 +563,18 @@
         for bit in over_tgt[2:]:
             lse = merge(lse, swap(lse, "tgt", bit))
         if step == 0:
-            lse, base, masked, kernel, top = call(
+            lse, base, kernel, top = call(
                 first_col_kernel,
-                [by_col, by_row, by_row, (rows, cols), by_col],
-                [column], [score, lse, row_aux], 0,
+                [by_col, by_row, (rows, cols), by_col],
+                [by_row, column], [score, lse, row_aux], 0,
             )
         else:
-            lse, f, masked = call(
-                col_kernel,
-                [by_col, by_row, by_row],
-                [by_row, column], [score, kernel, top, base, lse, row_aux], 0,
-            )
+            last = step == ITERS - 1
+            outs = [by_col, by_row, by_row] if last else [by_col]
+            scratch = [by_row, column] if last else [by_row, by_row, by_row, column]
+            lse, *held = call(col_kernel, outs, scratch, [score, kernel, top, base, lse, row_aux], 0)
+            if last:
+                f, masked = held
         if step < ITERS - 1:
             lse = side.land(side.pieces(side.hold(lse), step))
             lse = lax.all_to_all(jnp.broadcast_to(lse, (n_src, *by_col)), "src", 0, 0, tiled=True)
@@ -585,7 +590,7 @@
     ancestors, f, g = call(
         functools.partial(last_kernel, pieces=side.done),
         [(dims, share), by_row, by_col],
-        [by_col, (share // LANES, LANES), (share, LANES), (share, 3 * DEPTH)],
+        [by_col, (share // LANES, LANES), (share, LANES), (share, 2 * DEPTH)],
         [*side.slabs, *side.terms, both, col_aux, f, *side.tokens],
         18 * DEPTH * pairs, pairs, pin=False,
     )

time: 88.6 us -> 87.2 us (0.984)
  Pallas kernels: 24.4 us -> 21.8 us
    pallas_call x12, Pallas kernels: 18.4 us -> 15.8 us  [call(): pl.pallas_call(kernel, out_shape=[buffer(pltpu.VMEM if pin else jax.Shape...]
  transfers between devices with their start and end apart: 22 -> 22, of which waited for: 5 -> 6; matrix products, arithmetic and copies ran while one was open for 0% -> 0% of each run, Pallas kernels for 12% -> 10%
where the time goes in v4:
time: 87.2 us; the launch traced here: 86.9 us
  blocking collectives  41.5 us (48%)
  Pallas kernels  21.8 us (25%)
  starting transfers between devices  18.7 us (21%)
  waiting for transfers between devices  3.18 us (4%)
  between operations  1.56 us (2%)
    all_to_all x3, blocking collectives, shards(): lax.all_to_all(jnp.broadcast_to(lse, (n_src, *by_col)), 'src', 0, 0, tile...  30.8 us
    ppermute x22, starting transfers between devices, swap(): lax.ppermute(value, axis, [(i, i ^ step) for i in range(lax.axis_size(axi...  18.7 us
    pallas_call x12, Pallas kernels, call(): pl.pallas_call(kernel, out_shape=[buffer(pltpu.VMEM if pin else jax.Shape...  15.8 us
    all_to_all x1, blocking collectives, shards(): lax.all_to_all(jnp.broadcast_to(both, (n_src, *both.shape)), 'src', 0, 0,...  10.7 us
    pallas_call x1, Pallas kernels, shards(): pl.pallas_call(first_kernel, out_shape=[pltpu.VMEM(shape, jnp.float32) fo...  5.95 us
    ppermute x22, waiting for transfers between devices, swap(): lax.ppermute(value, axis, [(i, i ^ step) for i in range(lax.axis_size(axi...  3.18 us
  transfers between devices with their start and end apart: 22, of which 6 were waited for; matrix products, arithmetic and copies ran while one was open for 0% of the time, Pallas kernels for 10%

profile of v4, /device:TPU:0, one launch (start us, length us, event | category | flops | bytes accessed | tf_op | source)
XLA Modules:
  0.0 86.9 jit_solution(6471796643627832966)
XLA Ops:
  1.3 5.9 %shard_map.76 = (f32[512,4096]{1,0:T(8,128)S(1)}, f32[4,128]{1,0:T(4,128)S(1)}, f32[3,4,128]{2,1,0:T(4,128)S(1)}, f32[3,32,128]{2,1,0:T(8,128)S(1)}, f32[64,512]{1,0:T(8,128)S(1)}, /*index=5*/f32[1,104,128]{2,1,0:T(8,128)S(1)}) custom-call(f32[50,512]{1,0:T(8,128)} %src_hbm.1, f32[50,4096]{1,0:T(8,128)} %tgt_hbm.1, s32[8]{0:T(128)} %count_src_hbm.1, ...), custom_call_target="tpu_custom_call" | custom-call | flops 1610612736 | tf_op jit(solution)/shard_map/pallas_call | solution.py:520
  7.2 0.5 collective-permute-start
  7.7 2.6 %collective-permute-start.1 = (f32[4,128]{1,0:T(4,128)S(1)}, f32[4,128]{1,0:T(4,128)S(1)}, u32[]{:S(2)}, u32[]{:S(2)}) collective-permute-start(f32[4,128]{1,0:T(4,128)S(1)} %get-tuple-element.73), channel_id=1, source_target_pairs={{0,2},{1,3},{2,0},{3,1},{4,6},{5,7},{6,4},{7,5},{8,10},{9,11},{10,... | collective-permute-start | bytes 6152 | tf_op jit(solution)/shard_map/ppermute | solution.py:391
  10.4 1.8 %collective-permute-start.3 = (f32[1,104,128]{2,1,0:T(8,128)S(1)}, f32[1,104,128]{2,1,0:T(8,128)S(1)}, u32[]{:S(2)}, u32[]{:S(2)}) collective-permute-start(f32[1,104,128]{2,1,0:T(8,128)S(1)} %get-tuple-element.90), channel_id=1, source_target_pairs={{0,8},{4,12},{8,0},{12,4},{16,24},{20,28},{24,16},{28,20},{1,9},{5... | collective-permute-start | bytes 159752 | tf_op jit(solution)/shard_map/ppermute | solution.py:391
  12.2 2.6 %collective-permute-start.4 = (f32[1,104,128]{2,1,0:T(8,128)S(1)}, f32[1,104,128]{2,1,0:T(8,128)S(1)}, u32[]{:S(2)}, u32[]{:S(2)}) collective-permute-start(f32[1,104,128]{2,1,0:T(8,128)S(1)} %get-tuple-element.90), channel_id=1, source_target_pairs={{0,16},{4,20},{8,24},{12,28},{16,0},{20,4},{24,8},{28,12},{1,17},{... | collective-permute-start | bytes 159752 | tf_op jit(solution)/shard_map/ppermute | solution.py:391
  14.8 1.5 %collective-permute-start.5 = (f32[1,104,128]{2,1,0:T(8,128)S(1)}, f32[1,104,128]{2,1,0:T(8,128)S(1)}, u32[]{:S(2)}, u32[]{:S(2)}) collective-permute-start(f32[1,104,128]{2,1,0:T(8,128)S(1)} %get-tuple-element.90), channel_id=1, source_target_pairs={{0,4},{4,0},{8,12},{12,8},{16,20},{20,16},{24,28},{28,24},{1,5},{5... | collective-permute-start | bytes 159752 | tf_op jit(solution)/shard_map/ppermute | solution.py:391
  16.3 2.9 %shard_map.77 = (f32[32,128]{1,0:T(8,128)S(1)}, f32[4,128]{1,0:T(4,128)S(1)}, f32[512,4096]{1,0:T(8,128)S(1)}, f32[32,128]{1,0:T(8,128)S(1)}) custom-call(f32[512,4096]{1,0:T(8,128)S(1)} %get-tuple-element.72.score_ref, f32[4,128]{1,0:T(4,128)S(1)} %multiply_add_fusion.3.lse_ref, f32[3,4,128]{2,1,0:T(4,128)S(1)} %get-tuple-element.74.aux_ref.row_aux), custom_call_target="tpu_custom_call" | custom-call | tf_op jit(solution)/shard_map/pallas_call | solution.py:403
  19.3 10.9 %all_to_all.20.parts_ref = f32[8,32,128]{2,1,0:T(8,128)S(1)} all-to-all(f32[8,32,128]{2,1,0:T(8,128)S(1)} %broadcast_in_dim.12), channel_id=1, replica_groups=mesh['src'=8,'tgt'=4] {'src'}, dimensions={0} | all-to-all | bytes 262144 | tf_op jit(solution)/shard_map/all_to_all | solution.py:580
  30.2 1.1 %shard_map.78 = f32[4,128]{1,0:T(4,128)S(1)} custom-call(f32[512,4096]{1,0:T(8,128)S(1)} %get-tuple-element.72.score_ref, f32[512,4096]{1,0:T(8,128)S(1)} %get-tuple-element.75.kernel_ref, f32[32,128]{1,0:T(8,128)S(1)} %get-tuple-element.76.top_ref, f32[4,128]{1,0:T(4,128)S(1)} %get-tuple-element.77.base_ref, f32[8,32,128]{2,1,0:T(8,128)S(1)} %all_to_all.20.parts_ref, ...), custom_call_target="tpu_custom_call" | custom-call | tf_op jit(solution)/shard_map/pallas_call | solution.py:403
  31.4 1.6 %collective-permute-start.7 = (f32[4,128]{1,0:T(4,128)S(1)}, f32[4,128]{1,0:T(4,128)S(1)}, u32[]{:S(2)}, u32[]{:S(2)}) collective-permute-start(f32[4,128]{1,0:T(4,128)S(1)} %shard_map.78), channel_id=1, source_target_pairs={{0,2},{1,3},{2,0},{3,1},{4,6},{5,7},{6,4},{7,5},{8,10},{9,11},{10,... | collective-permute-start | bytes 6152 | tf_op jit(solution)/shard_map/ppermute | solution.py:391
  33.5 1.1 %collective-permute-start.11 = (f32[1,104,128]{2,1,0:T(8,128)S(1)}, f32[1,104,128]{2,1,0:T(8,128)S(1)}, u32[]{:S(2)}, u32[]{:S(2)}) collective-permute-start(f32[1,104,128]{2,1,0:T(8,128)S(1)} %collective-permute-done.4), channel_id=1, source_target_pairs={{0,8},{4,12},{8,0},{12,4},{16,24},{20,28},{24,16},{28,20},{1,9},{5... | collective-permute-start | bytes 159752 | tf_op jit(solution)/shard_map/ppermute | solution.py:391
  35.0 0.9 %collective-permute-done.8 = f32[4,128]{1,0:T(4,128)S(1)} collective-permute-done((f32[4,128]{1,0:T(4,128)S(1)}, f32[4,128]{1,0:T(4,128)S(1)}, u32[]{:S(2)}, u32[]{:S(2)}) %collective-permute-start.8) | collective-permute-done | bytes 2080 | tf_op jit(solution)/shard_map/ppermute | solution.py:391
  36.0 1.0 %shard_map.79 = f32[32,128]{1,0:T(8,128)S(1)} custom-call(f32[512,4096]{1,0:T(8,128)S(1)} %get-tuple-element.72.score_ref, f32[512,4096]{1,0:T(8,128)S(1)} %get-tuple-element.75.kernel_ref, f32[32,128]{1,0:T(8,128)S(1)} %get-tuple-element.76.top_ref, f32[4,128]{1,0:T(4,128)S(1)} %get-tuple-element.77.base_ref, f32[4,128]{1,0:T(4,128)S(1)} %multiply_add_fusion.2.lse_ref, ...), custom_call_target="tpu_custom_call" | custom-call | tf_op jit(solution)/shard_map/pallas_call | solution.py:403
  37.1 1.0 %shard_map.80 = (f32[512,1024]{1,0:T(8,128)S(1)}, bf16[1024,128]{1,0:T(8,128)(2,1)S(1)}, f32[8,128]{1,0:T(8,128)S(1)}, bf16[512,384]{1,0:T(8,128)(2,1)S(1)}, f32[512,128]{1,0:T(8,128)S(1)}) custom-call(f32[64,512]{1,0:T(8,128)S(1)} %get-tuple-element.116.own_ref, f32[4,104,128]{2,1,0:T(8,128)S(1)} %constant_dynamic-update-slice_fusion.mine_ref, ...), custom_call_target="tpu_custom_call" | custom-call | flops 402653184 | tf_op jit(solution)/shard_map/pallas_call | solution.py:403
  38.1 10.0 %all_to_all.21.parts_ref = f32[8,32,128]{2,1,0:T(8,128)S(1)} all-to-all(f32[8,32,128]{2,1,0:T(8,128)S(1)} %broadcast_in_dim.13), channel_id=1, replica_groups=mesh['src'=8,'tgt'=4] {'src'}, dimensions={0} | all-to-all | bytes 262144 | tf_op jit(solution)/shard_map/all_to_all | solution.py:580
  48.1 1.1 %shard_map.81 = f32[4,128]{1,0:T(4,128)S(1)} custom-call(f32[512,4096]{1,0:T(8,128)S(1)} %get-tuple-element.72.score_ref, f32[512,4096]{1,0:T(8,128)S(1)} %get-tuple-element.75.kernel_ref, f32[32,128]{1,0:T(8,128)S(1)} %get-tuple-element.76.top_ref, f32[4,128]{1,0:T(4,128)S(1)} %get-tuple-element.77.base_ref, f32[8,32,128]{2,1,0:T(8,128)S(1)} %all_to_all.21.parts_ref, ...), custom_call_target="tpu_custom_call" | custom-call | tf_op jit(solution)/shard_map/pallas_call | solution.py:403
  49.3 1.3 %collective-permute-start.13 = (f32[4,128]{1,0:T(4,128)S(1)}, f32[4,128]{1,0:T(4,128)S(1)}, u32[]{:S(2)}, u32[]{:S(2)}) collective-permute-start(f32[4,128]{1,0:T(4,128)S(1)} %shard_map.81), channel_id=1, source_target_pairs={{0,2},{1,3},{2,0},{3,1},{4,6},{5,7},{6,4},{7,5},{8,10},{9,11},{10,... | collective-permute-start | bytes 6152 | tf_op jit(solution)/shard_map/ppermute | solution.py:391
  50.6 0.5 collective-permute-start.14
  51.6 1.7 %collective-permute-start.16 = (f32[1,104,128]{2,1,0:T(8,128)S(1)}, f32[1,104,128]{2,1,0:T(8,128)S(1)}, u32[]{:S(2)}, u32[]{:S(2)}) collective-permute-start(f32[1,104,128]{2,1,0:T(8,128)S(1)} %collective-permute-done.4), channel_id=1, source_target_pairs={{0,4},{4,0},{8,12},{12,8},{16,20},{20,16},{24,28},{28,24},{1,5},{5... | collective-permute-start | bytes 159752 | tf_op jit(solution)/shard_map/ppermute | solution.py:391
  53.7 1.0 %shard_map.82 = f32[32,128]{1,0:T(8,128)S(1)} custom-call(f32[512,4096]{1,0:T(8,128)S(1)} %get-tuple-element.72.score_ref, f32[512,4096]{1,0:T(8,128)S(1)} %get-tuple-element.75.kernel_ref, f32[32,128]{1,0:T(8,128)S(1)} %get-tuple-element.76.top_ref, f32[4,128]{1,0:T(4,128)S(1)} %get-tuple-element.77.base_ref, f32[4,128]{1,0:T(4,128)S(1)} %multiply_add_fusion.1.lse_ref, ...), custom_call_target="tpu_custom_call" | custom-call | tf_op jit(solution)/shard_map/pallas_call | solution.py:403
  54.7 0.8 shard_map.83
  55.5 0.8 shard_map.84
  56.4 9.9 %all_to_all.22.parts_ref = f32[8,32,128]{2,1,0:T(8,128)S(1)} all-to-all(f32[8,32,128]{2,1,0:T(8,128)S(1)} %broadcast_in_dim.14), channel_id=1, replica_groups=mesh['src'=8,'tgt'=4] {'src'}, dimensions={0} | all-to-all | bytes 262144 | tf_op jit(solution)/shard_map/all_to_all | solution.py:580
  66.3 1.1 %shard_map.85 = f32[4,128]{1,0:T(4,128)S(1)} custom-call(f32[512,4096]{1,0:T(8,128)S(1)} %get-tuple-element.72.score_ref, f32[512,4096]{1,0:T(8,128)S(1)} %get-tuple-element.75.kernel_ref, f32[32,128]{1,0:T(8,128)S(1)} %get-tuple-element.76.top_ref, f32[4,128]{1,0:T(4,128)S(1)} %get-tuple-element.77.base_ref, f32[8,32,128]{2,1,0:T(8,128)S(1)} %all_to_all.22.parts_ref, ...), custom_call_target="tpu_custom_call" | custom-call | tf_op jit(solution)/shard_map/pallas_call | solution.py:403
  67.5 1.2 %collective-permute-start.20 = (f32[4,128]{1,0:T(4,128)S(1)}, f32[4,128]{1,0:T(4,128)S(1)}, u32[]{:S(2)}, u32[]{:S(2)}) collective-permute-start(f32[4,128]{1,0:T(4,128)S(1)} %shard_map.85), channel_id=1, source_target_pairs={{0,2},{1,3},{2,0},{3,1},{4,6},{5,7},{6,4},{7,5},{8,10},{9,11},{10,... | collective-permute-start | bytes 6152 | tf_op jit(solution)/shard_map/ppermute | solution.py:391
  68.9 0.9 collective-permute-start.21
  69.7 0.8 shard_map.86
  70.5 0.7 collective-permute-done.20
  71.2 0.7 collective-permute-done.21
  71.9 1.0 %shard_map.87 = (f32[32,128]{1,0:T(8,128)S(1)}, f32[4,128]{1,0:T(4,128)S(1)}, f32[4,128]{1,0:T(4,128)S(1)}) custom-call(f32[512,4096]{1,0:T(8,128)S(1)} %get-tuple-element.72.score_ref, f32[512,4096]{1,0:T(8,128)S(1)} %get-tuple-element.75.kernel_ref, f32[32,128]{1,0:T(8,128)S(1)} %get-tuple-element.76.top_ref, f32[4,128]{1,0:T(4,128)S(1)} %get-tuple-element.77.base_ref, ...), custom_call_target="tpu_custom_call" | custom-call | tf_op jit(solution)/shard_map/pallas_call | solution.py:403
  73.0 10.7 %all_to_all.23.refs_8_ = f32[8,36,128]{2,1,0:T(8,128)S(1)} all-to-all(f32[8,36,128]{2,1,0:T(8,128)S(1)} %broadcast_in_dim.15), channel_id=1, replica_groups=mesh['src'=8,'tgt'=4] {'src'}, dimensions={0} | all-to-all | bytes 294912 | tf_op jit(solution)/shard_map/all_to_all | solution.py:589
  83.6 3.2 %shard_map.88 = (f32[50,512]{1,0:T(8,128)}, f32[4,128]{1,0:T(4,128)}, f32[32,128]{1,0:T(8,128)}) custom-call(f32[512,1024]{1,0:T(8,128)S(1)} %get-tuple-element.94.refs_0_, f32[512,1024]{1,0:T(8,128)S(1)} %get-tuple-element.105.refs_1_, f32[512,1024]{1,0:T(8,128)S(1)} %get-tuple-element.108.refs_2_, f32[512,1024]{1,0:T(8,128)S(1)} %get-tuple-element.122.refs_3_, ...), custom_call_target="tpu_custom_call" | custom-call | flops 2415919104 | tf_op jit(solution)/shard_map/pallas_call | solution.py:403
  (46 shorter events, 2.5 us)
Async XLA Ops:
  7.2 7.6 %collective-permute-start = (f32[4,128]{1,0:T(4,128)S(1)}, f32[4,128]{1,0:T(4,128)S(1)}, u32[]{:S(2)}, u32[]{:S(2)}) collective-permute-start(f32[4,128]{1,0:T(4,128)S(1)} %get-tuple-element.73), channel_id=1, source_target_pairs={{0,1},{1,0},{2,3},{3,2},{4,5},{5,4},{6,7},{7,6},{8,9},{9,8},{10,11... | collective-permute-start | bytes 6152 | tf_op jit(solution)/shard_map/ppermute | solution.py:391
  7.7 8.5 %collective-permute-start.1 = (f32[4,128]{1,0:T(4,128)S(1)}, f32[4,128]{1,0:T(4,128)S(1)}, u32[]{:S(2)}, u32[]{:S(2)}) collective-permute-start(f32[4,128]{1,0:T(4,128)S(1)} %get-tuple-element.73), channel_id=1, source_target_pairs={{0,2},{1,3},{2,0},{3,1},{4,6},{5,7},{6,4},{7,5},{8,10},{9,11},{10,... | collective-permute-start | bytes 6152 | tf_op jit(solution)/shard_map/ppermute | solution.py:391
  10.3 5.9 %collective-permute-start.2 = (f32[4,128]{1,0:T(4,128)S(1)}, f32[4,128]{1,0:T(4,128)S(1)}, u32[]{:S(2)}, u32[]{:S(2)}) collective-permute-start(f32[4,128]{1,0:T(4,128)S(1)} %get-tuple-element.73), channel_id=1, source_target_pairs={{0,3},{1,2},{2,1},{3,0},{4,7},{5,6},{6,5},{7,4},{8,11},{9,10},{10,... | collective-permute-start | bytes 6152 | tf_op jit(solution)/shard_map/ppermute | solution.py:391
  10.4 8.8 %collective-permute-start.3 = (f32[1,104,128]{2,1,0:T(8,128)S(1)}, f32[1,104,128]{2,1,0:T(8,128)S(1)}, u32[]{:S(2)}, u32[]{:S(2)}) collective-permute-start(f32[1,104,128]{2,1,0:T(8,128)S(1)} %get-tuple-element.90), channel_id=1, source_target_pairs={{0,8},{4,12},{8,0},{12,4},{16,24},{20,28},{24,16},{28,20},{1,9},{5... | collective-permute-start | bytes 159752 | tf_op jit(solution)/shard_map/ppermute | solution.py:391
  12.2 7.0 %collective-permute-start.4 = (f32[1,104,128]{2,1,0:T(8,128)S(1)}, f32[1,104,128]{2,1,0:T(8,128)S(1)}, u32[]{:S(2)}, u32[]{:S(2)}) collective-permute-start(f32[1,104,128]{2,1,0:T(8,128)S(1)} %get-tuple-element.90), channel_id=1, source_target_pairs={{0,16},{4,20},{8,24},{12,28},{16,0},{20,4},{24,8},{28,12},{1,17},{... | collective-permute-start | bytes 159752 | tf_op jit(solution)/shard_map/ppermute | solution.py:391
  14.8 4.5 %collective-permute-start.5 = (f32[1,104,128]{2,1,0:T(8,128)S(1)}, f32[1,104,128]{2,1,0:T(8,128)S(1)}, u32[]{:S(2)}, u32[]{:S(2)}) collective-permute-start(f32[1,104,128]{2,1,0:T(8,128)S(1)} %get-tuple-element.90), channel_id=1, source_target_pairs={{0,4},{4,0},{8,12},{12,8},{16,20},{20,16},{24,28},{28,24},{1,5},{5... | collective-permute-start | bytes 159752 | tf_op jit(solution)/shard_map/ppermute | solution.py:391
  31.3 3.3 %collective-permute-start.6 = (f32[4,128]{1,0:T(4,128)S(1)}, f32[4,128]{1,0:T(4,128)S(1)}, u32[]{:S(2)}, u32[]{:S(2)}) collective-permute-start(f32[4,128]{1,0:T(4,128)S(1)} %shard_map.78), channel_id=1, source_target_pairs={{0,1},{1,0},{2,3},{3,2},{4,5},{5,4},{6,7},{7,6},{8,9},{9,8},{10,11... | collective-permute-start | bytes 6152 | tf_op jit(solution)/shard_map/ppermute | solution.py:391
  31.4 3.7 %collective-permute-start.7 = (f32[4,128]{1,0:T(4,128)S(1)}, f32[4,128]{1,0:T(4,128)S(1)}, u32[]{:S(2)}, u32[]{:S(2)}) collective-permute-start(f32[4,128]{1,0:T(4,128)S(1)} %shard_map.78), channel_id=1, source_target_pairs={{0,2},{1,3},{2,0},{3,1},{4,6},{5,7},{6,4},{7,5},{8,10},{9,11},{10,... | collective-permute-start | bytes 6152 | tf_op jit(solution)/shard_map/ppermute | solution.py:391
  33.0 3.0 %collective-permute-start.8 = (f32[4,128]{1,0:T(4,128)S(1)}, f32[4,128]{1,0:T(4,128)S(1)}, u32[]{:S(2)}, u32[]{:S(2)}) collective-permute-start(f32[4,128]{1,0:T(4,128)S(1)} %shard_map.78), channel_id=1, source_target_pairs={{0,3},{1,2},{2,1},{3,0},{4,7},{5,6},{6,5},{7,4},{8,11},{9,10},{10,... | collective-permute-start | bytes 6152 | tf_op jit(solution)/shard_map/ppermute | solution.py:391
  33.3 4.8 %collective-permute-start.10 = (f32[1,104,128]{2,1,0:T(8,128)S(1)}, f32[1,104,128]{2,1,0:T(8,128)S(1)}, u32[]{:S(2)}, u32[]{:S(2)}) collective-permute-start(f32[1,104,128]{2,1,0:T(8,128)S(1)} %collective-permute-done.3), channel_id=1, source_target_pairs={{0,4},{4,0},{8,12},{12,8},{16,20},{20,16},{24,28},{28,24},{1,5},{5... | collective-permute-start | bytes 159752 | tf_op jit(solution)/shard_map/ppermute | solution.py:391
  33.5 4.6 %collective-permute-start.11 = (f32[1,104,128]{2,1,0:T(8,128)S(1)}, f32[1,104,128]{2,1,0:T(8,128)S(1)}, u32[]{:S(2)}, u32[]{:S(2)}) collective-permute-start(f32[1,104,128]{2,1,0:T(8,128)S(1)} %collective-permute-done.4), channel_id=1, source_target_pairs={{0,8},{4,12},{8,0},{12,4},{16,24},{20,28},{24,16},{28,20},{1,9},{5... | collective-permute-start | bytes 159752 | tf_op jit(solution)/shard_map/ppermute | solution.py:391
  34.6 2.5 %collective-permute-start.9 = (f32[4,104,128]{2,1,0:T(8,128)S(1)}, f32[4,104,128]{2,1,0:T(8,128)S(1)}, u32[]{:S(2)}, u32[]{:S(2)}) collective-permute-start(f32[4,104,128]{2,1,0:T(8,128)S(1)} %constant_dynamic-update-slice_fusion.mine_ref), channel_id=1, source_target_pairs={{0,1},{1,0},{2,3},{3,2},{4,5},{5,4},{6,7},{7,6},{8,9},{9,8},{10,11... | collective-permute-start | bytes 638984 | tf_op jit(solution)/shard_map/ppermute | solution.py:391
  49.2 2.4 %collective-permute-start.12 = (f32[4,128]{1,0:T(4,128)S(1)}, f32[4,128]{1,0:T(4,128)S(1)}, u32[]{:S(2)}, u32[]{:S(2)}) collective-permute-start(f32[4,128]{1,0:T(4,128)S(1)} %shard_map.81), channel_id=1, source_target_pairs={{0,1},{1,0},{2,3},{3,2},{4,5},{5,4},{6,7},{7,6},{8,9},{9,8},{10,11... | collective-permute-start | bytes 6152 | tf_op jit(solution)/shard_map/ppermute | solution.py:391
  49.3 4.0 %collective-permute-start.13 = (f32[4,128]{1,0:T(4,128)S(1)}, f32[4,128]{1,0:T(4,128)S(1)}, u32[]{:S(2)}, u32[]{:S(2)}) collective-permute-start(f32[4,128]{1,0:T(4,128)S(1)} %shard_map.81), channel_id=1, source_target_pairs={{0,2},{1,3},{2,0},{3,1},{4,6},{5,7},{6,4},{7,5},{8,10},{9,11},{10,... | collective-permute-start | bytes 6152 | tf_op jit(solution)/shard_map/ppermute | solution.py:391
  50.6 3.0 %collective-permute-start.14 = (f32[4,128]{1,0:T(4,128)S(1)}, f32[4,128]{1,0:T(4,128)S(1)}, u32[]{:S(2)}, u32[]{:S(2)}) collective-permute-start(f32[4,128]{1,0:T(4,128)S(1)} %shard_map.81), channel_id=1, source_target_pairs={{0,3},{1,2},{2,1},{3,0},{4,7},{5,6},{6,5},{7,4},{8,11},{9,10},{10,... | collective-permute-start | bytes 6152 | tf_op jit(solution)/shard_map/ppermute | solution.py:391
  51.1 5.2 %collective-permute-start.17 = (f32[1,104,128]{2,1,0:T(8,128)S(1)}, f32[1,104,128]{2,1,0:T(8,128)S(1)}, u32[]{:S(2)}, u32[]{:S(2)}) collective-permute-start(f32[1,104,128]{2,1,0:T(8,128)S(1)} %collective-permute-done.11), channel_id=1, source_target_pairs={{0,4},{4,0},{8,12},{12,8},{16,20},{20,16},{24,28},{28,24},{1,5},{5... | collective-permute-start | bytes 159752 | tf_op jit(solution)/shard_map/ppermute | solution.py:391
  51.4 4.0 %collective-permute-start.15 = (f32[2,104,128]{2,1,0:T(8,128)S(1)}, f32[2,104,128]{2,1,0:T(8,128)S(1)}, u32[]{:S(2)}, u32[]{:S(2)}) collective-permute-start(f32[2,104,128]{2,1,0:T(8,128)S(1)} %constant_dynamic-update-slice_fusion.4.mine_ref), channel_id=1, source_target_pairs={{0,1},{1,0},{2,3},{3,2},{4,5},{5,4},{6,7},{7,6},{8,9},{9,8},{10,11... | collective-permute-start | bytes 319496 | tf_op jit(solution)/shard_map/ppermute | solution.py:391
  51.6 4.8 %collective-permute-start.16 = (f32[1,104,128]{2,1,0:T(8,128)S(1)}, f32[1,104,128]{2,1,0:T(8,128)S(1)}, u32[]{:S(2)}, u32[]{:S(2)}) collective-permute-start(f32[1,104,128]{2,1,0:T(8,128)S(1)} %collective-permute-done.4), channel_id=1, source_target_pairs={{0,4},{4,0},{8,12},{12,8},{16,20},{20,16},{24,28},{28,24},{1,5},{5... | collective-permute-start | bytes 159752 | tf_op jit(solution)/shard_map/ppermute | solution.py:391
  67.4 2.3 %collective-permute-start.18 = (f32[2,104,128]{2,1,0:T(8,128)S(1)}, f32[2,104,128]{2,1,0:T(8,128)S(1)}, u32[]{:S(2)}, u32[]{:S(2)}) collective-permute-start(f32[2,104,128]{2,1,0:T(8,128)S(1)} %constant_dynamic-update-slice_fusion.6.mine_ref), channel_id=1, source_target_pairs={{0,1},{1,0},{2,3},{3,2},{4,5},{5,4},{6,7},{7,6},{8,9},{9,8},{10,11... | collective-permute-start | bytes 319496 | tf_op jit(solution)/shard_map/ppermute | solution.py:391
  67.5 3.7 %collective-permute-start.20 = (f32[4,128]{1,0:T(4,128)S(1)}, f32[4,128]{1,0:T(4,128)S(1)}, u32[]{:S(2)}, u32[]{:S(2)}) collective-permute-start(f32[4,128]{1,0:T(4,128)S(1)} %shard_map.85), channel_id=1, source_target_pairs={{0,2},{1,3},{2,0},{3,1},{4,6},{5,7},{6,4},{7,5},{8,10},{9,11},{10,... | collective-permute-start | bytes 6152 | tf_op jit(solution)/shard_map/ppermute | solution.py:391
  68.7 2.5 %collective-permute-start.19 = (f32[4,128]{1,0:T(4,128)S(1)}, f32[4,128]{1,0:T(4,128)S(1)}, u32[]{:S(2)}, u32[]{:S(2)}) collective-permute-start(f32[4,128]{1,0:T(4,128)S(1)} %shard_map.85), channel_id=1, source_target_pairs={{0,1},{1,0},{2,3},{3,2},{4,5},{5,4},{6,7},{7,6},{8,9},{9,8},{10,11... | collective-permute-start | bytes 6152 | tf_op jit(solution)/shard_map/ppermute | solution.py:391
  68.9 3.0 %collective-permute-start.21 = (f32[4,128]{1,0:T(4,128)S(1)}, f32[4,128]{1,0:T(4,128)S(1)}, u32[]{:S(2)}, u32[]{:S(2)}) collective-permute-start(f32[4,128]{1,0:T(4,128)S(1)} %shard_map.85), channel_id=1, source_target_pairs={{0,3},{1,2},{2,1},{3,0},{4,7},{5,6},{6,5},{7,4},{8,11},{9,10},{10,... | collective-permute-start | bytes 6152 | tf_op jit(solution)/shard_map/ppermute | solution.py:391

commit v5 on v4

--- a/solution.py
+++ b/solution.py
@@ -188,7 +188,7 @@
     size = 512
 
     def scores(c):
-        here = pl.ds(pl.multiple_of(c * size, size), size)
+        here = slice(c * size, (c + 1) * size)
         right_pad[0:dims, :] = tgt_ref[:, here]
         right = right_pad[...]
         spot = lax.broadcasted_iota(jnp.int32, (1, size), 1) + c * size
@@ -203,7 +203,7 @@
     peak_ref[...] = jnp.full(peak_ref.shape, 2.0 * NEG, jnp.float32)
     total_ref[...] = jnp.zeros(total_ref.shape, jnp.float32)
 
-    def block(c, _):
+    for c in range(cols // size):
         z = scores(c)
         before = peak_ref[...]
         peak = functools.reduce(jnp.maximum, z, before)
@@ -211,9 +211,6 @@
             jnp.add, [jnp.exp2(v - peak) for v in z], total_ref[...] * jnp.exp2(before - peak)
         )
         peak_ref[...] = peak
-        return 0
-
-    lax.fori_loop(0, cols // size, block, 0)
     share = own_ref.shape[1]
     own_ref[0:dims, :] = tgt_ref[:, pl.ds(pl.multiple_of(lax.axis_index("src") * share, share), share)]
     fold_lanes(peak_ref, total_ref, lse_ref)

time: 87.2 us -> 85.4 us (0.979)
  Pallas kernels: 21.8 us -> 20 us
    pallas_call x1, Pallas kernels: 5.95 us -> 4.23 us  [shards(): pl.pallas_call(first_kernel, out_shape=[pltpu.VMEM(shape, jnp.float32) fo...]
where the time goes in v5:
time: 85.4 us; the launch traced here: 85.1 us
  blocking collectives  41.5 us (49%)
  Pallas kernels  20 us (23%)
  starting transfers between devices  18.7 us (22%)
  waiting for transfers between devices  3.19 us (4%)
  between operations  1.56 us (2%)
    all_to_all x3, blocking collectives, shards(): lax.all_to_all(jnp.broadcast_to(lse, (n_src, *by_col)), 'src', 0, 0, tile...  30.8 us
    ppermute x22, starting transfers between devices, swap(): lax.ppermute(value, axis, [(i, i ^ step) for i in range(lax.axis_size(axi...  18.7 us
    pallas_call x12, Pallas kernels, call(): pl.pallas_call(kernel, out_shape=[buffer(pltpu.VMEM if pin else jax.Shape...  15.8 us
    all_to_all x1, blocking collectives, shards(): lax.all_to_all(jnp.broadcast_to(both, (n_src, *both.shape)), 'src', 0, 0,...  10.7 us
    pallas_call x1, Pallas kernels, shards(): pl.pallas_call(first_kernel, out_shape=[pltpu.VMEM(shape, jnp.float32) fo...  4.23 us
    ppermute x22, waiting for transfers between devices, swap(): lax.ppermute(value, axis, [(i, i ^ step) for i in range(lax.axis_size(axi...  3.19 us
  transfers between devices with their start and end apart: 22, of which 6 were waited for; matrix products, arithmetic and copies ran while one was open for 0% of the time, Pallas kernels for 10%

profile of v5, /device:TPU:0, one launch (start us, length us, event | category | flops | bytes accessed | tf_op | source)
XLA Modules:
  0.0 85.1 jit_solution(16676031825179868849)
XLA Ops:
  1.3 4.2 %shard_map.76 = (f32[512,4096]{1,0:T(8,128)S(1)}, f32[4,128]{1,0:T(4,128)S(1)}, f32[3,4,128]{2,1,0:T(4,128)S(1)}, f32[3,32,128]{2,1,0:T(8,128)S(1)}, f32[64,512]{1,0:T(8,128)S(1)}, /*index=5*/f32[1,104,128]{2,1,0:T(8,128)S(1)}) custom-call(f32[50,512]{1,0:T(8,128)} %src_hbm.1, f32[50,4096]{1,0:T(8,128)} %tgt_hbm.1, s32[8]{0:T(128)} %count_src_hbm.1, ...), custom_call_target="tpu_custom_call" | custom-call | flops 1610612736 | tf_op jit(solution)/shard_map/pallas_call | solution.py:517
  5.5 0.5 collective-permute-start
  6.0 2.6 %collective-permute-start.1 = (f32[4,128]{1,0:T(4,128)S(1)}, f32[4,128]{1,0:T(4,128)S(1)}, u32[]{:S(2)}, u32[]{:S(2)}) collective-permute-start(f32[4,128]{1,0:T(4,128)S(1)} %get-tuple-element.73), channel_id=1, source_target_pairs={{0,2},{1,3},{2,0},{3,1},{4,6},{5,7},{6,4},{7,5},{8,10},{9,11},{10,... | collective-permute-start | bytes 6152 | tf_op jit(solution)/shard_map/ppermute | solution.py:388
  8.7 1.8 %collective-permute-start.3 = (f32[1,104,128]{2,1,0:T(8,128)S(1)}, f32[1,104,128]{2,1,0:T(8,128)S(1)}, u32[]{:S(2)}, u32[]{:S(2)}) collective-permute-start(f32[1,104,128]{2,1,0:T(8,128)S(1)} %get-tuple-element.90), channel_id=1, source_target_pairs={{0,8},{4,12},{8,0},{12,4},{16,24},{20,28},{24,16},{28,20},{1,9},{5... | collective-permute-start | bytes 159752 | tf_op jit(solution)/shard_map/ppermute | solution.py:388
  10.5 2.6 %collective-permute-start.4 = (f32[1,104,128]{2,1,0:T(8,128)S(1)}, f32[1,104,128]{2,1,0:T(8,128)S(1)}, u32[]{:S(2)}, u32[]{:S(2)}) collective-permute-start(f32[1,104,128]{2,1,0:T(8,128)S(1)} %get-tuple-element.90), channel_id=1, source_target_pairs={{0,16},{4,20},{8,24},{12,28},{16,0},{20,4},{24,8},{28,12},{1,17},{... | collective-permute-start | bytes 159752 | tf_op jit(solution)/shard_map/ppermute | solution.py:388
  13.1 1.5 %collective-permute-start.5 = (f32[1,104,128]{2,1,0:T(8,128)S(1)}, f32[1,104,128]{2,1,0:T(8,128)S(1)}, u32[]{:S(2)}, u32[]{:S(2)}) collective-permute-start(f32[1,104,128]{2,1,0:T(8,128)S(1)} %get-tuple-element.90), channel_id=1, source_target_pairs={{0,4},{4,0},{8,12},{12,8},{16,20},{20,16},{24,28},{28,24},{1,5},{5... | collective-permute-start | bytes 159752 | tf_op jit(solution)/shard_map/ppermute | solution.py:388
  14.6 2.9 %shard_map.77 = (f32[32,128]{1,0:T(8,128)S(1)}, f32[4,128]{1,0:T(4,128)S(1)}, f32[512,4096]{1,0:T(8,128)S(1)}, f32[32,128]{1,0:T(8,128)S(1)}) custom-call(f32[512,4096]{1,0:T(8,128)S(1)} %get-tuple-element.72.score_ref, f32[4,128]{1,0:T(4,128)S(1)} %multiply_add_fusion.3.lse_ref, f32[3,4,128]{2,1,0:T(4,128)S(1)} %get-tuple-element.74.aux_ref.row_aux), custom_call_target="tpu_custom_call" | custom-call | tf_op jit(solution)/shard_map/pallas_call | solution.py:400
  17.6 10.9 %all_to_all.20.parts_ref = f32[8,32,128]{2,1,0:T(8,128)S(1)} all-to-all(f32[8,32,128]{2,1,0:T(8,128)S(1)} %broadcast_in_dim.12), channel_id=1, replica_groups=mesh['src'=8,'tgt'=4] {'src'}, dimensions={0} | all-to-all | bytes 262144 | tf_op jit(solution)/shard_map/all_to_all | solution.py:577
  28.5 1.1 %shard_map.78 = f32[4,128]{1,0:T(4,128)S(1)} custom-call(f32[512,4096]{1,0:T(8,128)S(1)} %get-tuple-element.72.score_ref, f32[512,4096]{1,0:T(8,128)S(1)} %get-tuple-element.75.kernel_ref, f32[32,128]{1,0:T(8,128)S(1)} %get-tuple-element.76.top_ref, f32[4,128]{1,0:T(4,128)S(1)} %get-tuple-element.77.base_ref, f32[8,32,128]{2,1,0:T(8,128)S(1)} %all_to_all.20.parts_ref, ...), custom_call_target="tpu_custom_call" | custom-call | tf_op jit(solution)/shard_map/pallas_call | solution.py:400
  29.7 1.6 %collective-permute-start.7 = (f32[4,128]{1,0:T(4,128)S(1)}, f32[4,128]{1,0:T(4,128)S(1)}, u32[]{:S(2)}, u32[]{:S(2)}) collective-permute-start(f32[4,128]{1,0:T(4,128)S(1)} %shard_map.78), channel_id=1, source_target_pairs={{0,2},{1,3},{2,0},{3,1},{4,6},{5,7},{6,4},{7,5},{8,10},{9,11},{10,... | collective-permute-start | bytes 6152 | tf_op jit(solution)/shard_map/ppermute | solution.py:388
  31.8 1.1 %collective-permute-start.11 = (f32[1,104,128]{2,1,0:T(8,128)S(1)}, f32[1,104,128]{2,1,0:T(8,128)S(1)}, u32[]{:S(2)}, u32[]{:S(2)}) collective-permute-start(f32[1,104,128]{2,1,0:T(8,128)S(1)} %collective-permute-done.4), channel_id=1, source_target_pairs={{0,8},{4,12},{8,0},{12,4},{16,24},{20,28},{24,16},{28,20},{1,9},{5... | collective-permute-start | bytes 159752 | tf_op jit(solution)/shard_map/ppermute | solution.py:388
  33.3 0.9 %collective-permute-done.8 = f32[4,128]{1,0:T(4,128)S(1)} collective-permute-done((f32[4,128]{1,0:T(4,128)S(1)}, f32[4,128]{1,0:T(4,128)S(1)}, u32[]{:S(2)}, u32[]{:S(2)}) %collective-permute-start.8) | collective-permute-done | bytes 2080 | tf_op jit(solution)/shard_map/ppermute | solution.py:388
  34.3 1.0 %shard_map.79 = f32[32,128]{1,0:T(8,128)S(1)} custom-call(f32[512,4096]{1,0:T(8,128)S(1)} %get-tuple-element.72.score_ref, f32[512,4096]{1,0:T(8,128)S(1)} %get-tuple-element.75.kernel_ref, f32[32,128]{1,0:T(8,128)S(1)} %get-tuple-element.76.top_ref, f32[4,128]{1,0:T(4,128)S(1)} %get-tuple-element.77.base_ref, f32[4,128]{1,0:T(4,128)S(1)} %multiply_add_fusion.2.lse_ref, ...), custom_call_target="tpu_custom_call" | custom-call | tf_op jit(solution)/shard_map/pallas_call | solution.py:400
  35.3 1.0 %shard_map.80 = (f32[512,1024]{1,0:T(8,128)S(1)}, bf16[1024,128]{1,0:T(8,128)(2,1)S(1)}, f32[8,128]{1,0:T(8,128)S(1)}, bf16[512,384]{1,0:T(8,128)(2,1)S(1)}, f32[512,128]{1,0:T(8,128)S(1)}) custom-call(f32[64,512]{1,0:T(8,128)S(1)} %get-tuple-element.116.own_ref, f32[4,104,128]{2,1,0:T(8,128)S(1)} %constant_dynamic-update-slice_fusion.mine_ref, ...), custom_call_target="tpu_custom_call" | custom-call | flops 402653184 | tf_op jit(solution)/shard_map/pallas_call | solution.py:400
  36.4 10.0 %all_to_all.21.parts_ref = f32[8,32,128]{2,1,0:T(8,128)S(1)} all-to-all(f32[8,32,128]{2,1,0:T(8,128)S(1)} %broadcast_in_dim.13), channel_id=1, replica_groups=mesh['src'=8,'tgt'=4] {'src'}, dimensions={0} | all-to-all | bytes 262144 | tf_op jit(solution)/shard_map/all_to_all | solution.py:577
  46.4 1.1 %shard_map.81 = f32[4,128]{1,0:T(4,128)S(1)} custom-call(f32[512,4096]{1,0:T(8,128)S(1)} %get-tuple-element.72.score_ref, f32[512,4096]{1,0:T(8,128)S(1)} %get-tuple-element.75.kernel_ref, f32[32,128]{1,0:T(8,128)S(1)} %get-tuple-element.76.top_ref, f32[4,128]{1,0:T(4,128)S(1)} %get-tuple-element.77.base_ref, f32[8,32,128]{2,1,0:T(8,128)S(1)} %all_to_all.21.parts_ref, ...), custom_call_target="tpu_custom_call" | custom-call | tf_op jit(solution)/shard_map/pallas_call | solution.py:400
  47.6 1.3 %collective-permute-start.13 = (f32[4,128]{1,0:T(4,128)S(1)}, f32[4,128]{1,0:T(4,128)S(1)}, u32[]{:S(2)}, u32[]{:S(2)}) collective-permute-start(f32[4,128]{1,0:T(4,128)S(1)} %shard_map.81), channel_id=1, source_target_pairs={{0,2},{1,3},{2,0},{3,1},{4,6},{5,7},{6,4},{7,5},{8,10},{9,11},{10,... | collective-permute-start | bytes 6152 | tf_op jit(solution)/shard_map/ppermute | solution.py:388
  48.9 0.5 collective-permute-start.14
  49.9 1.7 %collective-permute-start.16 = (f32[1,104,128]{2,1,0:T(8,128)S(1)}, f32[1,104,128]{2,1,0:T(8,128)S(1)}, u32[]{:S(2)}, u32[]{:S(2)}) collective-permute-start(f32[1,104,128]{2,1,0:T(8,128)S(1)} %collective-permute-done.4), channel_id=1, source_target_pairs={{0,4},{4,0},{8,12},{12,8},{16,20},{20,16},{24,28},{28,24},{1,5},{5... | collective-permute-start | bytes 159752 | tf_op jit(solution)/shard_map/ppermute | solution.py:388
  51.9 1.0 %shard_map.82 = f32[32,128]{1,0:T(8,128)S(1)} custom-call(f32[512,4096]{1,0:T(8,128)S(1)} %get-tuple-element.72.score_ref, f32[512,4096]{1,0:T(8,128)S(1)} %get-tuple-element.75.kernel_ref, f32[32,128]{1,0:T(8,128)S(1)} %get-tuple-element.76.top_ref, f32[4,128]{1,0:T(4,128)S(1)} %get-tuple-element.77.base_ref, f32[4,128]{1,0:T(4,128)S(1)} %multiply_add_fusion.1.lse_ref, ...), custom_call_target="tpu_custom_call" | custom-call | tf_op jit(solution)/shard_map/pallas_call | solution.py:400
  53.0 0.8 shard_map.83
  53.8 0.8 shard_map.84
  54.7 9.9 %all_to_all.22.parts_ref = f32[8,32,128]{2,1,0:T(8,128)S(1)} all-to-all(f32[8,32,128]{2,1,0:T(8,128)S(1)} %broadcast_in_dim.14), channel_id=1, replica_groups=mesh['src'=8,'tgt'=4] {'src'}, dimensions={0} | all-to-all | bytes 262144 | tf_op jit(solution)/shard_map/all_to_all | solution.py:577
  64.6 1.1 %shard_map.85 = f32[4,128]{1,0:T(4,128)S(1)} custom-call(f32[512,4096]{1,0:T(8,128)S(1)} %get-tuple-element.72.score_ref, f32[512,4096]{1,0:T(8,128)S(1)} %get-tuple-element.75.kernel_ref, f32[32,128]{1,0:T(8,128)S(1)} %get-tuple-element.76.top_ref, f32[4,128]{1,0:T(4,128)S(1)} %get-tuple-element.77.base_ref, f32[8,32,128]{2,1,0:T(8,128)S(1)} %all_to_all.22.parts_ref, ...), custom_call_target="tpu_custom_call" | custom-call | tf_op jit(solution)/shard_map/pallas_call | solution.py:400
  65.8 1.2 %collective-permute-start.20 = (f32[4,128]{1,0:T(4,128)S(1)}, f32[4,128]{1,0:T(4,128)S(1)}, u32[]{:S(2)}, u32[]{:S(2)}) collective-permute-start(f32[4,128]{1,0:T(4,128)S(1)} %shard_map.85), channel_id=1, source_target_pairs={{0,2},{1,3},{2,0},{3,1},{4,6},{5,7},{6,4},{7,5},{8,10},{9,11},{10,... | collective-permute-start | bytes 6152 | tf_op jit(solution)/shard_map/ppermute | solution.py:388
  67.1 0.8 collective-permute-start.21
  68.0 0.8 shard_map.86
  68.8 0.7 collective-permute-done.20
  69.4 0.7 collective-permute-done.21
  70.2 1.0 %shard_map.87 = (f32[32,128]{1,0:T(8,128)S(1)}, f32[4,128]{1,0:T(4,128)S(1)}, f32[4,128]{1,0:T(4,128)S(1)}) custom-call(f32[512,4096]{1,0:T(8,128)S(1)} %get-tuple-element.72.score_ref, f32[512,4096]{1,0:T(8,128)S(1)} %get-tuple-element.75.kernel_ref, f32[32,128]{1,0:T(8,128)S(1)} %get-tuple-element.76.top_ref, f32[4,128]{1,0:T(4,128)S(1)} %get-tuple-element.77.base_ref, ...), custom_call_target="tpu_custom_call" | custom-call | tf_op jit(solution)/shard_map/pallas_call | solution.py:400
  71.3 10.7 %all_to_all.23.refs_8_ = f32[8,36,128]{2,1,0:T(8,128)S(1)} all-to-all(f32[8,36,128]{2,1,0:T(8,128)S(1)} %broadcast_in_dim.15), channel_id=1, replica_groups=mesh['src'=8,'tgt'=4] {'src'}, dimensions={0} | all-to-all | bytes 294912 | tf_op jit(solution)/shard_map/all_to_all | solution.py:586
  81.9 3.2 %shard_map.88 = (f32[50,512]{1,0:T(8,128)}, f32[4,128]{1,0:T(4,128)}, f32[32,128]{1,0:T(8,128)}) custom-call(f32[512,1024]{1,0:T(8,128)S(1)} %get-tuple-element.94.refs_0_, f32[512,1024]{1,0:T(8,128)S(1)} %get-tuple-element.105.refs_1_, f32[512,1024]{1,0:T(8,128)S(1)} %get-tuple-element.108.refs_2_, f32[512,1024]{1,0:T(8,128)S(1)} %get-tuple-element.122.refs_3_, ...), custom_call_target="tpu_custom_call" | custom-call | flops 2415919104 | tf_op jit(solution)/shard_map/pallas_call | solution.py:400
  (46 shorter events, 2.5 us)
Async XLA Ops:
  5.5 7.6 %collective-permute-start = (f32[4,128]{1,0:T(4,128)S(1)}, f32[4,128]{1,0:T(4,128)S(1)}, u32[]{:S(2)}, u32[]{:S(2)}) collective-permute-start(f32[4,128]{1,0:T(4,128)S(1)} %get-tuple-element.73), channel_id=1, source_target_pairs={{0,1},{1,0},{2,3},{3,2},{4,5},{5,4},{6,7},{7,6},{8,9},{9,8},{10,11... | collective-permute-start | bytes 6152 | tf_op jit(solution)/shard_map/ppermute | solution.py:388
  6.0 8.5 %collective-permute-start.1 = (f32[4,128]{1,0:T(4,128)S(1)}, f32[4,128]{1,0:T(4,128)S(1)}, u32[]{:S(2)}, u32[]{:S(2)}) collective-permute-start(f32[4,128]{1,0:T(4,128)S(1)} %get-tuple-element.73), channel_id=1, source_target_pairs={{0,2},{1,3},{2,0},{3,1},{4,6},{5,7},{6,4},{7,5},{8,10},{9,11},{10,... | collective-permute-start | bytes 6152 | tf_op jit(solution)/shard_map/ppermute | solution.py:388
  8.6 5.9 %collective-permute-start.2 = (f32[4,128]{1,0:T(4,128)S(1)}, f32[4,128]{1,0:T(4,128)S(1)}, u32[]{:S(2)}, u32[]{:S(2)}) collective-permute-start(f32[4,128]{1,0:T(4,128)S(1)} %get-tuple-element.73), channel_id=1, source_target_pairs={{0,3},{1,2},{2,1},{3,0},{4,7},{5,6},{6,5},{7,4},{8,11},{9,10},{10,... | collective-permute-start | bytes 6152 | tf_op jit(solution)/shard_map/ppermute | solution.py:388
  8.7 8.8 %collective-permute-start.3 = (f32[1,104,128]{2,1,0:T(8,128)S(1)}, f32[1,104,128]{2,1,0:T(8,128)S(1)}, u32[]{:S(2)}, u32[]{:S(2)}) collective-permute-start(f32[1,104,128]{2,1,0:T(8,128)S(1)} %get-tuple-element.90), channel_id=1, source_target_pairs={{0,8},{4,12},{8,0},{12,4},{16,24},{20,28},{24,16},{28,20},{1,9},{5... | collective-permute-start | bytes 159752 | tf_op jit(solution)/shard_map/ppermute | solution.py:388
  10.5 7.0 %collective-permute-start.4 = (f32[1,104,128]{2,1,0:T(8,128)S(1)}, f32[1,104,128]{2,1,0:T(8,128)S(1)}, u32[]{:S(2)}, u32[]{:S(2)}) collective-permute-start(f32[1,104,128]{2,1,0:T(8,128)S(1)} %get-tuple-element.90), channel_id=1, source_target_pairs={{0,16},{4,20},{8,24},{12,28},{16,0},{20,4},{24,8},{28,12},{1,17},{... | collective-permute-start | bytes 159752 | tf_op jit(solution)/shard_map/ppermute | solution.py:388
  13.1 4.5 %collective-permute-start.5 = (f32[1,104,128]{2,1,0:T(8,128)S(1)}, f32[1,104,128]{2,1,0:T(8,128)S(1)}, u32[]{:S(2)}, u32[]{:S(2)}) collective-permute-start(f32[1,104,128]{2,1,0:T(8,128)S(1)} %get-tuple-element.90), channel_id=1, source_target_pairs={{0,4},{4,0},{8,12},{12,8},{16,20},{20,16},{24,28},{28,24},{1,5},{5... | collective-permute-start | bytes 159752 | tf_op jit(solution)/shard_map/ppermute | solution.py:388
  29.6 3.3 %collective-permute-start.6 = (f32[4,128]{1,0:T(4,128)S(1)}, f32[4,128]{1,0:T(4,128)S(1)}, u32[]{:S(2)}, u32[]{:S(2)}) collective-permute-start(f32[4,128]{1,0:T(4,128)S(1)} %shard_map.78), channel_id=1, source_target_pairs={{0,1},{1,0},{2,3},{3,2},{4,5},{5,4},{6,7},{7,6},{8,9},{9,8},{10,11... | collective-permute-start | bytes 6152 | tf_op jit(solution)/shard_map/ppermute | solution.py:388
  29.7 3.7 %collective-permute-start.7 = (f32[4,128]{1,0:T(4,128)S(1)}, f32[4,128]{1,0:T(4,128)S(1)}, u32[]{:S(2)}, u32[]{:S(2)}) collective-permute-start(f32[4,128]{1,0:T(4,128)S(1)} %shard_map.78), channel_id=1, source_target_pairs={{0,2},{1,3},{2,0},{3,1},{4,6},{5,7},{6,4},{7,5},{8,10},{9,11},{10,... | collective-permute-start | bytes 6152 | tf_op jit(solution)/shard_map/ppermute | solution.py:388
  31.2 3.0 %collective-permute-start.8 = (f32[4,128]{1,0:T(4,128)S(1)}, f32[4,128]{1,0:T(4,128)S(1)}, u32[]{:S(2)}, u32[]{:S(2)}) collective-permute-start(f32[4,128]{1,0:T(4,128)S(1)} %shard_map.78), channel_id=1, source_target_pairs={{0,3},{1,2},{2,1},{3,0},{4,7},{5,6},{6,5},{7,4},{8,11},{9,10},{10,... | collective-permute-start | bytes 6152 | tf_op jit(solution)/shard_map/ppermute | solution.py:388
  31.5 4.8 %collective-permute-start.10 = (f32[1,104,128]{2,1,0:T(8,128)S(1)}, f32[1,104,128]{2,1,0:T(8,128)S(1)}, u32[]{:S(2)}, u32[]{:S(2)}) collective-permute-start(f32[1,104,128]{2,1,0:T(8,128)S(1)} %collective-permute-done.3), channel_id=1, source_target_pairs={{0,4},{4,0},{8,12},{12,8},{16,20},{20,16},{24,28},{28,24},{1,5},{5... | collective-permute-start | bytes 159752 | tf_op jit(solution)/shard_map/ppermute | solution.py:388
  31.8 4.6 %collective-permute-start.11 = (f32[1,104,128]{2,1,0:T(8,128)S(1)}, f32[1,104,128]{2,1,0:T(8,128)S(1)}, u32[]{:S(2)}, u32[]{:S(2)}) collective-permute-start(f32[1,104,128]{2,1,0:T(8,128)S(1)} %collective-permute-done.4), channel_id=1, source_target_pairs={{0,8},{4,12},{8,0},{12,4},{16,24},{20,28},{24,16},{28,20},{1,9},{5... | collective-permute-start | bytes 159752 | tf_op jit(solution)/shard_map/ppermute | solution.py:388
  32.9 2.5 %collective-permute-start.9 = (f32[4,104,128]{2,1,0:T(8,128)S(1)}, f32[4,104,128]{2,1,0:T(8,128)S(1)}, u32[]{:S(2)}, u32[]{:S(2)}) collective-permute-start(f32[4,104,128]{2,1,0:T(8,128)S(1)} %constant_dynamic-update-slice_fusion.mine_ref), channel_id=1, source_target_pairs={{0,1},{1,0},{2,3},{3,2},{4,5},{5,4},{6,7},{7,6},{8,9},{9,8},{10,11... | collective-permute-start | bytes 638984 | tf_op jit(solution)/shard_map/ppermute | solution.py:388
  47.5 2.4 %collective-permute-start.12 = (f32[4,128]{1,0:T(4,128)S(1)}, f32[4,128]{1,0:T(4,128)S(1)}, u32[]{:S(2)}, u32[]{:S(2)}) collective-permute-start(f32[4,128]{1,0:T(4,128)S(1)} %shard_map.81), channel_id=1, source_target_pairs={{0,1},{1,0},{2,3},{3,2},{4,5},{5,4},{6,7},{7,6},{8,9},{9,8},{10,11... | collective-permute-start | bytes 6152 | tf_op jit(solution)/shard_map/ppermute | solution.py:388
  47.6 4.0 %collective-permute-start.13 = (f32[4,128]{1,0:T(4,128)S(1)}, f32[4,128]{1,0:T(4,128)S(1)}, u32[]{:S(2)}, u32[]{:S(2)}) collective-permute-start(f32[4,128]{1,0:T(4,128)S(1)} %shard_map.81), channel_id=1, source_target_pairs={{0,2},{1,3},{2,0},{3,1},{4,6},{5,7},{6,4},{7,5},{8,10},{9,11},{10,... | collective-permute-start | bytes 6152 | tf_op jit(solution)/shard_map/ppermute | solution.py:388
  48.9 3.0 %collective-permute-start.14 = (f32[4,128]{1,0:T(4,128)S(1)}, f32[4,128]{1,0:T(4,128)S(1)}, u32[]{:S(2)}, u32[]{:S(2)}) collective-permute-start(f32[4,128]{1,0:T(4,128)S(1)} %shard_map.81), channel_id=1, source_target_pairs={{0,3},{1,2},{2,1},{3,0},{4,7},{5,6},{6,5},{7,4},{8,11},{9,10},{10,... | collective-permute-start | bytes 6152 | tf_op jit(solution)/shard_map/ppermute | solution.py:388
  49.4 5.2 %collective-permute-start.17 = (f32[1,104,128]{2,1,0:T(8,128)S(1)}, f32[1,104,128]{2,1,0:T(8,128)S(1)}, u32[]{:S(2)}, u32[]{:S(2)}) collective-permute-start(f32[1,104,128]{2,1,0:T(8,128)S(1)} %collective-permute-done.11), channel_id=1, source_target_pairs={{0,4},{4,0},{8,12},{12,8},{16,20},{20,16},{24,28},{28,24},{1,5},{5... | collective-permute-start | bytes 159752 | tf_op jit(solution)/shard_map/ppermute | solution.py:388
  49.7 4.0 %collective-permute-start.15 = (f32[2,104,128]{2,1,0:T(8,128)S(1)}, f32[2,104,128]{2,1,0:T(8,128)S(1)}, u32[]{:S(2)}, u32[]{:S(2)}) collective-permute-start(f32[2,104,128]{2,1,0:T(8,128)S(1)} %constant_dynamic-update-slice_fusion.4.mine_ref), channel_id=1, source_target_pairs={{0,1},{1,0},{2,3},{3,2},{4,5},{5,4},{6,7},{7,6},{8,9},{9,8},{10,11... | collective-permute-start | bytes 319496 | tf_op jit(solution)/shard_map/ppermute | solution.py:388
  49.9 4.8 %collective-permute-start.16 = (f32[1,104,128]{2,1,0:T(8,128)S(1)}, f32[1,104,128]{2,1,0:T(8,128)S(1)}, u32[]{:S(2)}, u32[]{:S(2)}) collective-permute-start(f32[1,104,128]{2,1,0:T(8,128)S(1)} %collective-permute-done.4), channel_id=1, source_target_pairs={{0,4},{4,0},{8,12},{12,8},{16,20},{20,16},{24,28},{28,24},{1,5},{5... | collective-permute-start | bytes 159752 | tf_op jit(solution)/shard_map/ppermute | solution.py:388
  65.7 2.3 %collective-permute-start.18 = (f32[2,104,128]{2,1,0:T(8,128)S(1)}, f32[2,104,128]{2,1,0:T(8,128)S(1)}, u32[]{:S(2)}, u32[]{:S(2)}) collective-permute-start(f32[2,104,128]{2,1,0:T(8,128)S(1)} %constant_dynamic-update-slice_fusion.6.mine_ref), channel_id=1, source_target_pairs={{0,1},{1,0},{2,3},{3,2},{4,5},{5,4},{6,7},{7,6},{8,9},{9,8},{10,11... | collective-permute-start | bytes 319496 | tf_op jit(solution)/shard_map/ppermute | solution.py:388
  65.8 3.7 %collective-permute-start.20 = (f32[4,128]{1,0:T(4,128)S(1)}, f32[4,128]{1,0:T(4,128)S(1)}, u32[]{:S(2)}, u32[]{:S(2)}) collective-permute-start(f32[4,128]{1,0:T(4,128)S(1)} %shard_map.85), channel_id=1, source_target_pairs={{0,2},{1,3},{2,0},{3,1},{4,6},{5,7},{6,4},{7,5},{8,10},{9,11},{10,... | collective-permute-start | bytes 6152 | tf_op jit(solution)/shard_map/ppermute | solution.py:388
  67.0 2.5 %collective-permute-start.19 = (f32[4,128]{1,0:T(4,128)S(1)}, f32[4,128]{1,0:T(4,128)S(1)}, u32[]{:S(2)}, u32[]{:S(2)}) collective-permute-start(f32[4,128]{1,0:T(4,128)S(1)} %shard_map.85), channel_id=1, source_target_pairs={{0,1},{1,0},{2,3},{3,2},{4,5},{5,4},{6,7},{7,6},{8,9},{9,8},{10,11... | collective-permute-start | bytes 6152 | tf_op jit(solution)/shard_map/ppermute | solution.py:388
  67.1 3.0 %collective-permute-start.21 = (f32[4,128]{1,0:T(4,128)S(1)}, f32[4,128]{1,0:T(4,128)S(1)}, u32[]{:S(2)}, u32[]{:S(2)}) collective-permute-start(f32[4,128]{1,0:T(4,128)S(1)} %shard_map.85), channel_id=1, source_target_pairs={{0,3},{1,2},{2,1},{3,0},{4,7},{5,6},{6,5},{7,4},{8,11},{9,10},{10,... | collective-permute-start | bytes 6152 | tf_op jit(solution)/shard_map/ppermute | solution.py:388

commit v6 on v5

--- a/solution.py
+++ b/solution.py
@@ -81,6 +81,7 @@
     rows, cols = score_ref.shape
     group = 16
     tall = 4
+    written_out = kernel_ref is not None
 
     for first in range(0, cols // LANES, group):
         lanes = [slice((first + k) * LANES, (first + k + 1) * LANES) for k in range(group)]
@@ -93,7 +94,7 @@
             return tops
 
         start = (jnp.full((8, LANES), -jnp.inf, jnp.float32),) * group
-        tops = lax.fori_loop(0, rows // (8 * tall), peaks, start)
+        tops = lax.fori_loop(0, rows // (8 * tall), peaks, start, unroll=written_out)
         tops = [jnp.max(t, axis=0, keepdims=True) - SHIFT for t in tops]
         wide_tops = [jnp.broadcast_to(t, (8, LANES)) for t in tops]
 
@@ -109,7 +110,7 @@
             return sums
 
         start = (jnp.zeros((8, LANES), jnp.float32),) * group
-        sums = lax.fori_loop(0, rows // (8 * tall), totals, start)
+        sums = lax.fori_loop(0, rows // (8 * tall), totals, start, unroll=written_out)
         for k, (t, u) in enumerate(zip(tops, sums)):
             spot = slice(first + k, first + k + 1)
             if top_ref is not None:
@@ -261,7 +262,7 @@
             total_ref[s, :] = u
         return 0
 
-    lax.fori_loop(0, rows // (8 * tall), block, 0)
+    lax.fori_loop(0, rows // (8 * tall), block, 0, unroll=True)
     for k in range(out_ref.shape[0]):
         out_ref[k : k + 1, :] = jnp.sum(total_ref[k * LANES : (k + 1) * LANES, :].T, axis=0, keepdims=True)
 
@@ -278,7 +279,8 @@
             sums = tuple(u + kernel_ref[here, s] * factor for u, s in zip(sums, lanes))
         return sums
 
-    sums = lax.fori_loop(0, rows // (8 * tall), block, (jnp.zeros((8, LANES), jnp.float32),) * len(lanes))
+    start = (jnp.zeros((8, LANES), jnp.float32),) * len(lanes)
+    sums = lax.fori_loop(0, rows // (8 * tall), block, start, unroll=True)
     for k, u in enumerate(sums):
         out_ref[k : k + 1, :] = jnp.sum(u, axis=0, keepdims=True)
 
@@ -421,7 +423,7 @@
         self.coming = {}
         if len(bits) >= 3:
             z, w, x = bits[:3]
-            self.fetches = [[(0, z), (0, w), (0, x)], [(z, x), (w, z)], [(w, x), (w ^ z, x)], []]
+            self.fetches = [[(0, w), (0, z), (0, x)], [(z, x), (w, z)], [(w, x), (w ^ z, x)], []]
             self.groups = [[], [0, z, w, x], [z ^ x, w ^ z], [w ^ x, w ^ z ^ x]]
             self.bits = bits[3:]
         else:

time: 85.4 us -> 83.9 us (0.982)
  Pallas kernels: 20 us -> 17.9 us
    pallas_call x12, Pallas kernels: 15.8 us -> 13.7 us  [call(): pl.pallas_call(kernel, out_shape=[buffer(pltpu.VMEM if pin else jax.Shape...]
  transfers between devices with their start and end apart: 22 -> 22, of which waited for: 6 -> 6; matrix products, arithmetic and copies ran while one was open for 0% -> 0% of each run, Pallas kernels for 10% -> 9%
where the time goes in v6:
time: 83.9 us; the launch traced here: 83.6 us
  blocking collectives  41.5 us (49%)
  starting transfers between devices  18.7 us (22%)
  Pallas kernels  17.9 us (21%)
  waiting for transfers between devices  3.87 us (5%)
  between operations  1.57 us (2%)
    all_to_all x3, blocking collectives, shards(): lax.all_to_all(jnp.broadcast_to(lse, (n_src, *by_col)), 'src', 0, 0, tile...  30.8 us
    ppermute x22, starting transfers between devices, swap(): lax.ppermute(value, axis, [(i, i ^ step) for i in range(lax.axis_size(axi...  18.7 us
    pallas_call x12, Pallas kernels, call(): pl.pallas_call(kernel, out_shape=[buffer(pltpu.VMEM if pin else jax.Shape...  13.7 us
    all_to_all x1, blocking collectives, shards(): lax.all_to_all(jnp.broadcast_to(both, (n_src, *both.shape)), 'src', 0, 0,...  10.7 us
    pallas_call x1, Pallas kernels, shards(): pl.pallas_call(first_kernel, out_shape=[pltpu.VMEM(shape, jnp.float32) fo...  4.23 us
    ppermute x22, waiting for transfers between devices, swap(): lax.ppermute(value, axis, [(i, i ^ step) for i in range(lax.axis_size(axi...  3.87 us
  transfers between devices with their start and end apart: 22, of which 6 were waited for; matrix products, arithmetic and copies ran while one was open for 0% of the time, Pallas kernels for 9%

profile of v6, /device:TPU:0, one launch (start us, length us, event | category | flops | bytes accessed | tf_op | source)
XLA Modules:
  0.0 83.6 jit_solution(11886996371218578687)
XLA Ops:
  1.3 4.2 %shard_map.76 = (f32[512,4096]{1,0:T(8,128)S(1)}, f32[4,128]{1,0:T(4,128)S(1)}, f32[3,4,128]{2,1,0:T(4,128)S(1)}, f32[3,32,128]{2,1,0:T(8,128)S(1)}, f32[64,512]{1,0:T(8,128)S(1)}, /*index=5*/f32[1,104,128]{2,1,0:T(8,128)S(1)}) custom-call(f32[50,512]{1,0:T(8,128)} %src_hbm.1, f32[50,4096]{1,0:T(8,128)} %tgt_hbm.1, s32[8]{0:T(128)} %count_src_hbm.1, ...), custom_call_target="tpu_custom_call" | custom-call | flops 1610612736 | tf_op jit(solution)/shard_map/pallas_call | solution.py:519
  5.5 0.5 collective-permute-start
  6.0 2.6 %collective-permute-start.1 = (f32[4,128]{1,0:T(4,128)S(1)}, f32[4,128]{1,0:T(4,128)S(1)}, u32[]{:S(2)}, u32[]{:S(2)}) collective-permute-start(f32[4,128]{1,0:T(4,128)S(1)} %get-tuple-element.73), channel_id=1, source_target_pairs={{0,2},{1,3},{2,0},{3,1},{4,6},{5,7},{6,4},{7,5},{8,10},{9,11},{10,... | collective-permute-start | bytes 6152 | tf_op jit(solution)/shard_map/ppermute | solution.py:390
  8.7 2.8 %collective-permute-start.3 = (f32[1,104,128]{2,1,0:T(8,128)S(1)}, f32[1,104,128]{2,1,0:T(8,128)S(1)}, u32[]{:S(2)}, u32[]{:S(2)}) collective-permute-start(f32[1,104,128]{2,1,0:T(8,128)S(1)} %get-tuple-element.90), channel_id=1, source_target_pairs={{0,16},{4,20},{8,24},{12,28},{16,0},{20,4},{24,8},{28,12},{1,17},{... | collective-permute-start | bytes 159752 | tf_op jit(solution)/shard_map/ppermute | solution.py:390
  11.5 1.6 %collective-permute-start.4 = (f32[1,104,128]{2,1,0:T(8,128)S(1)}, f32[1,104,128]{2,1,0:T(8,128)S(1)}, u32[]{:S(2)}, u32[]{:S(2)}) collective-permute-start(f32[1,104,128]{2,1,0:T(8,128)S(1)} %get-tuple-element.90), channel_id=1, source_target_pairs={{0,8},{4,12},{8,0},{12,4},{16,24},{20,28},{24,16},{28,20},{1,9},{5... | collective-permute-start | bytes 159752 | tf_op jit(solution)/shard_map/ppermute | solution.py:390
  13.1 1.5 %collective-permute-start.5 = (f32[1,104,128]{2,1,0:T(8,128)S(1)}, f32[1,104,128]{2,1,0:T(8,128)S(1)}, u32[]{:S(2)}, u32[]{:S(2)}) collective-permute-start(f32[1,104,128]{2,1,0:T(8,128)S(1)} %get-tuple-element.90), channel_id=1, source_target_pairs={{0,4},{4,0},{8,12},{12,8},{16,20},{20,16},{24,28},{28,24},{1,5},{5... | collective-permute-start | bytes 159752 | tf_op jit(solution)/shard_map/ppermute | solution.py:390
  14.6 2.1 %shard_map.77 = (f32[32,128]{1,0:T(8,128)S(1)}, f32[4,128]{1,0:T(4,128)S(1)}, f32[512,4096]{1,0:T(8,128)S(1)}, f32[32,128]{1,0:T(8,128)S(1)}) custom-call(f32[512,4096]{1,0:T(8,128)S(1)} %get-tuple-element.72.score_ref, f32[4,128]{1,0:T(4,128)S(1)} %multiply_add_fusion.3.lse_ref, f32[3,4,128]{2,1,0:T(4,128)S(1)} %get-tuple-element.74.aux_ref.row_aux), custom_call_target="tpu_custom_call" | custom-call | tf_op jit(solution)/shard_map/pallas_call | solution.py:402
  17.2 10.7 %all_to_all.20.parts_ref = f32[8,32,128]{2,1,0:T(8,128)S(1)} all-to-all(f32[8,32,128]{2,1,0:T(8,128)S(1)} %broadcast_in_dim.12), channel_id=1, replica_groups=mesh['src'=8,'tgt'=4] {'src'}, dimensions={0} | all-to-all | bytes 262144 | tf_op jit(solution)/shard_map/all_to_all | solution.py:579
  27.9 0.8 shard_map.78
  28.8 1.6 %collective-permute-start.7 = (f32[4,128]{1,0:T(4,128)S(1)}, f32[4,128]{1,0:T(4,128)S(1)}, u32[]{:S(2)}, u32[]{:S(2)}) collective-permute-start(f32[4,128]{1,0:T(4,128)S(1)} %shard_map.78), channel_id=1, source_target_pairs={{0,2},{1,3},{2,0},{3,1},{4,6},{5,7},{6,4},{7,5},{8,10},{9,11},{10,... | collective-permute-start | bytes 6152 | tf_op jit(solution)/shard_map/ppermute | solution.py:390
  31.0 0.9 %collective-permute-start.11 = (f32[1,104,128]{2,1,0:T(8,128)S(1)}, f32[1,104,128]{2,1,0:T(8,128)S(1)}, u32[]{:S(2)}, u32[]{:S(2)}) collective-permute-start(f32[1,104,128]{2,1,0:T(8,128)S(1)} %collective-permute-done.3), channel_id=1, source_target_pairs={{0,8},{4,12},{8,0},{12,4},{16,24},{20,28},{24,16},{28,20},{1,9},{5... | collective-permute-start | bytes 159752 | tf_op jit(solution)/shard_map/ppermute | solution.py:390
  32.4 0.9 %collective-permute-done.8 = f32[4,128]{1,0:T(4,128)S(1)} collective-permute-done((f32[4,128]{1,0:T(4,128)S(1)}, f32[4,128]{1,0:T(4,128)S(1)}, u32[]{:S(2)}, u32[]{:S(2)}) %collective-permute-start.8) | collective-permute-done | bytes 2080 | tf_op jit(solution)/shard_map/ppermute | solution.py:390
  33.4 0.8 shard_map.79
  34.2 1.0 %shard_map.80 = (f32[512,1024]{1,0:T(8,128)S(1)}, bf16[1024,128]{1,0:T(8,128)(2,1)S(1)}, f32[8,128]{1,0:T(8,128)S(1)}, bf16[512,384]{1,0:T(8,128)(2,1)S(1)}, f32[512,128]{1,0:T(8,128)S(1)}) custom-call(f32[64,512]{1,0:T(8,128)S(1)} %get-tuple-element.116.own_ref, f32[4,104,128]{2,1,0:T(8,128)S(1)} %constant_dynamic-update-slice_fusion.mine_ref, ...), custom_call_target="tpu_custom_call" | custom-call | flops 402653184 | tf_op jit(solution)/shard_map/pallas_call | solution.py:402
  35.3 10.2 %all_to_all.21.parts_ref = f32[8,32,128]{2,1,0:T(8,128)S(1)} all-to-all(f32[8,32,128]{2,1,0:T(8,128)S(1)} %broadcast_in_dim.13), channel_id=1, replica_groups=mesh['src'=8,'tgt'=4] {'src'}, dimensions={0} | all-to-all | bytes 262144 | tf_op jit(solution)/shard_map/all_to_all | solution.py:579
  45.4 0.8 shard_map.81
  46.3 1.6 %collective-permute-start.13 = (f32[4,128]{1,0:T(4,128)S(1)}, f32[4,128]{1,0:T(4,128)S(1)}, u32[]{:S(2)}, u32[]{:S(2)}) collective-permute-start(f32[4,128]{1,0:T(4,128)S(1)} %shard_map.81), channel_id=1, source_target_pairs={{0,2},{1,3},{2,0},{3,1},{4,6},{5,7},{6,4},{7,5},{8,10},{9,11},{10,... | collective-permute-start | bytes 6152 | tf_op jit(solution)/shard_map/ppermute | solution.py:390
  48.6 1.7 %collective-permute-start.16 = (f32[1,104,128]{2,1,0:T(8,128)S(1)}, f32[1,104,128]{2,1,0:T(8,128)S(1)}, u32[]{:S(2)}, u32[]{:S(2)}) collective-permute-start(f32[1,104,128]{2,1,0:T(8,128)S(1)} %collective-permute-done.3), channel_id=1, source_target_pairs={{0,4},{4,0},{8,12},{12,8},{16,20},{20,16},{24,28},{28,24},{1,5},{5... | collective-permute-start | bytes 159752 | tf_op jit(solution)/shard_map/ppermute | solution.py:390
  50.3 0.6 collective-permute-done.14
  51.0 1.0 %shard_map.82 = f32[32,128]{1,0:T(8,128)S(1)} custom-call(f32[512,4096]{1,0:T(8,128)S(1)} %get-tuple-element.72.score_ref, f32[512,4096]{1,0:T(8,128)S(1)} %get-tuple-element.75.kernel_ref, f32[32,128]{1,0:T(8,128)S(1)} %get-tuple-element.76.top_ref, f32[4,128]{1,0:T(4,128)S(1)} %get-tuple-element.77.base_ref, f32[4,128]{1,0:T(4,128)S(1)} %multiply_add_fusion.1.lse_ref, ...), custom_call_target="tpu_custom_call" | custom-call | tf_op jit(solution)/shard_map/pallas_call | solution.py:402
  52.0 0.8 shard_map.83
  52.7 0.8 shard_map.84
  53.6 10.0 %all_to_all.22.parts_ref = f32[8,32,128]{2,1,0:T(8,128)S(1)} all-to-all(f32[8,32,128]{2,1,0:T(8,128)S(1)} %broadcast_in_dim.14), channel_id=1, replica_groups=mesh['src'=8,'tgt'=4] {'src'}, dimensions={0} | all-to-all | bytes 262144 | tf_op jit(solution)/shard_map/all_to_all | solution.py:579
  63.6 0.8 shard_map.85
  64.5 1.2 %collective-permute-start.20 = (f32[4,128]{1,0:T(4,128)S(1)}, f32[4,128]{1,0:T(4,128)S(1)}, u32[]{:S(2)}, u32[]{:S(2)}) collective-permute-start(f32[4,128]{1,0:T(4,128)S(1)} %shard_map.85), channel_id=1, source_target_pairs={{0,2},{1,3},{2,0},{3,1},{4,6},{5,7},{6,4},{7,5},{8,10},{9,11},{10,... | collective-permute-start | bytes 6152 | tf_op jit(solution)/shard_map/ppermute | solution.py:390
  65.9 0.8 collective-permute-start.21
  66.7 0.8 shard_map.86
  67.5 0.7 collective-permute-done.20
  68.1 0.7 collective-permute-done.21
  68.9 0.8 shard_map.87
  69.7 10.7 %all_to_all.23.refs_8_ = f32[8,36,128]{2,1,0:T(8,128)S(1)} all-to-all(f32[8,36,128]{2,1,0:T(8,128)S(1)} %broadcast_in_dim.15), channel_id=1, replica_groups=mesh['src'=8,'tgt'=4] {'src'}, dimensions={0} | all-to-all | bytes 294912 | tf_op jit(solution)/shard_map/all_to_all | solution.py:588
  80.4 3.2 %shard_map.88 = (f32[50,512]{1,0:T(8,128)}, f32[4,128]{1,0:T(4,128)}, f32[32,128]{1,0:T(8,128)}) custom-call(f32[512,1024]{1,0:T(8,128)S(1)} %get-tuple-element.94.refs_0_, f32[512,1024]{1,0:T(8,128)S(1)} %get-tuple-element.105.refs_1_, f32[512,1024]{1,0:T(8,128)S(1)} %get-tuple-element.108.refs_2_, f32[512,1024]{1,0:T(8,128)S(1)} %get-tuple-element.122.refs_3_, ...), custom_call_target="tpu_custom_call" | custom-call | flops 2415919104 | tf_op jit(solution)/shard_map/pallas_call | solution.py:402
  (46 shorter events, 3.0 us)
Async XLA Ops:
  5.5 7.6 %collective-permute-start = (f32[4,128]{1,0:T(4,128)S(1)}, f32[4,128]{1,0:T(4,128)S(1)}, u32[]{:S(2)}, u32[]{:S(2)}) collective-permute-start(f32[4,128]{1,0:T(4,128)S(1)} %get-tuple-element.73), channel_id=1, source_target_pairs={{0,1},{1,0},{2,3},{3,2},{4,5},{5,4},{6,7},{7,6},{8,9},{9,8},{10,11... | collective-permute-start | bytes 6152 | tf_op jit(solution)/shard_map/ppermute | solution.py:390
  6.0 8.5 %collective-permute-start.1 = (f32[4,128]{1,0:T(4,128)S(1)}, f32[4,128]{1,0:T(4,128)S(1)}, u32[]{:S(2)}, u32[]{:S(2)}) collective-permute-start(f32[4,128]{1,0:T(4,128)S(1)} %get-tuple-element.73), channel_id=1, source_target_pairs={{0,2},{1,3},{2,0},{3,1},{4,6},{5,7},{6,4},{7,5},{8,10},{9,11},{10,... | collective-permute-start | bytes 6152 | tf_op jit(solution)/shard_map/ppermute | solution.py:390
  8.6 5.9 %collective-permute-start.2 = (f32[4,128]{1,0:T(4,128)S(1)}, f32[4,128]{1,0:T(4,128)S(1)}, u32[]{:S(2)}, u32[]{:S(2)}) collective-permute-start(f32[4,128]{1,0:T(4,128)S(1)} %get-tuple-element.73), channel_id=1, source_target_pairs={{0,3},{1,2},{2,1},{3,0},{4,7},{5,6},{6,5},{7,4},{8,11},{9,10},{10,... | collective-permute-start | bytes 6152 | tf_op jit(solution)/shard_map/ppermute | solution.py:390
  8.7 8.0 %collective-permute-start.3 = (f32[1,104,128]{2,1,0:T(8,128)S(1)}, f32[1,104,128]{2,1,0:T(8,128)S(1)}, u32[]{:S(2)}, u32[]{:S(2)}) collective-permute-start(f32[1,104,128]{2,1,0:T(8,128)S(1)} %get-tuple-element.90), channel_id=1, source_target_pairs={{0,16},{4,20},{8,24},{12,28},{16,0},{20,4},{24,8},{28,12},{1,17},{... | collective-permute-start | bytes 159752 | tf_op jit(solution)/shard_map/ppermute | solution.py:390
  11.5 5.2 %collective-permute-start.4 = (f32[1,104,128]{2,1,0:T(8,128)S(1)}, f32[1,104,128]{2,1,0:T(8,128)S(1)}, u32[]{:S(2)}, u32[]{:S(2)}) collective-permute-start(f32[1,104,128]{2,1,0:T(8,128)S(1)} %get-tuple-element.90), channel_id=1, source_target_pairs={{0,8},{4,12},{8,0},{12,4},{16,24},{20,28},{24,16},{28,20},{1,9},{5... | collective-permute-start | bytes 159752 | tf_op jit(solution)/shard_map/ppermute | solution.py:390
  13.1 4.1 %collective-permute-start.5 = (f32[1,104,128]{2,1,0:T(8,128)S(1)}, f32[1,104,128]{2,1,0:T(8,128)S(1)}, u32[]{:S(2)}, u32[]{:S(2)}) collective-permute-start(f32[1,104,128]{2,1,0:T(8,128)S(1)} %get-tuple-element.90), channel_id=1, source_target_pairs={{0,4},{4,0},{8,12},{12,8},{16,20},{20,16},{24,28},{28,24},{1,5},{5... | collective-permute-start | bytes 159752 | tf_op jit(solution)/shard_map/ppermute | solution.py:390
  28.7 3.3 %collective-permute-start.6 = (f32[4,128]{1,0:T(4,128)S(1)}, f32[4,128]{1,0:T(4,128)S(1)}, u32[]{:S(2)}, u32[]{:S(2)}) collective-permute-start(f32[4,128]{1,0:T(4,128)S(1)} %shard_map.78), channel_id=1, source_target_pairs={{0,1},{1,0},{2,3},{3,2},{4,5},{5,4},{6,7},{7,6},{8,9},{9,8},{10,11... | collective-permute-start | bytes 6152 | tf_op jit(solution)/shard_map/ppermute | solution.py:390
  28.8 3.7 %collective-permute-start.7 = (f32[4,128]{1,0:T(4,128)S(1)}, f32[4,128]{1,0:T(4,128)S(1)}, u32[]{:S(2)}, u32[]{:S(2)}) collective-permute-start(f32[4,128]{1,0:T(4,128)S(1)} %shard_map.78), channel_id=1, source_target_pairs={{0,2},{1,3},{2,0},{3,1},{4,6},{5,7},{6,4},{7,5},{8,10},{9,11},{10,... | collective-permute-start | bytes 6152 | tf_op jit(solution)/shard_map/ppermute | solution.py:390
  30.4 3.0 %collective-permute-start.8 = (f32[4,128]{1,0:T(4,128)S(1)}, f32[4,128]{1,0:T(4,128)S(1)}, u32[]{:S(2)}, u32[]{:S(2)}) collective-permute-start(f32[4,128]{1,0:T(4,128)S(1)} %shard_map.78), channel_id=1, source_target_pairs={{0,3},{1,2},{2,1},{3,0},{4,7},{5,6},{6,5},{7,4},{8,11},{9,10},{10,... | collective-permute-start | bytes 6152 | tf_op jit(solution)/shard_map/ppermute | solution.py:390
  30.6 4.6 %collective-permute-start.10 = (f32[1,104,128]{2,1,0:T(8,128)S(1)}, f32[1,104,128]{2,1,0:T(8,128)S(1)}, u32[]{:S(2)}, u32[]{:S(2)}) collective-permute-start(f32[1,104,128]{2,1,0:T(8,128)S(1)} %collective-permute-done.4), channel_id=1, source_target_pairs={{0,4},{4,0},{8,12},{12,8},{16,20},{20,16},{24,28},{28,24},{1,5},{5... | collective-permute-start | bytes 159752 | tf_op jit(solution)/shard_map/ppermute | solution.py:390
  31.0 4.2 %collective-permute-start.11 = (f32[1,104,128]{2,1,0:T(8,128)S(1)}, f32[1,104,128]{2,1,0:T(8,128)S(1)}, u32[]{:S(2)}, u32[]{:S(2)}) collective-permute-start(f32[1,104,128]{2,1,0:T(8,128)S(1)} %collective-permute-done.3), channel_id=1, source_target_pairs={{0,8},{4,12},{8,0},{12,4},{16,24},{20,28},{24,16},{28,20},{1,9},{5... | collective-permute-start | bytes 159752 | tf_op jit(solution)/shard_map/ppermute | solution.py:390
  32.0 2.2 %collective-permute-start.9 = (f32[4,104,128]{2,1,0:T(8,128)S(1)}, f32[4,104,128]{2,1,0:T(8,128)S(1)}, u32[]{:S(2)}, u32[]{:S(2)}) collective-permute-start(f32[4,104,128]{2,1,0:T(8,128)S(1)} %constant_dynamic-update-slice_fusion.mine_ref), channel_id=1, source_target_pairs={{0,1},{1,0},{2,3},{3,2},{4,5},{5,4},{6,7},{7,6},{8,9},{9,8},{10,11... | collective-permute-start | bytes 638984 | tf_op jit(solution)/shard_map/ppermute | solution.py:390
  46.3 2.4 %collective-permute-start.12 = (f32[4,128]{1,0:T(4,128)S(1)}, f32[4,128]{1,0:T(4,128)S(1)}, u32[]{:S(2)}, u32[]{:S(2)}) collective-permute-start(f32[4,128]{1,0:T(4,128)S(1)} %shard_map.81), channel_id=1, source_target_pairs={{0,1},{1,0},{2,3},{3,2},{4,5},{5,4},{6,7},{7,6},{8,9},{9,8},{10,11... | collective-permute-start | bytes 6152 | tf_op jit(solution)/shard_map/ppermute | solution.py:390
  46.3 4.0 %collective-permute-start.13 = (f32[4,128]{1,0:T(4,128)S(1)}, f32[4,128]{1,0:T(4,128)S(1)}, u32[]{:S(2)}, u32[]{:S(2)}) collective-permute-start(f32[4,128]{1,0:T(4,128)S(1)} %shard_map.81), channel_id=1, source_target_pairs={{0,2},{1,3},{2,0},{3,1},{4,6},{5,7},{6,4},{7,5},{8,10},{9,11},{10,... | collective-permute-start | bytes 6152 | tf_op jit(solution)/shard_map/ppermute | solution.py:390
  47.9 3.0 %collective-permute-start.14 = (f32[4,128]{1,0:T(4,128)S(1)}, f32[4,128]{1,0:T(4,128)S(1)}, u32[]{:S(2)}, u32[]{:S(2)}) collective-permute-start(f32[4,128]{1,0:T(4,128)S(1)} %shard_map.81), channel_id=1, source_target_pairs={{0,3},{1,2},{2,1},{3,0},{4,7},{5,6},{6,5},{7,4},{8,11},{9,10},{10,... | collective-permute-start | bytes 6152 | tf_op jit(solution)/shard_map/ppermute | solution.py:390
  48.2 5.3 %collective-permute-start.17 = (f32[1,104,128]{2,1,0:T(8,128)S(1)}, f32[1,104,128]{2,1,0:T(8,128)S(1)}, u32[]{:S(2)}, u32[]{:S(2)}) collective-permute-start(f32[1,104,128]{2,1,0:T(8,128)S(1)} %collective-permute-done.11), channel_id=1, source_target_pairs={{0,4},{4,0},{8,12},{12,8},{16,20},{20,16},{24,28},{28,24},{1,5},{5... | collective-permute-start | bytes 159752 | tf_op jit(solution)/shard_map/ppermute | solution.py:390
  48.6 4.2 %collective-permute-start.15 = (f32[2,104,128]{2,1,0:T(8,128)S(1)}, f32[2,104,128]{2,1,0:T(8,128)S(1)}, u32[]{:S(2)}, u32[]{:S(2)}) collective-permute-start(f32[2,104,128]{2,1,0:T(8,128)S(1)} %constant_dynamic-update-slice_fusion.4.mine_ref), channel_id=1, source_target_pairs={{0,1},{1,0},{2,3},{3,2},{4,5},{5,4},{6,7},{7,6},{8,9},{9,8},{10,11... | collective-permute-start | bytes 319496 | tf_op jit(solution)/shard_map/ppermute | solution.py:390
  48.6 4.9 %collective-permute-start.16 = (f32[1,104,128]{2,1,0:T(8,128)S(1)}, f32[1,104,128]{2,1,0:T(8,128)S(1)}, u32[]{:S(2)}, u32[]{:S(2)}) collective-permute-start(f32[1,104,128]{2,1,0:T(8,128)S(1)} %collective-permute-done.3), channel_id=1, source_target_pairs={{0,4},{4,0},{8,12},{12,8},{16,20},{20,16},{24,28},{28,24},{1,5},{5... | collective-permute-start | bytes 159752 | tf_op jit(solution)/shard_map/ppermute | solution.py:390
  64.4 2.3 %collective-permute-start.18 = (f32[2,104,128]{2,1,0:T(8,128)S(1)}, f32[2,104,128]{2,1,0:T(8,128)S(1)}, u32[]{:S(2)}, u32[]{:S(2)}) collective-permute-start(f32[2,104,128]{2,1,0:T(8,128)S(1)} %constant_dynamic-update-slice_fusion.6.mine_ref), channel_id=1, source_target_pairs={{0,1},{1,0},{2,3},{3,2},{4,5},{5,4},{6,7},{7,6},{8,9},{9,8},{10,11... | collective-permute-start | bytes 319496 | tf_op jit(solution)/shard_map/ppermute | solution.py:390
  64.5 3.7 %collective-permute-start.20 = (f32[4,128]{1,0:T(4,128)S(1)}, f32[4,128]{1,0:T(4,128)S(1)}, u32[]{:S(2)}, u32[]{:S(2)}) collective-permute-start(f32[4,128]{1,0:T(4,128)S(1)} %shard_map.85), channel_id=1, source_target_pairs={{0,2},{1,3},{2,0},{3,1},{4,6},{5,7},{6,4},{7,5},{8,10},{9,11},{10,... | collective-permute-start | bytes 6152 | tf_op jit(solution)/shard_map/ppermute | solution.py:390
  65.7 2.4 %collective-permute-start.19 = (f32[4,128]{1,0:T(4,128)S(1)}, f32[4,128]{1,0:T(4,128)S(1)}, u32[]{:S(2)}, u32[]{:S(2)}) collective-permute-start(f32[4,128]{1,0:T(4,128)S(1)} %shard_map.85), channel_id=1, source_target_pairs={{0,1},{1,0},{2,3},{3,2},{4,5},{5,4},{6,7},{7,6},{8,9},{9,8},{10,11... | collective-permute-start | bytes 6152 | tf_op jit(solution)/shard_map/ppermute | solution.py:390
  65.9 3.0 %collective-permute-start.21 = (f32[4,128]{1,0:T(4,128)S(1)}, f32[4,128]{1,0:T(4,128)S(1)}, u32[]{:S(2)}, u32[]{:S(2)}) collective-permute-start(f32[4,128]{1,0:T(4,128)S(1)} %shard_map.85), channel_id=1, source_target_pairs={{0,3},{1,2},{2,1},{3,0},{4,7},{5,6},{6,5},{7,4},{8,11},{9,10},{10,... | collective-permute-start | bytes 6152 | tf_op jit(solution)/shard_map/ppermute | solution.py:390

commit v7 on v6

--- a/solution.py
+++ b/solution.py
@@ -297,14 +297,26 @@
     masked_ref[...] = jnp.where(aux_ref[2] > 0, f, NEG)
 
 
-def first_col_kernel(score_ref, lse_ref, aux_ref, out_ref, f_ref, kernel_ref, top_ref, masked_ref, col_ref):
+def spread(lse, send_ref, masked=None):
+    n_col = lse.shape[0]
+    for k in range(send_ref.shape[0]):
+        send_ref[k, 0:n_col, :] = lse
+        if masked is not None:
+            send_ref[k, n_col:, :] = masked
+
+
+def first_col_kernel(
+    score_ref, lse_ref, aux_ref, send_ref, f_ref, kernel_ref, top_ref, out_ref, masked_ref, col_ref
+):
     set_f(lse_ref, aux_ref, f_ref, masked_ref)
     to_sublanes(f_ref, col_ref)
     col_lse(score_ref, col_ref, out_ref, kernel_ref, top_ref)
+    spread(out_ref[...], send_ref)
 
 
 def col_kernel(
-    score_ref, kernel_ref, top_ref, base_ref, lse_ref, aux_ref, out_ref, f_ref, masked_ref, factor_ref, col_ref
+    score_ref, kernel_ref, top_ref, base_ref, lse_ref, aux_ref, send_ref, f_ref, out_ref, masked_ref, factor_ref,
+    col_ref, *, last,
 ):
     set_f(lse_ref, aux_ref, f_ref, masked_ref)
     factor_ref[...] = jnp.exp2(f_ref[...] - base_ref[...])
@@ -313,12 +325,14 @@
     total = out_ref[...]
     top = top_ref[...]
     redo = out_of_range(total, top > 0.5 * NEG, factor_ref[...], ROW_FACTOR_MAX)
-    out_ref[...] = jnp.where(total > 0, top + jnp.log2(total), NEG)
+    masked = masked_ref[...] if last else None
+    spread(jnp.where(total > 0, top + jnp.log2(total), NEG), send_ref, masked)
 
     @pl.when(redo)
     def _():
         to_sublanes(f_ref, col_ref)
         col_lse(score_ref, col_ref, out_ref)
+        spread(out_ref[...], send_ref, masked)
 
 
 def merged(parts):
@@ -465,6 +479,8 @@
             value, *held = tie(value, *self.coming.values())
             self.blocks.update(zip(self.coming, held))
             self.coming = {}
+        if self.theirs:
+            value, self.theirs[-1] = tie(value, self.theirs[-1])
         return value
 
     def piece(self):
@@ -557,26 +573,30 @@
             lse = side.hold(lse)
         others = side.start(step, lse, exchange)
         if step == ITERS - 1:
-            others[0] = side.pieces(others[0], 1)
+            others[0] = side.pieces(others[0], len(side.todo))
         lse = combine(lse, others)
         for bit in over_tgt[2:]:
             lse = merge(lse, swap(lse, "tgt", bit))
         if step == 0:
             lse, base, kernel, top = call(
                 first_col_kernel,
-                [by_col, by_row, (rows, cols), by_col],
-                [by_row, column], [score, lse, row_aux], 0,
+                [(n_src, *by_col), by_row, (rows, cols), by_col],
+                [by_col, by_row, column], [score, lse, row_aux], 0,
             )
         else:
             last = step == ITERS - 1
-            outs = [by_col, by_row, by_row] if last else [by_col]
-            scratch = [by_row, column] if last else [by_row, by_row, by_row, column]
-            lse, *held = call(col_kernel, outs, scratch, [score, kernel, top, base, lse, row_aux], 0)
+            extra = by_row[0] if last else 0
+            lse, *held = call(
+                functools.partial(col_kernel, last=last),
+                [(n_src, by_col[0] + extra, LANES)] + [by_row] * last,
+                [by_row] * (not last) + [by_col, by_row, by_row, column],
+                [score, kernel, top, base, lse, row_aux], 0,
+            )
             if last:
-                f, masked = held
+                (f,) = held
         if step < ITERS - 1:
-            lse = side.land(side.pieces(side.hold(lse), step))
-            lse = lax.all_to_all(jnp.broadcast_to(lse, (n_src, *by_col)), "src", 0, 0, tiled=True)
+            lse = side.land(side.pieces(side.hold(lse), min(step, 1)))
+            lse = lax.all_to_all(lse, "src", 0, 0, tiled=True)
             (lse,) = call(
                 row_kernel,
                 [by_row],
@@ -584,8 +604,7 @@
                 [score, kernel, top, base, lse, row_aux, col_aux], 0,
             )
     lse = side.finish(lse)
-    both = jnp.concatenate([lse, masked], axis=0)
-    both = lax.all_to_all(jnp.broadcast_to(both, (n_src, *both.shape)), "src", 0, 0, tiled=True)
+    both = lax.all_to_all(lse, "src", 0, 0, tiled=True)
     ancestors, f, g = call(
         functools.partial(last_kernel, pieces=side.done),
         [(dims, share), by_row, by_col],

time: 83.9 us -> 83.6 us (level)
  transfers between devices with their start and end apart: 22 -> 22, of which waited for: 6 -> 9; matrix products, arithmetic and copies ran while one was open for 0% -> 0% of each run, Pallas kernels for 9% -> 9%
where the time goes in v7:
time: 83.6 us; the launch traced here: 83.3 us
  blocking collectives  40.9 us (49%)
  starting transfers between devices  19.4 us (23%)
  Pallas kernels  17.9 us (21%)
  waiting for transfers between devices  3.43 us (4%)
  between operations  1.49 us (2%)
    all_to_all x3, blocking collectives, shards(): lse = lax.all_to_all(lse, 'src', 0, 0, tiled=True)  30.4 us
    ppermute x22, starting transfers between devices, swap(): lax.ppermute(value, axis, [(i, i ^ step) for i in range(lax.axis_size(axi...  19.4 us
    pallas_call x12, Pallas kernels, call(): pl.pallas_call(kernel, out_shape=[buffer(pltpu.VMEM if pin else jax.Shape...  13.7 us
    all_to_all x1, blocking collectives, shards(): both = lax.all_to_all(lse, 'src', 0, 0, tiled=True)  10.5 us
    pallas_call x1, Pallas kernels, shards(): pl.pallas_call(first_kernel, out_shape=[pltpu.VMEM(shape, jnp.float32) fo...  4.23 us
    ppermute x22, waiting for transfers between devices, swap(): lax.ppermute(value, axis, [(i, i ^ step) for i in range(lax.axis_size(axi...  3.43 us
  transfers between devices with their start and end apart: 22, of which 9 were waited for; matrix products, arithmetic and copies ran while one was open for 0% of the time, Pallas kernels for 9%

profile of v7, /device:TPU:0, one launch (start us, length us, event | category | flops | bytes accessed | tf_op | source)
XLA Modules:
  0.0 83.3 jit_solution(7192361336708706622)
XLA Ops:
  1.3 4.2 %shard_map.76 = (f32[512,4096]{1,0:T(8,128)S(1)}, f32[4,128]{1,0:T(4,128)S(1)}, f32[3,4,128]{2,1,0:T(4,128)S(1)}, f32[3,32,128]{2,1,0:T(8,128)S(1)}, f32[64,512]{1,0:T(8,128)S(1)}, /*index=5*/f32[1,104,128]{2,1,0:T(8,128)S(1)}) custom-call(f32[50,512]{1,0:T(8,128)} %src_hbm.1, f32[50,4096]{1,0:T(8,128)} %tgt_hbm.1, s32[8]{0:T(128)} %count_src_hbm.1, ...), custom_call_target="tpu_custom_call" | custom-call | flops 1610612736 | tf_op jit(solution)/shard_map/pallas_call | solution.py:535
  5.5 3.0 %collective-permute-start.1 = (f32[4,128]{1,0:T(4,128)S(1)}, f32[4,128]{1,0:T(4,128)S(1)}, u32[]{:S(2)}, u32[]{:S(2)}) collective-permute-start(f32[4,128]{1,0:T(4,128)S(1)} %get-tuple-element.76), channel_id=1, source_target_pairs={{0,2},{1,3},{2,0},{3,1},{4,6},{5,7},{6,4},{7,5},{8,10},{9,11},{10,... | collective-permute-start | bytes 6152 | tf_op jit(solution)/shard_map/ppermute | solution.py:404
  8.7 3.0 %collective-permute-start.3 = (f32[1,104,128]{2,1,0:T(8,128)S(1)}, f32[1,104,128]{2,1,0:T(8,128)S(1)}, u32[]{:S(2)}, u32[]{:S(2)}) collective-permute-start(f32[1,104,128]{2,1,0:T(8,128)S(1)} %get-tuple-element.93), channel_id=1, source_target_pairs={{0,16},{4,20},{8,24},{12,28},{16,0},{20,4},{24,8},{28,12},{1,17},{... | collective-permute-start | bytes 159752 | tf_op jit(solution)/shard_map/ppermute | solution.py:404
  11.8 1.6 %collective-permute-start.4 = (f32[1,104,128]{2,1,0:T(8,128)S(1)}, f32[1,104,128]{2,1,0:T(8,128)S(1)}, u32[]{:S(2)}, u32[]{:S(2)}) collective-permute-start(f32[1,104,128]{2,1,0:T(8,128)S(1)} %get-tuple-element.93), channel_id=1, source_target_pairs={{0,8},{4,12},{8,0},{12,4},{16,24},{20,28},{24,16},{28,20},{1,9},{5... | collective-permute-start | bytes 159752 | tf_op jit(solution)/shard_map/ppermute | solution.py:404
  13.3 1.5 %collective-permute-start.5 = (f32[1,104,128]{2,1,0:T(8,128)S(1)}, f32[1,104,128]{2,1,0:T(8,128)S(1)}, u32[]{:S(2)}, u32[]{:S(2)}) collective-permute-start(f32[1,104,128]{2,1,0:T(8,128)S(1)} %get-tuple-element.93), channel_id=1, source_target_pairs={{0,4},{4,0},{8,12},{12,8},{16,20},{20,16},{24,28},{28,24},{1,5},{5... | collective-permute-start | bytes 159752 | tf_op jit(solution)/shard_map/ppermute | solution.py:404
  14.9 2.1 %shard_map.77 = (f32[8,32,128]{2,1,0:T(8,128)S(1)}, f32[4,128]{1,0:T(4,128)S(1)}, f32[512,4096]{1,0:T(8,128)S(1)}, f32[32,128]{1,0:T(8,128)S(1)}) custom-call(f32[512,4096]{1,0:T(8,128)S(1)} %get-tuple-element.75.score_ref, f32[4,128]{1,0:T(4,128)S(1)} %multiply_add_fusion.3.lse_ref, f32[3,4,128]{2,1,0:T(4,128)S(1)} %get-tuple-element.77.aux_ref.row_aux), custom_call_target="tpu_custom_call" | custom-call | tf_op jit(solution)/shard_map/pallas_call | solution.py:416
  17.0 0.5 collective-permute-done.5
  17.5 10.3 %all_to_all.20.parts_ref = f32[8,32,128]{2,1,0:T(8,128)S(1)} all-to-all(f32[8,32,128]{2,1,0:T(8,128)S(1)} %get-tuple-element.85), channel_id=1, replica_groups=mesh['src'=8,'tgt'=4] {'src'}, dimensions={0} | all-to-all | bytes 262144 | tf_op jit(solution)/shard_map/all_to_all | solution.py:599
  27.8 0.8 shard_map.78
  28.6 1.6 %collective-permute-start.7 = (f32[4,128]{1,0:T(4,128)S(1)}, f32[4,128]{1,0:T(4,128)S(1)}, u32[]{:S(2)}, u32[]{:S(2)}) collective-permute-start(f32[4,128]{1,0:T(4,128)S(1)} %shard_map.78), channel_id=1, source_target_pairs={{0,2},{1,3},{2,0},{3,1},{4,6},{5,7},{6,4},{7,5},{8,10},{9,11},{10,... | collective-permute-start | bytes 6152 | tf_op jit(solution)/shard_map/ppermute | solution.py:404
  30.2 0.6 collective-permute-start.6
  31.0 1.1 %collective-permute-start.11 = (f32[1,104,128]{2,1,0:T(8,128)S(1)}, f32[1,104,128]{2,1,0:T(8,128)S(1)}, u32[]{:S(2)}, u32[]{:S(2)}) collective-permute-start(f32[1,104,128]{2,1,0:T(8,128)S(1)} %collective-permute-done.3), channel_id=1, source_target_pairs={{0,8},{4,12},{8,0},{12,4},{16,24},{20,28},{24,16},{28,20},{1,9},{5... | collective-permute-start | bytes 159752 | tf_op jit(solution)/shard_map/ppermute | solution.py:404
  32.2 0.9 %collective-permute-done.8 = f32[4,128]{1,0:T(4,128)S(1)} collective-permute-done((f32[4,128]{1,0:T(4,128)S(1)}, f32[4,128]{1,0:T(4,128)S(1)}, u32[]{:S(2)}, u32[]{:S(2)}) %collective-permute-start.8) | collective-permute-done | bytes 2080 | tf_op jit(solution)/shard_map/ppermute | solution.py:404
  33.2 0.8 shard_map.79
  34.0 1.0 %shard_map.80 = (f32[512,1024]{1,0:T(8,128)S(1)}, bf16[1024,128]{1,0:T(8,128)(2,1)S(1)}, f32[8,128]{1,0:T(8,128)S(1)}, bf16[512,384]{1,0:T(8,128)(2,1)S(1)}, f32[512,128]{1,0:T(8,128)S(1)}) custom-call(f32[64,512]{1,0:T(8,128)S(1)} %get-tuple-element.119.own_ref, f32[4,104,128]{2,1,0:T(8,128)S(1)} %constant_dynamic-update-slice_fusion.mine_ref, ...), custom_call_target="tpu_custom_call" | custom-call | flops 402653184 | tf_op jit(solution)/shard_map/pallas_call | solution.py:416
  35.2 10.2 %all_to_all.21.parts_ref = f32[8,32,128]{2,1,0:T(8,128)S(1)} all-to-all(f32[8,32,128]{2,1,0:T(8,128)S(1)} %shard_map.79), channel_id=1, replica_groups=mesh['src'=8,'tgt'=4] {'src'}, dimensions={0} | all-to-all | bytes 262144 | tf_op jit(solution)/shard_map/all_to_all | solution.py:599
  45.4 0.8 shard_map.81
  46.2 1.6 %collective-permute-start.13 = (f32[4,128]{1,0:T(4,128)S(1)}, f32[4,128]{1,0:T(4,128)S(1)}, u32[]{:S(2)}, u32[]{:S(2)}) collective-permute-start(f32[4,128]{1,0:T(4,128)S(1)} %shard_map.81), channel_id=1, source_target_pairs={{0,2},{1,3},{2,0},{3,1},{4,6},{5,7},{6,4},{7,5},{8,10},{9,11},{10,... | collective-permute-start | bytes 6152 | tf_op jit(solution)/shard_map/ppermute | solution.py:404
  47.8 0.6 collective-permute-start.12
  48.8 1.7 %collective-permute-start.16 = (f32[1,104,128]{2,1,0:T(8,128)S(1)}, f32[1,104,128]{2,1,0:T(8,128)S(1)}, u32[]{:S(2)}, u32[]{:S(2)}) collective-permute-start(f32[1,104,128]{2,1,0:T(8,128)S(1)} %collective-permute-done.11), channel_id=1, source_target_pairs={{0,4},{4,0},{8,12},{12,8},{16,20},{20,16},{24,28},{28,24},{1,5},{5... | collective-permute-start | bytes 159752 | tf_op jit(solution)/shard_map/ppermute | solution.py:404
  50.8 1.0 %shard_map.82 = f32[8,32,128]{2,1,0:T(8,128)S(1)} custom-call(f32[512,4096]{1,0:T(8,128)S(1)} %get-tuple-element.75.score_ref, f32[512,4096]{1,0:T(8,128)S(1)} %get-tuple-element.78.kernel_ref, f32[32,128]{1,0:T(8,128)S(1)} %get-tuple-element.79.top_ref, f32[4,128]{1,0:T(4,128)S(1)} %get-tuple-element.80.base_ref, f32[4,128]{1,0:T(4,128)S(1)} %multiply_add_fusion.1.lse_ref, ...), custom_call_target="tpu_custom_call" | custom-call | tf_op jit(solution)/shard_map/pallas_call | solution.py:416
  51.8 0.8 shard_map.83
  52.7 0.6 collective-permute-done.16
  53.3 9.9 %all_to_all.22.parts_ref = f32[8,32,128]{2,1,0:T(8,128)S(1)} all-to-all(f32[8,32,128]{2,1,0:T(8,128)S(1)} %shard_map.82), channel_id=1, replica_groups=mesh['src'=8,'tgt'=4] {'src'}, dimensions={0} | all-to-all | bytes 262144 | tf_op jit(solution)/shard_map/all_to_all | solution.py:599
  63.2 0.8 shard_map.84
  64.1 1.6 %collective-permute-start.20 = (f32[4,128]{1,0:T(4,128)S(1)}, f32[4,128]{1,0:T(4,128)S(1)}, u32[]{:S(2)}, u32[]{:S(2)}) collective-permute-start(f32[4,128]{1,0:T(4,128)S(1)} %shard_map.84), channel_id=1, source_target_pairs={{0,2},{1,3},{2,0},{3,1},{4,6},{5,7},{6,4},{7,5},{8,10},{9,11},{10,... | collective-permute-start | bytes 6152 | tf_op jit(solution)/shard_map/ppermute | solution.py:404
  66.3 0.8 shard_map.85
  67.1 0.7 collective-permute-done.20
  67.8 0.8 shard_map.86
  68.7 0.8 shard_map.87
  69.5 10.5 %all_to_all.23.refs_8_ = f32[8,36,128]{2,1,0:T(8,128)S(1)} all-to-all(f32[8,36,128]{2,1,0:T(8,128)S(1)} %get-tuple-element.138), channel_id=1, replica_groups=mesh['src'=8,'tgt'=4] {'src'}, dimensions={0} | all-to-all | bytes 294912 | tf_op jit(solution)/shard_map/all_to_all | solution.py:607
  80.0 3.3 %shard_map.88 = (f32[50,512]{1,0:T(8,128)}, f32[4,128]{1,0:T(4,128)}, f32[32,128]{1,0:T(8,128)}) custom-call(f32[512,1024]{1,0:T(8,128)S(1)} %get-tuple-element.97.refs_0_, f32[512,1024]{1,0:T(8,128)S(1)} %get-tuple-element.110.refs_1_, f32[512,1024]{1,0:T(8,128)S(1)} %get-tuple-element.121.refs_2_, f32[512,1024]{1,0:T(8,128)S(1)} %get-tuple-element.127.refs_3_, ...), custom_call_target="tpu_custom_call" | custom-call | flops 2415919104 | tf_op jit(solution)/shard_map/pallas_call | solution.py:416
  (41 shorter events, 2.5 us)
Async XLA Ops:
  5.5 7.8 %collective-permute-start.1 = (f32[4,128]{1,0:T(4,128)S(1)}, f32[4,128]{1,0:T(4,128)S(1)}, u32[]{:S(2)}, u32[]{:S(2)}) collective-permute-start(f32[4,128]{1,0:T(4,128)S(1)} %get-tuple-element.76), channel_id=1, source_target_pairs={{0,2},{1,3},{2,0},{3,1},{4,6},{5,7},{6,4},{7,5},{8,10},{9,11},{10,... | collective-permute-start | bytes 6152 | tf_op jit(solution)/shard_map/ppermute | solution.py:404
  8.5 6.3 %collective-permute-start.2 = (f32[4,128]{1,0:T(4,128)S(1)}, f32[4,128]{1,0:T(4,128)S(1)}, u32[]{:S(2)}, u32[]{:S(2)}) collective-permute-start(f32[4,128]{1,0:T(4,128)S(1)} %get-tuple-element.76), channel_id=1, source_target_pairs={{0,3},{1,2},{2,1},{3,0},{4,7},{5,6},{6,5},{7,4},{8,11},{9,10},{10,... | collective-permute-start | bytes 6152 | tf_op jit(solution)/shard_map/ppermute | solution.py:404
  8.5 6.3 %collective-permute-start = (f32[4,128]{1,0:T(4,128)S(1)}, f32[4,128]{1,0:T(4,128)S(1)}, u32[]{:S(2)}, u32[]{:S(2)}) collective-permute-start(f32[4,128]{1,0:T(4,128)S(1)} %get-tuple-element.76), channel_id=1, source_target_pairs={{0,1},{1,0},{2,3},{3,2},{4,5},{5,4},{6,7},{7,6},{8,9},{9,8},{10,11... | collective-permute-start | bytes 6152 | tf_op jit(solution)/shard_map/ppermute | solution.py:404
  8.7 8.2 %collective-permute-start.3 = (f32[1,104,128]{2,1,0:T(8,128)S(1)}, f32[1,104,128]{2,1,0:T(8,128)S(1)}, u32[]{:S(2)}, u32[]{:S(2)}) collective-permute-start(f32[1,104,128]{2,1,0:T(8,128)S(1)} %get-tuple-element.93), channel_id=1, source_target_pairs={{0,16},{4,20},{8,24},{12,28},{16,0},{20,4},{24,8},{28,12},{1,17},{... | collective-permute-start | bytes 159752 | tf_op jit(solution)/shard_map/ppermute | solution.py:404
  11.8 5.2 %collective-permute-start.4 = (f32[1,104,128]{2,1,0:T(8,128)S(1)}, f32[1,104,128]{2,1,0:T(8,128)S(1)}, u32[]{:S(2)}, u32[]{:S(2)}) collective-permute-start(f32[1,104,128]{2,1,0:T(8,128)S(1)} %get-tuple-element.93), channel_id=1, source_target_pairs={{0,8},{4,12},{8,0},{12,4},{16,24},{20,28},{24,16},{28,20},{1,9},{5... | collective-permute-start | bytes 159752 | tf_op jit(solution)/shard_map/ppermute | solution.py:404
  13.3 4.1 %collective-permute-start.5 = (f32[1,104,128]{2,1,0:T(8,128)S(1)}, f32[1,104,128]{2,1,0:T(8,128)S(1)}, u32[]{:S(2)}, u32[]{:S(2)}) collective-permute-start(f32[1,104,128]{2,1,0:T(8,128)S(1)} %get-tuple-element.93), channel_id=1, source_target_pairs={{0,4},{4,0},{8,12},{12,8},{16,20},{20,16},{24,28},{28,24},{1,5},{5... | collective-permute-start | bytes 159752 | tf_op jit(solution)/shard_map/ppermute | solution.py:404
  28.6 3.7 %collective-permute-start.7 = (f32[4,128]{1,0:T(4,128)S(1)}, f32[4,128]{1,0:T(4,128)S(1)}, u32[]{:S(2)}, u32[]{:S(2)}) collective-permute-start(f32[4,128]{1,0:T(4,128)S(1)} %shard_map.78), channel_id=1, source_target_pairs={{0,2},{1,3},{2,0},{3,1},{4,6},{5,7},{6,4},{7,5},{8,10},{9,11},{10,... | collective-permute-start | bytes 6152 | tf_op jit(solution)/shard_map/ppermute | solution.py:404
  30.2 3.0 %collective-permute-start.8 = (f32[4,128]{1,0:T(4,128)S(1)}, f32[4,128]{1,0:T(4,128)S(1)}, u32[]{:S(2)}, u32[]{:S(2)}) collective-permute-start(f32[4,128]{1,0:T(4,128)S(1)} %shard_map.78), channel_id=1, source_target_pairs={{0,3},{1,2},{2,1},{3,0},{4,7},{5,6},{6,5},{7,4},{8,11},{9,10},{10,... | collective-permute-start | bytes 6152 | tf_op jit(solution)/shard_map/ppermute | solution.py:404
  30.2 3.0 %collective-permute-start.6 = (f32[4,128]{1,0:T(4,128)S(1)}, f32[4,128]{1,0:T(4,128)S(1)}, u32[]{:S(2)}, u32[]{:S(2)}) collective-permute-start(f32[4,128]{1,0:T(4,128)S(1)} %shard_map.78), channel_id=1, source_target_pairs={{0,1},{1,0},{2,3},{3,2},{4,5},{5,4},{6,7},{7,6},{8,9},{9,8},{10,11... | collective-permute-start | bytes 6152 | tf_op jit(solution)/shard_map/ppermute | solution.py:404
  30.8 4.3 %collective-permute-start.10 = (f32[1,104,128]{2,1,0:T(8,128)S(1)}, f32[1,104,128]{2,1,0:T(8,128)S(1)}, u32[]{:S(2)}, u32[]{:S(2)}) collective-permute-start(f32[1,104,128]{2,1,0:T(8,128)S(1)} %collective-permute-done.4), channel_id=1, source_target_pairs={{0,4},{4,0},{8,12},{12,8},{16,20},{20,16},{24,28},{28,24},{1,5},{5... | collective-permute-start | bytes 159752 | tf_op jit(solution)/shard_map/ppermute | solution.py:404
  31.0 4.1 %collective-permute-start.11 = (f32[1,104,128]{2,1,0:T(8,128)S(1)}, f32[1,104,128]{2,1,0:T(8,128)S(1)}, u32[]{:S(2)}, u32[]{:S(2)}) collective-permute-start(f32[1,104,128]{2,1,0:T(8,128)S(1)} %collective-permute-done.3), channel_id=1, source_target_pairs={{0,8},{4,12},{8,0},{12,4},{16,24},{20,28},{24,16},{28,20},{1,9},{5... | collective-permute-start | bytes 159752 | tf_op jit(solution)/shard_map/ppermute | solution.py:404
  32.2 1.8 %collective-permute-start.9 = (f32[4,104,128]{2,1,0:T(8,128)S(1)}, f32[4,104,128]{2,1,0:T(8,128)S(1)}, u32[]{:S(2)}, u32[]{:S(2)}) collective-permute-start(f32[4,104,128]{2,1,0:T(8,128)S(1)} %constant_dynamic-update-slice_fusion.mine_ref), channel_id=1, source_target_pairs={{0,1},{1,0},{2,3},{3,2},{4,5},{5,4},{6,7},{7,6},{8,9},{9,8},{10,11... | collective-permute-start | bytes 638984 | tf_op jit(solution)/shard_map/ppermute | solution.py:404
  46.2 4.3 %collective-permute-start.13 = (f32[4,128]{1,0:T(4,128)S(1)}, f32[4,128]{1,0:T(4,128)S(1)}, u32[]{:S(2)}, u32[]{:S(2)}) collective-permute-start(f32[4,128]{1,0:T(4,128)S(1)} %shard_map.81), channel_id=1, source_target_pairs={{0,2},{1,3},{2,0},{3,1},{4,6},{5,7},{6,4},{7,5},{8,10},{9,11},{10,... | collective-permute-start | bytes 6152 | tf_op jit(solution)/shard_map/ppermute | solution.py:404
  47.8 3.0 %collective-permute-start.14 = (f32[4,128]{1,0:T(4,128)S(1)}, f32[4,128]{1,0:T(4,128)S(1)}, u32[]{:S(2)}, u32[]{:S(2)}) collective-permute-start(f32[4,128]{1,0:T(4,128)S(1)} %shard_map.81), channel_id=1, source_target_pairs={{0,3},{1,2},{2,1},{3,0},{4,7},{5,6},{6,5},{7,4},{8,11},{9,10},{10,... | collective-permute-start | bytes 6152 | tf_op jit(solution)/shard_map/ppermute | solution.py:404
  47.8 3.0 %collective-permute-start.12 = (f32[4,128]{1,0:T(4,128)S(1)}, f32[4,128]{1,0:T(4,128)S(1)}, u32[]{:S(2)}, u32[]{:S(2)}) collective-permute-start(f32[4,128]{1,0:T(4,128)S(1)} %shard_map.81), channel_id=1, source_target_pairs={{0,1},{1,0},{2,3},{3,2},{4,5},{5,4},{6,7},{7,6},{8,9},{9,8},{10,11... | collective-permute-start | bytes 6152 | tf_op jit(solution)/shard_map/ppermute | solution.py:404
  48.4 4.3 %collective-permute-start.15 = (f32[1,104,128]{2,1,0:T(8,128)S(1)}, f32[1,104,128]{2,1,0:T(8,128)S(1)}, u32[]{:S(2)}, u32[]{:S(2)}) collective-permute-start(f32[1,104,128]{2,1,0:T(8,128)S(1)} %collective-permute-done.3), channel_id=1, source_target_pairs={{0,4},{4,0},{8,12},{12,8},{16,20},{20,16},{24,28},{28,24},{1,5},{5... | collective-permute-start | bytes 159752 | tf_op jit(solution)/shard_map/ppermute | solution.py:404
  48.8 4.5 %collective-permute-start.16 = (f32[1,104,128]{2,1,0:T(8,128)S(1)}, f32[1,104,128]{2,1,0:T(8,128)S(1)}, u32[]{:S(2)}, u32[]{:S(2)}) collective-permute-start(f32[1,104,128]{2,1,0:T(8,128)S(1)} %collective-permute-done.11), channel_id=1, source_target_pairs={{0,4},{4,0},{8,12},{12,8},{16,20},{20,16},{24,28},{28,24},{1,5},{5... | collective-permute-start | bytes 159752 | tf_op jit(solution)/shard_map/ppermute | solution.py:404
  50.5 2.8 %collective-permute-start.17 = (f32[2,104,128]{2,1,0:T(8,128)S(1)}, f32[2,104,128]{2,1,0:T(8,128)S(1)}, u32[]{:S(2)}, u32[]{:S(2)}) collective-permute-start(f32[2,104,128]{2,1,0:T(8,128)S(1)} %constant_dynamic-update-slice_fusion.4.mine_ref), channel_id=1, source_target_pairs={{0,1},{1,0},{2,3},{3,2},{4,5},{5,4},{6,7},{7,6},{8,9},{9,8},{10,11... | collective-permute-start | bytes 319496 | tf_op jit(solution)/shard_map/ppermute | solution.py:404
  64.0 3.7 %collective-permute-start.18 = (f32[2,104,128]{2,1,0:T(8,128)S(1)}, f32[2,104,128]{2,1,0:T(8,128)S(1)}, u32[]{:S(2)}, u32[]{:S(2)}) collective-permute-start(f32[2,104,128]{2,1,0:T(8,128)S(1)} %constant_dynamic-update-slice_fusion.6.mine_ref), channel_id=1, source_target_pairs={{0,1},{1,0},{2,3},{3,2},{4,5},{5,4},{6,7},{7,6},{8,9},{9,8},{10,11... | collective-permute-start | bytes 319496 | tf_op jit(solution)/shard_map/ppermute | solution.py:404
  64.1 3.7 %collective-permute-start.20 = (f32[4,128]{1,0:T(4,128)S(1)}, f32[4,128]{1,0:T(4,128)S(1)}, u32[]{:S(2)}, u32[]{:S(2)}) collective-permute-start(f32[4,128]{1,0:T(4,128)S(1)} %shard_map.84), channel_id=1, source_target_pairs={{0,2},{1,3},{2,0},{3,1},{4,6},{5,7},{6,4},{7,5},{8,10},{9,11},{10,... | collective-permute-start | bytes 6152 | tf_op jit(solution)/shard_map/ppermute | solution.py:404
  65.7 3.0 %collective-permute-start.21 = (f32[4,128]{1,0:T(4,128)S(1)}, f32[4,128]{1,0:T(4,128)S(1)}, u32[]{:S(2)}, u32[]{:S(2)}) collective-permute-start(f32[4,128]{1,0:T(4,128)S(1)} %shard_map.84), channel_id=1, source_target_pairs={{0,3},{1,2},{2,1},{3,0},{4,7},{5,6},{6,5},{7,4},{8,11},{9,10},{10,... | collective-permute-start | bytes 6152 | tf_op jit(solution)/shard_map/ppermute | solution.py:404
  66.0 2.7 %collective-permute-start.19 = (f32[4,128]{1,0:T(4,128)S(1)}, f32[4,128]{1,0:T(4,128)S(1)}, u32[]{:S(2)}, u32[]{:S(2)}) collective-permute-start(f32[4,128]{1,0:T(4,128)S(1)} %shard_map.84), channel_id=1, source_target_pairs={{0,1},{1,0},{2,3},{3,2},{4,5},{5,4},{6,7},{7,6},{8,9},{9,8},{10,11... | collective-permute-start | bytes 6152 | tf_op jit(solution)/shard_map/ppermute | solution.py:404

commit v8 on v7

--- a/solution.py
+++ b/solution.py
@@ -433,16 +433,18 @@
         self.own = own
         self.rows = rows
         self.n_half = n_half
-        self.blocks = {0: half}
+        self.blocks = {(0,): half}
         self.coming = {}
         if len(bits) >= 3:
             z, w, x = bits[:3]
-            self.fetches = [[(0, w), (0, z), (0, x)], [(z, x), (w, z)], [(w, x), (w ^ z, x)], []]
-            self.groups = [[], [0, z, w, x], [z ^ x, w ^ z], [w ^ x, w ^ z ^ x]]
+            self.fetches = [
+                [([(0,)], w), ([(0,)], z), ([(0,)], x)], [([(z,)], x), ([(w,)], z)], [([(w,), (w ^ z,)], x)], []
+            ]
+            self.groups = [[], [(0,), (z,), (w,), (x,)], [(z ^ x,), (w ^ z,)], [(w ^ x, w ^ z ^ x)]]
             self.bits = bits[3:]
         else:
             self.fetches = [[]] * ITERS
-            self.groups = [[]] * (ITERS - 1) + [[0]]
+            self.groups = [[]] * (ITERS - 1) + [[(0,)]]
             self.bits = bits
         self.ready = None
         self.mine = []
@@ -455,17 +457,20 @@
         self.done = []
 
     def start(self, step, value, exchange):
-        used = sorted({offset for offset, _ in self.fetches[step]} | set(self.groups[step]))
+        used = sorted({key for keys, _ in self.fetches[step] for key in keys} | set(self.groups[step]))
         if step and used:
-            value, *held = tie(value, *[self.blocks[offset] for offset in used])
+            value, *held = tie(value, *[self.blocks[key] for key in used])
             self.blocks.update(zip(used, held))
         others = exchange(value)
-        for offset, bit in self.fetches[step]:
-            self.coming[offset ^ bit] = swap(self.blocks[offset], "src", bit)
+        for keys, bit in self.fetches[step]:
+            self.coming[tuple(offset ^ bit for key in keys for offset in key)] = swap(self.joined(keys), "src", bit)
         if self.groups[step]:
-            held = [self.blocks[offset] for offset in self.groups[step]]
-            self.add(held[0] if len(held) == 1 else jnp.concatenate(held, axis=0), self.groups[step])
+            self.add(self.joined(self.groups[step]), [offset for key in self.groups[step] for offset in key])
         return others
+
+    def joined(self, keys):
+        held = [self.blocks[key] for key in keys]
+        return held[0] if len(held) == 1 else jnp.concatenate(held, axis=0)
 
     def add(self, mine, offsets):
         group = len(self.mine)

time: 83.6 us -> 83.5 us (level)
  waiting for transfers between devices: 3.43 us -> 5.12 us
  starting transfers between devices: 19.4 us -> 17.8 us
    ppermute x22 -> x21, waiting for transfers between devices: 3.43 us -> 5.12 us  [swap(): lax.ppermute(value, axis, [(i, i ^ step) for i in range(lax.axis_size(axi...]
    ppermute x22 -> x21, starting transfers between devices: 19.4 us -> 17.8 us  [swap(): lax.ppermute(value, axis, [(i, i ^ step) for i in range(lax.axis_size(axi...]
  transfers between devices with their start and end apart: 22 -> 21, of which waited for: 9 -> 9; matrix products, arithmetic and copies ran while one was open for 0% -> 0% of each run, Pallas kernels for 9% -> 9%
where the time goes in v8:
time: 83.5 us; the launch traced here: 83.2 us
  blocking collectives  40.7 us (49%)
  Pallas kernels  17.9 us (21%)
  starting transfers between devices  17.8 us (21%)
  waiting for transfers between devices  5.12 us (6%)
  between operations  1.47 us (2%)
    all_to_all x3, blocking collectives, shards(): lse = lax.all_to_all(lse, 'src', 0, 0, tiled=True)  30.2 us
    ppermute x21, starting transfers between devices, swap(): lax.ppermute(value, axis, [(i, i ^ step) for i in range(lax.axis_size(axi...  17.8 us
    pallas_call x12, Pallas kernels, call(): pl.pallas_call(kernel, out_shape=[buffer(pltpu.VMEM if pin else jax.Shape...  13.7 us
    all_to_all x1, blocking collectives, shards(): both = lax.all_to_all(lse, 'src', 0, 0, tiled=True)  10.5 us
    ppermute x21, waiting for transfers between devices, swap(): lax.ppermute(value, axis, [(i, i ^ step) for i in range(lax.axis_size(axi...  5.12 us
    pallas_call x1, Pallas kernels, shards(): pl.pallas_call(first_kernel, out_shape=[pltpu.VMEM(shape, jnp.float32) fo...  4.23 us
  transfers between devices with their start and end apart: 21, of which 9 were waited for; matrix products, arithmetic and copies ran while one was open for 0% of the time, Pallas kernels for 9%

profile of v8, /device:TPU:0, one launch (start us, length us, event | category | flops | bytes accessed | tf_op | source)
XLA Modules:
  0.0 83.2 jit_solution(14656038210374442682)
XLA Ops:
  1.3 4.2 %shard_map.76 = (f32[512,4096]{1,0:T(8,128)S(1)}, f32[4,128]{1,0:T(4,128)S(1)}, f32[3,4,128]{2,1,0:T(4,128)S(1)}, f32[3,32,128]{2,1,0:T(8,128)S(1)}, f32[64,512]{1,0:T(8,128)S(1)}, /*index=5*/f32[1,104,128]{2,1,0:T(8,128)S(1)}) custom-call(f32[50,512]{1,0:T(8,128)} %src_hbm.1, f32[50,4096]{1,0:T(8,128)} %tgt_hbm.1, s32[8]{0:T(128)} %count_src_hbm.1, ...), custom_call_target="tpu_custom_call" | custom-call | flops 1610612736 | tf_op jit(solution)/shard_map/pallas_call | solution.py:540
  5.5 3.0 %collective-permute-start.1 = (f32[4,128]{1,0:T(4,128)S(1)}, f32[4,128]{1,0:T(4,128)S(1)}, u32[]{:S(2)}, u32[]{:S(2)}) collective-permute-start(f32[4,128]{1,0:T(4,128)S(1)} %get-tuple-element.74), channel_id=1, source_target_pairs={{0,2},{1,3},{2,0},{3,1},{4,6},{5,7},{6,4},{7,5},{8,10},{9,11},{10,... | collective-permute-start | bytes 6152 | tf_op jit(solution)/shard_map/ppermute | solution.py:404
  8.7 3.0 %collective-permute-start.3 = (f32[1,104,128]{2,1,0:T(8,128)S(1)}, f32[1,104,128]{2,1,0:T(8,128)S(1)}, u32[]{:S(2)}, u32[]{:S(2)}) collective-permute-start(f32[1,104,128]{2,1,0:T(8,128)S(1)} %get-tuple-element.91), channel_id=1, source_target_pairs={{0,16},{4,20},{8,24},{12,28},{16,0},{20,4},{24,8},{28,12},{1,17},{... | collective-permute-start | bytes 159752 | tf_op jit(solution)/shard_map/ppermute | solution.py:404
  11.8 1.6 %collective-permute-start.4 = (f32[1,104,128]{2,1,0:T(8,128)S(1)}, f32[1,104,128]{2,1,0:T(8,128)S(1)}, u32[]{:S(2)}, u32[]{:S(2)}) collective-permute-start(f32[1,104,128]{2,1,0:T(8,128)S(1)} %get-tuple-element.91), channel_id=1, source_target_pairs={{0,8},{4,12},{8,0},{12,4},{16,24},{20,28},{24,16},{28,20},{1,9},{5... | collective-permute-start | bytes 159752 | tf_op jit(solution)/shard_map/ppermute | solution.py:404
  13.3 1.5 %collective-permute-start.5 = (f32[1,104,128]{2,1,0:T(8,128)S(1)}, f32[1,104,128]{2,1,0:T(8,128)S(1)}, u32[]{:S(2)}, u32[]{:S(2)}) collective-permute-start(f32[1,104,128]{2,1,0:T(8,128)S(1)} %get-tuple-element.91), channel_id=1, source_target_pairs={{0,4},{4,0},{8,12},{12,8},{16,20},{20,16},{24,28},{28,24},{1,5},{5... | collective-permute-start | bytes 159752 | tf_op jit(solution)/shard_map/ppermute | solution.py:404
  14.9 2.1 %shard_map.77 = (f32[8,32,128]{2,1,0:T(8,128)S(1)}, f32[4,128]{1,0:T(4,128)S(1)}, f32[512,4096]{1,0:T(8,128)S(1)}, f32[32,128]{1,0:T(8,128)S(1)}) custom-call(f32[512,4096]{1,0:T(8,128)S(1)} %get-tuple-element.73.score_ref, f32[4,128]{1,0:T(4,128)S(1)} %multiply_add_fusion.3.lse_ref, f32[3,4,128]{2,1,0:T(4,128)S(1)} %get-tuple-element.75.aux_ref.row_aux), custom_call_target="tpu_custom_call" | custom-call | tf_op jit(solution)/shard_map/pallas_call | solution.py:416
  17.5 10.3 %all_to_all.20.parts_ref = f32[8,32,128]{2,1,0:T(8,128)S(1)} all-to-all(f32[8,32,128]{2,1,0:T(8,128)S(1)} %get-tuple-element.83), channel_id=1, replica_groups=mesh['src'=8,'tgt'=4] {'src'}, dimensions={0} | all-to-all | bytes 262144 | tf_op jit(solution)/shard_map/all_to_all | solution.py:604
  27.8 0.8 shard_map.78
  28.6 1.6 %collective-permute-start.7 = (f32[4,128]{1,0:T(4,128)S(1)}, f32[4,128]{1,0:T(4,128)S(1)}, u32[]{:S(2)}, u32[]{:S(2)}) collective-permute-start(f32[4,128]{1,0:T(4,128)S(1)} %shard_map.78), channel_id=1, source_target_pairs={{0,2},{1,3},{2,0},{3,1},{4,6},{5,7},{6,4},{7,5},{8,10},{9,11},{10,... | collective-permute-start | bytes 6152 | tf_op jit(solution)/shard_map/ppermute | solution.py:404
  30.2 0.6 collective-permute-start.6
  31.0 1.1 %collective-permute-start.11 = (f32[1,104,128]{2,1,0:T(8,128)S(1)}, f32[1,104,128]{2,1,0:T(8,128)S(1)}, u32[]{:S(2)}, u32[]{:S(2)}) collective-permute-start(f32[1,104,128]{2,1,0:T(8,128)S(1)} %collective-permute-done.3), channel_id=1, source_target_pairs={{0,8},{4,12},{8,0},{12,4},{16,24},{20,28},{24,16},{28,20},{1,9},{5... | collective-permute-start | bytes 159752 | tf_op jit(solution)/shard_map/ppermute | solution.py:404
  32.2 0.9 %collective-permute-done.8 = f32[4,128]{1,0:T(4,128)S(1)} collective-permute-done((f32[4,128]{1,0:T(4,128)S(1)}, f32[4,128]{1,0:T(4,128)S(1)}, u32[]{:S(2)}, u32[]{:S(2)}) %collective-permute-start.8) | collective-permute-done | bytes 2080 | tf_op jit(solution)/shard_map/ppermute | solution.py:404
  33.2 0.8 shard_map.79
  34.0 1.0 %shard_map.80 = (f32[512,1024]{1,0:T(8,128)S(1)}, bf16[1024,128]{1,0:T(8,128)(2,1)S(1)}, f32[8,128]{1,0:T(8,128)S(1)}, bf16[512,384]{1,0:T(8,128)(2,1)S(1)}, f32[512,128]{1,0:T(8,128)S(1)}) custom-call(f32[64,512]{1,0:T(8,128)S(1)} %get-tuple-element.117.own_ref, f32[4,104,128]{2,1,0:T(8,128)S(1)} %constant_dynamic-update-slice_fusion.mine_ref, ...), custom_call_target="tpu_custom_call" | custom-call | flops 402653184 | tf_op jit(solution)/shard_map/pallas_call | solution.py:416
  35.2 10.2 %all_to_all.21.parts_ref = f32[8,32,128]{2,1,0:T(8,128)S(1)} all-to-all(f32[8,32,128]{2,1,0:T(8,128)S(1)} %shard_map.79), channel_id=1, replica_groups=mesh['src'=8,'tgt'=4] {'src'}, dimensions={0} | all-to-all | bytes 262144 | tf_op jit(solution)/shard_map/all_to_all | solution.py:604
  45.4 0.8 shard_map.81
  46.2 1.6 %collective-permute-start.13 = (f32[4,128]{1,0:T(4,128)S(1)}, f32[4,128]{1,0:T(4,128)S(1)}, u32[]{:S(2)}, u32[]{:S(2)}) collective-permute-start(f32[4,128]{1,0:T(4,128)S(1)} %shard_map.81), channel_id=1, source_target_pairs={{0,2},{1,3},{2,0},{3,1},{4,6},{5,7},{6,4},{7,5},{8,10},{9,11},{10,... | collective-permute-start | bytes 6152 | tf_op jit(solution)/shard_map/ppermute | solution.py:404
  47.8 0.6 collective-permute-start.12
  48.9 0.9 %collective-permute-done.13 = f32[4,128]{1,0:T(4,128)S(1)} collective-permute-done((f32[4,128]{1,0:T(4,128)S(1)}, f32[4,128]{1,0:T(4,128)S(1)}, u32[]{:S(2)}, u32[]{:S(2)}) %collective-permute-start.13) | collective-permute-done | bytes 2080 | tf_op jit(solution)/shard_map/ppermute | solution.py:404
  49.9 0.9 %collective-permute-done.14 = f32[4,128]{1,0:T(4,128)S(1)} collective-permute-done((f32[4,128]{1,0:T(4,128)S(1)}, f32[4,128]{1,0:T(4,128)S(1)}, u32[]{:S(2)}, u32[]{:S(2)}) %collective-permute-start.14) | collective-permute-done | bytes 2080 | tf_op jit(solution)/shard_map/ppermute | solution.py:404
  50.8 1.0 %shard_map.82 = f32[8,32,128]{2,1,0:T(8,128)S(1)} custom-call(f32[512,4096]{1,0:T(8,128)S(1)} %get-tuple-element.73.score_ref, f32[512,4096]{1,0:T(8,128)S(1)} %get-tuple-element.76.kernel_ref, f32[32,128]{1,0:T(8,128)S(1)} %get-tuple-element.77.top_ref, f32[4,128]{1,0:T(4,128)S(1)} %get-tuple-element.78.base_ref, f32[4,128]{1,0:T(4,128)S(1)} %multiply_add_fusion.1.lse_ref, ...), custom_call_target="tpu_custom_call" | custom-call | tf_op jit(solution)/shard_map/pallas_call | solution.py:416
  51.8 0.8 shard_map.83
  52.6 0.8 collective-permute-done.15.mine_ref
  53.4 9.7 %all_to_all.22.parts_ref = f32[8,32,128]{2,1,0:T(8,128)S(1)} all-to-all(f32[8,32,128]{2,1,0:T(8,128)S(1)} %shard_map.82), channel_id=1, replica_groups=mesh['src'=8,'tgt'=4] {'src'}, dimensions={0} | all-to-all | bytes 262144 | tf_op jit(solution)/shard_map/all_to_all | solution.py:604
  63.1 0.8 shard_map.84
  64.0 1.6 %collective-permute-start.19 = (f32[4,128]{1,0:T(4,128)S(1)}, f32[4,128]{1,0:T(4,128)S(1)}, u32[]{:S(2)}, u32[]{:S(2)}) collective-permute-start(f32[4,128]{1,0:T(4,128)S(1)} %shard_map.84), channel_id=1, source_target_pairs={{0,2},{1,3},{2,0},{3,1},{4,6},{5,7},{6,4},{7,5},{8,10},{9,11},{10,... | collective-permute-start | bytes 6152 | tf_op jit(solution)/shard_map/ppermute | solution.py:404
  66.2 0.8 shard_map.85
  67.0 0.7 collective-permute-done.19
  67.7 0.8 shard_map.86
  68.6 0.8 shard_map.87
  69.4 10.5 %all_to_all.23.refs_8_ = f32[8,36,128]{2,1,0:T(8,128)S(1)} all-to-all(f32[8,36,128]{2,1,0:T(8,128)S(1)} %get-tuple-element.134), channel_id=1, replica_groups=mesh['src'=8,'tgt'=4] {'src'}, dimensions={0} | all-to-all | bytes 294912 | tf_op jit(solution)/shard_map/all_to_all | solution.py:612
  79.9 3.3 %shard_map.88 = (f32[50,512]{1,0:T(8,128)}, f32[4,128]{1,0:T(4,128)}, f32[32,128]{1,0:T(8,128)}) custom-call(f32[512,1024]{1,0:T(8,128)S(1)} %get-tuple-element.95.refs_0_, f32[512,1024]{1,0:T(8,128)S(1)} %get-tuple-element.108.refs_1_, f32[512,1024]{1,0:T(8,128)S(1)} %get-tuple-element.119.refs_2_, f32[512,1024]{1,0:T(8,128)S(1)} %get-tuple-element.123.refs_3_, ...), custom_call_target="tpu_custom_call" | custom-call | flops 2415919104 | tf_op jit(solution)/shard_map/pallas_call | solution.py:416
  (38 shorter events, 2.7 us)
Async XLA Ops:
  5.5 7.8 %collective-permute-start.1 = (f32[4,128]{1,0:T(4,128)S(1)}, f32[4,128]{1,0:T(4,128)S(1)}, u32[]{:S(2)}, u32[]{:S(2)}) collective-permute-start(f32[4,128]{1,0:T(4,128)S(1)} %get-tuple-element.74), channel_id=1, source_target_pairs={{0,2},{1,3},{2,0},{3,1},{4,6},{5,7},{6,4},{7,5},{8,10},{9,11},{10,... | collective-permute-start | bytes 6152 | tf_op jit(solution)/shard_map/ppermute | solution.py:404
  8.5 6.3 %collective-permute-start.2 = (f32[4,128]{1,0:T(4,128)S(1)}, f32[4,128]{1,0:T(4,128)S(1)}, u32[]{:S(2)}, u32[]{:S(2)}) collective-permute-start(f32[4,128]{1,0:T(4,128)S(1)} %get-tuple-element.74), channel_id=1, source_target_pairs={{0,3},{1,2},{2,1},{3,0},{4,7},{5,6},{6,5},{7,4},{8,11},{9,10},{10,... | collective-permute-start | bytes 6152 | tf_op jit(solution)/shard_map/ppermute | solution.py:404
  8.5 6.3 %collective-permute-start = (f32[4,128]{1,0:T(4,128)S(1)}, f32[4,128]{1,0:T(4,128)S(1)}, u32[]{:S(2)}, u32[]{:S(2)}) collective-permute-start(f32[4,128]{1,0:T(4,128)S(1)} %get-tuple-element.74), channel_id=1, source_target_pairs={{0,1},{1,0},{2,3},{3,2},{4,5},{5,4},{6,7},{7,6},{8,9},{9,8},{10,11... | collective-permute-start | bytes 6152 | tf_op jit(solution)/shard_map/ppermute | solution.py:404
  8.7 8.2 %collective-permute-start.3 = (f32[1,104,128]{2,1,0:T(8,128)S(1)}, f32[1,104,128]{2,1,0:T(8,128)S(1)}, u32[]{:S(2)}, u32[]{:S(2)}) collective-permute-start(f32[1,104,128]{2,1,0:T(8,128)S(1)} %get-tuple-element.91), channel_id=1, source_target_pairs={{0,16},{4,20},{8,24},{12,28},{16,0},{20,4},{24,8},{28,12},{1,17},{... | collective-permute-start | bytes 159752 | tf_op jit(solution)/shard_map/ppermute | solution.py:404
  11.8 5.2 %collective-permute-start.4 = (f32[1,104,128]{2,1,0:T(8,128)S(1)}, f32[1,104,128]{2,1,0:T(8,128)S(1)}, u32[]{:S(2)}, u32[]{:S(2)}) collective-permute-start(f32[1,104,128]{2,1,0:T(8,128)S(1)} %get-tuple-element.91), channel_id=1, source_target_pairs={{0,8},{4,12},{8,0},{12,4},{16,24},{20,28},{24,16},{28,20},{1,9},{5... | collective-permute-start | bytes 159752 | tf_op jit(solution)/shard_map/ppermute | solution.py:404
  13.3 4.1 %collective-permute-start.5 = (f32[1,104,128]{2,1,0:T(8,128)S(1)}, f32[1,104,128]{2,1,0:T(8,128)S(1)}, u32[]{:S(2)}, u32[]{:S(2)}) collective-permute-start(f32[1,104,128]{2,1,0:T(8,128)S(1)} %get-tuple-element.91), channel_id=1, source_target_pairs={{0,4},{4,0},{8,12},{12,8},{16,20},{20,16},{24,28},{28,24},{1,5},{5... | collective-permute-start | bytes 159752 | tf_op jit(solution)/shard_map/ppermute | solution.py:404
  28.6 3.7 %collective-permute-start.7 = (f32[4,128]{1,0:T(4,128)S(1)}, f32[4,128]{1,0:T(4,128)S(1)}, u32[]{:S(2)}, u32[]{:S(2)}) collective-permute-start(f32[4,128]{1,0:T(4,128)S(1)} %shard_map.78), channel_id=1, source_target_pairs={{0,2},{1,3},{2,0},{3,1},{4,6},{5,7},{6,4},{7,5},{8,10},{9,11},{10,... | collective-permute-start | bytes 6152 | tf_op jit(solution)/shard_map/ppermute | solution.py:404
  30.2 3.0 %collective-permute-start.8 = (f32[4,128]{1,0:T(4,128)S(1)}, f32[4,128]{1,0:T(4,128)S(1)}, u32[]{:S(2)}, u32[]{:S(2)}) collective-permute-start(f32[4,128]{1,0:T(4,128)S(1)} %shard_map.78), channel_id=1, source_target_pairs={{0,3},{1,2},{2,1},{3,0},{4,7},{5,6},{6,5},{7,4},{8,11},{9,10},{10,... | collective-permute-start | bytes 6152 | tf_op jit(solution)/shard_map/ppermute | solution.py:404
  30.2 3.0 %collective-permute-start.6 = (f32[4,128]{1,0:T(4,128)S(1)}, f32[4,128]{1,0:T(4,128)S(1)}, u32[]{:S(2)}, u32[]{:S(2)}) collective-permute-start(f32[4,128]{1,0:T(4,128)S(1)} %shard_map.78), channel_id=1, source_target_pairs={{0,1},{1,0},{2,3},{3,2},{4,5},{5,4},{6,7},{7,6},{8,9},{9,8},{10,11... | collective-permute-start | bytes 6152 | tf_op jit(solution)/shard_map/ppermute | solution.py:404
  30.8 4.3 %collective-permute-start.10 = (f32[1,104,128]{2,1,0:T(8,128)S(1)}, f32[1,104,128]{2,1,0:T(8,128)S(1)}, u32[]{:S(2)}, u32[]{:S(2)}) collective-permute-start(f32[1,104,128]{2,1,0:T(8,128)S(1)} %collective-permute-done.4), channel_id=1, source_target_pairs={{0,4},{4,0},{8,12},{12,8},{16,20},{20,16},{24,28},{28,24},{1,5},{5... | collective-permute-start | bytes 159752 | tf_op jit(solution)/shard_map/ppermute | solution.py:404
  31.0 4.1 %collective-permute-start.11 = (f32[1,104,128]{2,1,0:T(8,128)S(1)}, f32[1,104,128]{2,1,0:T(8,128)S(1)}, u32[]{:S(2)}, u32[]{:S(2)}) collective-permute-start(f32[1,104,128]{2,1,0:T(8,128)S(1)} %collective-permute-done.3), channel_id=1, source_target_pairs={{0,8},{4,12},{8,0},{12,4},{16,24},{20,28},{24,16},{28,20},{1,9},{5... | collective-permute-start | bytes 159752 | tf_op jit(solution)/shard_map/ppermute | solution.py:404
  32.2 1.8 %collective-permute-start.9 = (f32[4,104,128]{2,1,0:T(8,128)S(1)}, f32[4,104,128]{2,1,0:T(8,128)S(1)}, u32[]{:S(2)}, u32[]{:S(2)}) collective-permute-start(f32[4,104,128]{2,1,0:T(8,128)S(1)} %constant_dynamic-update-slice_fusion.mine_ref), channel_id=1, source_target_pairs={{0,1},{1,0},{2,3},{3,2},{4,5},{5,4},{6,7},{7,6},{8,9},{9,8},{10,11... | collective-permute-start | bytes 638984 | tf_op jit(solution)/shard_map/ppermute | solution.py:404
  46.2 3.7 %collective-permute-start.13 = (f32[4,128]{1,0:T(4,128)S(1)}, f32[4,128]{1,0:T(4,128)S(1)}, u32[]{:S(2)}, u32[]{:S(2)}) collective-permute-start(f32[4,128]{1,0:T(4,128)S(1)} %shard_map.81), channel_id=1, source_target_pairs={{0,2},{1,3},{2,0},{3,1},{4,6},{5,7},{6,4},{7,5},{8,10},{9,11},{10,... | collective-permute-start | bytes 6152 | tf_op jit(solution)/shard_map/ppermute | solution.py:404
  47.8 3.0 %collective-permute-start.14 = (f32[4,128]{1,0:T(4,128)S(1)}, f32[4,128]{1,0:T(4,128)S(1)}, u32[]{:S(2)}, u32[]{:S(2)}) collective-permute-start(f32[4,128]{1,0:T(4,128)S(1)} %shard_map.81), channel_id=1, source_target_pairs={{0,3},{1,2},{2,1},{3,0},{4,7},{5,6},{6,5},{7,4},{8,11},{9,10},{10,... | collective-permute-start | bytes 6152 | tf_op jit(solution)/shard_map/ppermute | solution.py:404
  47.8 3.0 %collective-permute-start.12 = (f32[4,128]{1,0:T(4,128)S(1)}, f32[4,128]{1,0:T(4,128)S(1)}, u32[]{:S(2)}, u32[]{:S(2)}) collective-permute-start(f32[4,128]{1,0:T(4,128)S(1)} %shard_map.81), channel_id=1, source_target_pairs={{0,1},{1,0},{2,3},{3,2},{4,5},{5,4},{6,7},{7,6},{8,9},{9,8},{10,11... | collective-permute-start | bytes 6152 | tf_op jit(solution)/shard_map/ppermute | solution.py:404
  48.4 4.9 %collective-permute-start.15 = (f32[2,104,128]{2,1,0:T(8,128)S(1)}, f32[2,104,128]{2,1,0:T(8,128)S(1)}, u32[]{:S(2)}, u32[]{:S(2)}) collective-permute-start(f32[2,104,128]{2,1,0:T(8,128)S(1)} %pad_maximum_fusion), channel_id=1, source_target_pairs={{0,4},{4,0},{8,12},{12,8},{16,20},{20,16},{24,28},{28,24},{1,5},{5... | collective-permute-start | bytes 319496 | tf_op jit(solution)/shard_map/ppermute | solution.py:404
  48.9 4.5 %collective-permute-start.16 = (f32[2,104,128]{2,1,0:T(8,128)S(1)}, f32[2,104,128]{2,1,0:T(8,128)S(1)}, u32[]{:S(2)}, u32[]{:S(2)}) collective-permute-start(f32[2,104,128]{2,1,0:T(8,128)S(1)} %constant_dynamic-update-slice_fusion.4.mine_ref), channel_id=1, source_target_pairs={{0,1},{1,0},{2,3},{3,2},{4,5},{5,4},{6,7},{7,6},{8,9},{9,8},{10,11... | collective-permute-start | bytes 319496 | tf_op jit(solution)/shard_map/ppermute | solution.py:404
  63.9 3.7 %collective-permute-start.17 = (f32[2,104,128]{2,1,0:T(8,128)S(1)}, f32[2,104,128]{2,1,0:T(8,128)S(1)}, u32[]{:S(2)}, u32[]{:S(2)}) collective-permute-start(f32[2,104,128]{2,1,0:T(8,128)S(1)} %collective-permute-done.15.mine_ref), channel_id=1, source_target_pairs={{0,1},{1,0},{2,3},{3,2},{4,5},{5,4},{6,7},{7,6},{8,9},{9,8},{10,11... | collective-permute-start | bytes 319496 | tf_op jit(solution)/shard_map/ppermute | solution.py:404
  64.0 3.7 %collective-permute-start.19 = (f32[4,128]{1,0:T(4,128)S(1)}, f32[4,128]{1,0:T(4,128)S(1)}, u32[]{:S(2)}, u32[]{:S(2)}) collective-permute-start(f32[4,128]{1,0:T(4,128)S(1)} %shard_map.84), channel_id=1, source_target_pairs={{0,2},{1,3},{2,0},{3,1},{4,6},{5,7},{6,4},{7,5},{8,10},{9,11},{10,... | collective-permute-start | bytes 6152 | tf_op jit(solution)/shard_map/ppermute | solution.py:404
  65.6 3.0 %collective-permute-start.20 = (f32[4,128]{1,0:T(4,128)S(1)}, f32[4,128]{1,0:T(4,128)S(1)}, u32[]{:S(2)}, u32[]{:S(2)}) collective-permute-start(f32[4,128]{1,0:T(4,128)S(1)} %shard_map.84), channel_id=1, source_target_pairs={{0,3},{1,2},{2,1},{3,0},{4,7},{5,6},{6,5},{7,4},{8,11},{9,10},{10,... | collective-permute-start | bytes 6152 | tf_op jit(solution)/shard_map/ppermute | solution.py:404
  65.9 2.7 %collective-permute-start.18 = (f32[4,128]{1,0:T(4,128)S(1)}, f32[4,128]{1,0:T(4,128)S(1)}, u32[]{:S(2)}, u32[]{:S(2)}) collective-permute-start(f32[4,128]{1,0:T(4,128)S(1)} %shard_map.84), channel_id=1, source_target_pairs={{0,1},{1,0},{2,3},{3,2},{4,5},{5,4},{6,7},{7,6},{8,9},{9,8},{10,11... | collective-permute-start | bytes 6152 | tf_op jit(solution)/shard_map/ppermute | solution.py:404
